TPU v7x, 32 devices: a whole 2x2x4 slice. The times are simulated.
32 devices in a mesh: emb: 4 (over y, x), row: 4 (over z), phase: 2 (over core).
Axes of the slice: x: 2, y: 2, z: 4, core: 2. Of those that a mesh axis runs over, the one named last changes fastest.
Arguments:
- item_table: bfloat16 [4096, 512], P('emb'), may hold values from -10 to 10
- item_owner: int32 [4, 2, 1024, 1], P('emb', 'phase', 'row'), may hold values from 0 to 3; in each aligned block of 256 rows (0 to 255, 256 to 511, ..., all dimensions but the last counted through in order) at most 128 rows name the same one
- item_slot: int32 [4, 2, 1024], P('emb', 'phase', 'row'), may hold values from 0 to 1023
- seq_lengths: int32 [4, 2, 2], P('emb'), may hold values from 1 to 768, 1024 in all within a row
- row_grads: bfloat16 [4, 2, 1024, 512], P('emb', 'phase', 'row'), may hold values from -6 to 6
- proj_weight: bfloat16 [2, 512, 2048], P('phase'), may hold values from -2 to 2
- out_weight: bfloat16 [2, 512, 512], P('phase'), may hold values from -0.25 to 0.25
- final_gain: float32 [512], replicated, may hold values from 0.1 to 1.9
Outputs:
- sequence_states: bfloat16 [4, 2, 1024, 512], P('emb', 'phase', 'row')
- table_grad: float32 [4096, 512], P(('emb', 'row', 'phase'))
Inputs may be any that keep to these rules, and one draw needn't show every extreme that they name: `item_owner`: among the 256 tokens of one device, at most 128 name the same owner, and in every draw some device has an owner named by exactly 128 of its tokens. `seq_lengths`: the 2 lengths of one micro-batch of one group sum to 1024; neither is longer than 768.
All inputs are finite; a program needn't handle non-finite values.
Results may differ from a plain program's by a relative error of at most 0.013.
Values may be sent and summed in bfloat16 or wider, within the bound.
No kernel may reach another device: no remote copies, remote signals or barrier semaphores. Data moves between devices by JAX's collectives and lax.ppermute only.
A program may use at most 64 MiB of HBM per device.

v0:
```python
import jax
import jax.numpy as jnp
from jax import lax
from jax.sharding import PartitionSpec as P

HEADS = 4
HEAD_DIM = 128


norm_eps = 1e-05


def passed_along(shard, axis, by):
    count = lax.axis_size(axis)
    pairs = [(i, i + by) for i in range(count) if 0 <= i + by < count]
    return lax.ppermute(shard, axis, pairs)


def layer_norm(values):
    average = jnp.mean(values, axis=-1, keepdims=True)
    centered = values - average
    return centered * lax.rsqrt(jnp.mean(centered * centered, axis=-1, keepdims=True) + norm_eps)


def segment_of(positions, lengths):
    bounds = jnp.cumsum(lengths)[:-1]
    return jnp.sum((positions[:, None] >= bounds[None, :]).astype(jnp.int32), axis=1)


def attend_keys(query_rows, query_pos, query_seg, lengths, running, pieces):
    key_piece, value_piece = pieces
    key_count = key_piece.shape[0]
    key_pos = jnp.arange(key_count, dtype=jnp.int32)
    key_seg = segment_of(key_pos, lengths)
    visible = (key_pos[None, :] <= query_pos[:, None]) & (key_seg[None, :] == query_seg[:, None])
    query_heads = query_rows.reshape(query_rows.shape[0], HEADS, HEAD_DIM)
    key_heads = key_piece.reshape(key_count, HEADS, HEAD_DIM)
    value_heads = value_piece.reshape(key_count, HEADS, HEAD_DIM)
    scores = jnp.einsum("qhd,khd->hqk", query_heads, key_heads, preferred_element_type=jnp.float32)
    attn_weights = jnp.where(visible[None], jax.nn.silu(scores), 0.0).astype(jnp.bfloat16)
    update = jnp.einsum(
        "hqk,khd->qhd", attn_weights, value_heads, preferred_element_type=jnp.float32
    )
    return update.reshape(running.shape)


def hstu_layer(feed_rows, proj_weight, out_weight, lengths):
    count_rows = feed_rows.shape[0]
    normed = layer_norm(feed_rows.astype(jnp.float32)).astype(jnp.bfloat16)
    projected = jnp.dot(normed, proj_weight[0], preferred_element_type=jnp.float32)
    activated = jax.nn.silu(projected).astype(jnp.bfloat16)
    inner_width = HEADS * HEAD_DIM
    gate_rows = activated[:, :inner_width]
    value_rows = activated[:, inner_width : 2 * inner_width]
    query_rows = activated[:, 2 * inner_width : 3 * inner_width]
    key_rows = activated[:, 3 * inner_width :]
    query_pos = lax.axis_index("row") * count_rows + jnp.arange(count_rows, dtype=jnp.int32)
    query_seg = segment_of(query_pos, lengths)
    mixed_heads = attend_keys(
        query_rows,
        query_pos,
        query_seg,
        lengths,
        jnp.zeros((count_rows, inner_width), jnp.float32),
        (
            lax.all_gather(key_rows, "row", axis=0, tiled=True),
            lax.all_gather(value_rows, "row", axis=0, tiled=True),
        ),
    )
    gated = (layer_norm(mixed_heads) * gate_rows.astype(jnp.float32)).astype(jnp.bfloat16)
    branch = jnp.dot(gated, out_weight[0], preferred_element_type=jnp.float32)
    return feed_rows.astype(jnp.float32) + branch


def body(
    item_table, item_owner, item_slot, seq_lengths, row_grads, proj_weight, out_weight, final_gain
):
    parties = lax.axis_size("emb")
    owners = item_owner.reshape(-1)
    slot_ids = item_slot.reshape(-1)
    count_rows = owners.shape[0]
    model_width = item_table.shape[1]
    owned_rows = item_table.shape[0]
    capacity = max(16, 2 * count_rows // parties)
    onehot = (owners[:, None] == jnp.arange(parties, dtype=jnp.int32)[None, :]).astype(jnp.int32)
    places = jnp.sum((jnp.cumsum(onehot, axis=0) - onehot) * onehot, axis=1)
    request = jnp.full((parties, capacity), -1, jnp.int32).at[owners, places].set(slot_ids)
    grad_rows = row_grads.reshape(count_rows, model_width)
    outgoing = (
        jnp.zeros((parties, capacity, model_width), jnp.bfloat16).at[owners, places].set(grad_rows)
    )
    asked_slots = lax.all_to_all(request, "emb", split_axis=0, concat_axis=0, tiled=True)
    arrived = lax.all_to_all(outgoing, "emb", split_axis=0, concat_axis=0, tiled=True)
    is_valid = asked_slots >= 0
    looked = jnp.take(item_table, jnp.maximum(asked_slots, 0), axis=0)
    looked = jnp.where(is_valid[..., None], looked, jnp.zeros_like(looked))
    returned = lax.all_to_all(looked, "emb", split_axis=0, concat_axis=0, tiled=True)
    returned, asked_kept = (returned, asked_slots)
    own_rows = returned[owners, places]
    other_rows = passed_along(own_rows, "phase", -1)
    phase_id = lax.axis_index("phase")
    is_first = phase_id == 0
    phase_inputs = [own_rows, other_rows, other_rows]
    carried = own_rows
    outputs = []
    for tick_index in range(3):
        feed_rows = jnp.where(is_first, phase_inputs[tick_index], carried)
        micro = jnp.clip(tick_index - phase_id, 0, 1)
        lengths = lax.dynamic_index_in_dim(seq_lengths[0], micro, 0, keepdims=False)
        residual_sum = hstu_layer(feed_rows, proj_weight, out_weight, lengths)
        plain_rows = residual_sum.astype(jnp.bfloat16)
        closing = (layer_norm(residual_sum) * final_gain).astype(jnp.bfloat16)
        outputs.append(jnp.where(is_first, plain_rows, closing))
        if tick_index < 2:
            carried = passed_along(plain_rows, "phase", 1)
    returned_first = passed_along(outputs[1], "phase", -1)
    final_rows = jnp.where(is_first, returned_first, outputs[2])
    sequence_states = final_rows.reshape(1, 1, count_rows, model_width)
    flat_slots = asked_kept.reshape(-1)
    targets = jnp.where(flat_slots >= 0, flat_slots, owned_rows)
    partial_value = (
        jnp.zeros((owned_rows, model_width), jnp.float32)
        .at[targets]
        .add(arrived.reshape(-1, model_width).astype(jnp.float32), mode="drop")
    )
    table_grad = lax.psum_scatter(
        partial_value.astype(jnp.bfloat16), ("row", "phase"), scatter_dimension=0, tiled=True
    ).astype(jnp.float32)
    return (sequence_states, table_grad)


def solution(mesh):
    placed = (
        P("emb", None),
        P("emb", "phase", "row", None),
        P("emb", "phase", "row"),
        P("emb", None, None),
        P("emb", "phase", "row", None),
        P("phase", None, None),
        P("phase", None, None),
        P(),
    )
    return jax.shard_map(
        body,
        mesh=mesh,
        in_specs=placed,
        out_specs=(P("emb", "phase", "row", None), P(("emb", "row", "phase"), None)),
        check_vma=False,
    )
```

profile of v0, /device:TPU:0, one launch (start us, length us, event | category | flops | bytes accessed | tf_op | source)
XLA Modules:
  0.0 278.8 jit_solution(2654513513537177928)
XLA Ops:
  8.9 1.2 reduce-window.16
  11.9 21.4 %scatter_fusion = s32[4,128]{1,0:T(4,128)S(1)} fusion(s32[4,128]{1,0:T(4,128)S(1)} %broadcast_in_dim.49, s32[256]{0:T(256)S(1)} %bitcast.173, s32[256]{0:T(256)} %bitcast.197), kind=kCustom, calls=%fused_computation.2 | custom fusion | bytes 5120 | tf_op jit(solution)/shard_map/scatter | solution.py:87
  33.3 9.6 %all_to_all.19 = s32[4,1,128]{2,1,0:T(1,128)S(1)} all-to-all(s32[4,1,128]{2,1,0:T(1,128)S(1)} %bitcast.172), channel_id=1, replica_groups=mesh['emb'=4,'row'=4,'phase'=2] {'emb'}, dimensions={0} | all-to-all | bytes 4096 | tf_op jit(solution)/shard_map/all_to_all | solution.py:92
  43.0 2.6 gather_fusion
  45.6 1.2 select_select_fusion
  46.8 9.8 %all_to_all.20 = bf16[4,128,512]{2,1,0:T(8,128)(2,1)S(1)} all-to-all(bf16[4,128,512]{2,1,0:T(8,128)(2,1)S(1)} %select_select_fusion), channel_id=1, replica_groups=mesh['emb'=4,'row'=4,'phase'=2] {'emb'}, dimensions={0} | all-to-all | bytes 1048576 | tf_op jit(solution)/shard_map/all_to_all | solution.py:97
  56.6 2.1 gather_fusion.1
  60.0 1.0 copy-done.7
  60.9 0.9 slice_bitcast_fusion.2
  63.4 1.5 fusion.31
  64.9 1.3 collective-permute-start
  66.2 23.5 %all-gather.7.cloned.1.call-done = bf16[1024,512]{1,0:T(8,128)(2,1)} async-done(((bf16[256,512]{1,0:T(8,128)(2,1)}), bf16[1024,512]{1,0:T(8,128)(2,1)}) %all-gather.7.cloned.1.call-update) | async-done | bytes 1048592 | tf_op jit(solution)/shard_map/all_gather | solution.py:67
  89.7 2.3 copy.68
  92.0 27.3 %all-gather.9.cloned.1.call-done = bf16[1024,512]{1,0:T(8,128)(2,1)} async-done(((bf16[256,512]{1,0:T(8,128)(2,1)}), bf16[1024,512]{1,0:T(8,128)(2,1)}) %all-gather.9.cloned.1.call-update) | async-done | bytes 1048592 | tf_op jit(solution)/shard_map/all_gather | solution.py:66
  119.3 3.6 %fusion.106 = (f32[256]{0:T(256)S(1)}, f32[4,128,256]{2,1,0:T(8,128)S(1)}) fusion(bf16[1024,4,128]{0,2,1:T(8,128)(2,1)} %bitcast.182, pred[256,1024]{1,0:T(8,128)(4,1)} %get-tuple-element.23, bf16[32,4,8,128]{3,2,1,0:T(8,128)(2,1)} %get-tuple-element.16, bf16[1024,512]{1,0:T(8,128)(2,1)} %all-gather.9.cloned.1.call-done), kind=kOutput, calls=%fused_computation.164 | convolution fusion | flops 543293184 | bytes 3146752 | tf_op jit(solution)/shard_map/hqk,khd->qhd/dot_general | solution.py:41
  123.0 1.0 copy.69
  124.1 1.5 fusion.15
  125.5 1.6 collective-permute-start.1
  127.2 1.1 collective-permute-done.1
  128.3 1.1 convert_reduce_fusion.1
  129.6 0.9 multiply_convert_fusion.1
  130.5 1.0 copy-done.5
  131.5 0.9 slice_bitcast_fusion.1
  133.8 34.3 %scatter_fusion.1 = bf16[4,128,512]{2,1,0:T(8,128)(2,1)} fusion(bf16[4,128,512]{2,1,0:T(8,128)(2,1)} %broadcast.425, s32[256]{0:T(256)S(1)} %bitcast.174, bf16[256,512]{1,0:T(8,128)(2,1)S(1)} %bitcast.184), kind=kCustom, calls=%fused_computation.3 | custom fusion | bytes 788480 | tf_op jit(solution)/shard_map/scatter | solution.py:90
  168.1 3.6 %all-to-all-start.2 = ((bf16[4,128,512]{2,1,0:T(8,128)(2,1)}), bf16[4,128,512]{2,1,0:T(8,128)(2,1)S(1)}, u32[]{:S(2)}, u32[]{:S(2)}) async-start(bf16[4,128,512]{2,1,0:T(8,128)(2,1)} %scatter_fusion.1), calls=%async_computation.2 | async-start | bytes 1048576 | tf_op jit(solution)/shard_map/all_to_all | solution.py:93
  171.8 8.0 %all-to-all-done.2 = bf16[4,128,512]{2,1,0:T(8,128)(2,1)S(1)} async-done(((bf16[4,128,512]{2,1,0:T(8,128)(2,1)}), bf16[4,128,512]{2,1,0:T(8,128)(2,1)S(1)}, u32[]{:S(2)}, u32[]{:S(2)}) %all-to-all-start.2) | async-done | bytes 524320 | tf_op jit(solution)/shard_map/all_to_all | solution.py:93
  179.8 5.1 %scatter_custom_fusion.2 = f32[1024,512]{1,0:T(8,128)} fusion(s32[512]{0:T(512)S(1)} %bitcast.194, bf16[512,512]{1,0:T(8,128)(2,1)S(1)} %bitcast.180, f32[]{:T(128)} %constant.95.clone.1), kind=kCustom, calls=%fused_computation.30 | custom fusion | flops 524288 | bytes 2621444 | tf_op jit(solution)/shard_map/scatter-add | solution.py:124
  184.9 2.7 convert_element_type.178
  187.7 2.3 copy.70
  190.0 3.6 %fusion.111 = (f32[256]{0:T(256)S(1)}, f32[4,128,256]{2,1,0:T(8,128)S(1)}) fusion(bf16[1024,4,128]{0,2,1:T(8,128)(2,1)} %bitcast.183, pred[256,1024]{1,0:T(8,128)(4,1)} %get-tuple-element.22, bf16[32,4,8,128]{3,2,1,0:T(8,128)(2,1)} %get-tuple-element.13, bf16[1024,512]{1,0:T(8,128)(2,1)} %all-gather.13.cloned.1.call-done), kind=kOutput, calls=%fused_computation.165 | convolution fusion | flops 543293184 | bytes 3146752 | tf_op jit(solution)/shard_map/hqk,khd->qhd/dot_general | solution.py:41
  194.4 1.2 copy.71
  195.6 1.4 fusion.116
  197.3 0.9 fusion.55
  198.1 1.3 collective-permute-start.3
  199.5 1.1 collective-permute-done.3
  200.6 1.1 convert_reduce_fusion
  202.9 1.0 copy-done.6
  203.8 0.9 slice_bitcast_fusion
  205.3 18.3 %reduce-scatter.2.cloned.1.call-done = bf16[128,512]{1,0:T(8,128)(2,1)} async-done(((bf16[1024,512]{1,0:T(8,128)(2,1)}), bf16[128,512]{1,0:T(8,128)(2,1)}) %reduce-scatter.2.cloned.1.call-update) | async-done | bytes 131088 | tf_op jit(solution)/shard_map/reduce_scatter | solution.py:126
  223.6 1.6 convert_element_type.179
  225.3 1.3 collective-permute-start.2
  226.6 7.3 %all-gather.15.cloned.1.call-done = bf16[1024,512]{1,0:T(8,128)(2,1)} async-done(((bf16[256,512]{1,0:T(8,128)(2,1)}), bf16[1024,512]{1,0:T(8,128)(2,1)}) %all-gather.15.cloned.1.call-update) | async-done | bytes 1048592 | tf_op jit(solution)/shard_map/all_gather | solution.py:67
  233.9 2.3 copy.72
  236.2 26.0 %all-gather.17.cloned.1.call-done = bf16[1024,512]{1,0:T(8,128)(2,1)} async-done(((bf16[256,512]{1,0:T(8,128)(2,1)}), bf16[1024,512]{1,0:T(8,128)(2,1)}) %all-gather.17.cloned.1.call-update) | async-done | bytes 1048592 | tf_op jit(solution)/shard_map/all_gather | solution.py:66
  262.2 3.6 %fusion.117 = (f32[256]{0:T(256)S(1)}, f32[4,128,256]{2,1,0:T(8,128)S(1)}) fusion(bf16[1024,4,128]{0,2,1:T(8,128)(2,1)} %bitcast.181, pred[256,1024]{1,0:T(8,128)(4,1)} %get-tuple-element.21, bf16[32,4,8,128]{3,2,1,0:T(8,128)(2,1)} %get-tuple-element.10, bf16[1024,512]{1,0:T(8,128)(2,1)} %all-gather.17.cloned.1.call-done), kind=kOutput, calls=%fused_computation.167 | convolution fusion | flops 543293184 | bytes 3146752 | tf_op jit(solution)/shard_map/hqk,khd->qhd/dot_general | solution.py:41
  266.6 1.2 copy.73
  267.8 1.4 fusion.122
  269.5 1.9 fusion.58
  (89 shorter events, 11.0 us)
Async XLA Ops:
  8.0 51.1 %copy-start = (bf16[1,512,2048]{2,1,0:T(8,128)(2,1)S(1)}, bf16[1,512,2048]{2,1,0:T(8,128)(2,1)}, u32[]{:S(2)}) copy-start(bf16[1,512,2048]{2,1,0:T(8,128)(2,1)} %param.13) | copy-start | bytes 6291460
  8.0 35.0 %copy-start.1 = (bf16[1024,512]{1,0:T(8,128)(2,1)S(1)}, bf16[1024,512]{1,0:T(8,128)(2,1)}, u32[]{:S(2)}) copy-start(bf16[1024,512]{1,0:T(8,128)(2,1)} %param.8) | copy-start | bytes 3145732
  8.0 81.7 %all-gather.7.cloned.1.call-start = ((), (), s32[]{:S(2)}) async-start(), calls=%async_computation.4 | async-start | bytes 1310720 | tf_op jit(solution)/shard_map/all_gather | solution.py:67
  59.9 1.0 copy-start.7
  60.9 1.7 copy-start.10
  61.9 57.4 %all-gather.9.cloned.1.call-start = ((), (), s32[]{:S(2)}) async-start(), calls=%async_computation.5 | async-start | bytes 1310720 | tf_op jit(solution)/shard_map/all_gather | solution.py:66
  62.6 125.1 %all-gather.11.cloned.1.call-start = ((), (), s32[]{:S(2)}) async-start(), calls=%async_computation.6 | async-start | bytes 1310720 | tf_op jit(solution)/shard_map/all_gather | solution.py:67
  64.9 62.2 %collective-permute-start = (bf16[256,512]{1,0:T(8,128)(2,1)S(1)}, bf16[256,512]{1,0:T(8,128)(2,1)}, u32[]{:S(2)}, u32[]{:S(2)}) collective-permute-start(bf16[256,512]{1,0:T(8,128)(2,1)S(1)} %gather_fusion.1), channel_id=1, source_target_pairs={{1,0},{3,2},{5,4},{7,6},{9,8},{11,10},{13,12},{15,14},{17,16},{19,... | collective-permute-start | bytes 786440 | tf_op jit(solution)/shard_map/ppermute | solution.py:16
  119.3 4.8 %copy-start.2 = (bf16[1,512,512]{2,1,0:T(8,128)(2,1)S(1)}, bf16[1,512,512]{2,1,0:T(8,128)(2,1)}, u32[]{:S(2)}) copy-start(bf16[1,512,512]{2,1,0:T(8,128)(2,1)} %param.14) | copy-start | bytes 1572868
  125.5 2.8 collective-permute-start.1
  130.5 1.0 copy-start.5
  131.5 2.3 copy-start.8
  132.4 57.6 %all-gather.13.cloned.1.call-start = ((), (), s32[]{:S(2)}) async-start(), calls=%async_computation.7 | async-start | bytes 1310720 | tf_op jit(solution)/shard_map/all_gather | solution.py:66
  168.1 11.7 %all-to-all-start.2 = ((bf16[4,128,512]{2,1,0:T(8,128)(2,1)}), bf16[4,128,512]{2,1,0:T(8,128)(2,1)S(1)}, u32[]{:S(2)}, u32[]{:S(2)}) async-start(bf16[4,128,512]{2,1,0:T(8,128)(2,1)} %scatter_fusion.1), calls=%async_computation.2 | async-start | bytes 1048576 | tf_op jit(solution)/shard_map/all_to_all | solution.py:93
  171.7 51.9 %reduce-scatter.2.cloned.1.call-start = ((), (), s32[]{:S(2)}) async-start(), calls=%async_computation.10 | async-start | bytes 1179648 | tf_op jit(solution)/shard_map/reduce_scatter | solution.py:126
  187.7 46.2 %all-gather.15.cloned.1.call-start = ((), (), s32[]{:S(2)}) async-start(), calls=%async_computation.8 | async-start | bytes 1310720 | tf_op jit(solution)/shard_map/all_gather | solution.py:67
  193.6 0.8 copy-start.3
  193.6 3.6 %copy-start.9 = (f32[512]{0:T(512)S(1)}, f32[512]{0:T(512)}, u32[]{:S(2)}) copy-start(f32[512]{0:T(512)} %param.15) | copy-start | bytes 6148
  198.1 2.5 collective-permute-start.3
  202.8 1.0 copy-start.6
  204.8 57.4 %all-gather.17.cloned.1.call-start = ((), (), s32[]{:S(2)}) async-start(), calls=%async_computation.9 | async-start | bytes 1310720 | tf_op jit(solution)/shard_map/all_gather | solution.py:66
  225.3 44.2 %collective-permute-start.2 = (bf16[256,512]{1,0:T(8,128)(2,1)}, bf16[256,512]{1,0:T(8,128)(2,1)}, u32[]{:S(2)}, u32[]{:S(2)}) collective-permute-start(bf16[256,512]{1,0:T(8,128)(2,1)} %get-tuple-element.4), channel_id=1, source_target_pairs={{1,0},{3,2},{5,4},{7,6},{9,8},{11,10},{13,12},{15,14},{17,16},{19,... | collective-permute-start | bytes 786440 | tf_op jit(solution)/shard_map/ppermute | solution.py:16
  265.8 0.8 copy-start.4
Sparse Core Ops, SparseCore 0:
  62.0 27.6 all-gather.6
  91.8 27.4 all-gather.8
  132.5 27.7 all-gather.10
  162.3 27.4 all-gather.12
  204.9 28.9 all-gather.14
  235.3 26.8 all-gather.16
Sparse Core Ops, SparseCore 1:
  187.7 35.8 reduce-scatter.1
where the time goes:
time: 281 us; the launch traced here: 279 us
  waiting for transfers between devices  115 us (41%)
  local copies, waits for them, and re-layouts  78.9 us (28%)
  other arithmetic  23 us (8%)
  blocking collectives  19.4 us (7%)
  matrix products  17.6 us (6%)
  between operations  16 us (6%)
  starting transfers between devices  9.46 us (3%)
    all_gather x3, waiting for transfers between devices, hstu_layer(): lax.all_gather(key_rows, 'row', axis=0, tiled=True)  53.4 us
    scatter x1, local copies, waits for them, and re-layouts, body(): jnp.zeros((parties, capacity, model_width), jnp.bfloat16).at[owners, places]  34.3 us
    all_gather x3, waiting for transfers between devices, hstu_layer(): lax.all_gather(value_rows, 'row', axis=0, tiled=True)  30.8 us
    scatter x1, local copies, waits for them, and re-layouts, body(): jnp.full((parties, capacity), -1, jnp.int32).at[owners, places]  21.4 us
    reduce_scatter x1, waiting for transfers between devices, body(): lax.psum_scatter(partial_value.astype(jnp.bfloat16), ('row', 'phase'), sc...  18.3 us
    dot_general x3, matrix products, attend_keys(): jnp.einsum('hqk,khd->qhd', attn_weights, value_heads, preferred_element_t...  10.8 us
    all_to_all x1, blocking collectives, body(): lax.all_to_all(looked, 'emb', split_axis=0, concat_axis=0, tiled=True)  9.77 us
    all_to_all x1, blocking collectives, body(): lax.all_to_all(request, 'emb', split_axis=0, concat_axis=0, tiled=True)  9.61 us
  transfers between devices with their start and end apart: 12, of which 8 were waited for; matrix products, arithmetic and copies ran while one was open for 28% of the time, Pallas kernels for 0%

commit v1 on v0

v1 whole, which is shorter than its diff:
```python
import functools

import jax
import jax.numpy as jnp
from jax import lax
from jax.experimental import pallas as pl
from jax.experimental.pallas import tpu as pltpu
from jax.sharding import PartitionSpec as P

HEADS = 4
HEAD_DIM = 128
INNER = HEADS * HEAD_DIM
SLOT_BASE = 128

norm_eps = 1e-05

NT = (((1,), (1,)), ((), ()))


def exchanged(shard, axis, by):
    count = lax.axis_size(axis)
    return lax.ppermute(shard, axis, [(i, i ^ by) for i in range(count)])


def layer_norm(values):
    average = jnp.mean(values, axis=-1, keepdims=True)
    centered = values - average
    return centered * lax.rsqrt(jnp.mean(centered * centered, axis=-1, keepdims=True) + norm_eps)


def silu(values):
    half = 0.5 * values
    return half * jnp.tanh(half) + half


def dot(left, right):
    return jnp.dot(left, right, preferred_element_type=jnp.float32)


def as_column(row):
    count = row.shape[1]
    down = lax.broadcasted_iota(jnp.int32, (count, count), 0)
    along = lax.broadcasted_iota(jnp.int32, (count, count), 1)
    picked = jnp.where(down == along, jnp.broadcast_to(row, (count, count)), 0.0)
    return jnp.sum(picked, axis=1, keepdims=True)


def pack_kernel(parties, capacity, owner_ref, slot_ref, grad_ref, *packed_refs):
    owner = owner_ref[...]
    slot = slot_ref[...]
    count = owner.shape[1]
    before = (
        lax.broadcasted_iota(jnp.int32, (count, count), 0)
        < lax.broadcasted_iota(jnp.int32, (count, count), 1)
    ).astype(jnp.bfloat16)
    high = slot // SLOT_BASE
    low = slot - high * SLOT_BASE
    line = lax.broadcasted_iota(jnp.int32, (16, count), 0)
    codes = jnp.where(line == 0, high + 1, jnp.where(line == 1, low, 0))
    codes = codes.astype(jnp.float32).astype(jnp.bfloat16)
    place = lax.broadcasted_iota(jnp.int32, (capacity, count), 0)
    for party in range(parties):
        named = owner == party
        flags = jnp.broadcast_to(named, (16, count)).astype(jnp.float32).astype(jnp.bfloat16)
        rank = dot(flags, before)[0:1].astype(jnp.int32)
        chosen = (named & (rank == place)).astype(jnp.float32).astype(jnp.bfloat16)
        packed_refs[party][0:capacity, :] = dot(chosen, grad_ref[...]).astype(jnp.bfloat16)
        sent_codes = lax.dot_general(codes, chosen, NT, preferred_element_type=jnp.float32)
        packed_refs[party][capacity : capacity + 16, 0:capacity] = sent_codes.astype(jnp.bfloat16)


def scatter_kernel(parties, capacity, row_ids, place_ref, *refs):
    arrived = refs[:parties]
    keep_ref, send_ref = refs[parties:]
    rows, phases = row_ids
    my_row, my_phase = place_ref[0], place_ref[1]
    block = keep_ref.shape[0] // rows
    values = jnp.concatenate([ref[0:capacity, :] for ref in arrived], axis=0)
    slots = []
    for ref in arrived:
        codes = ref[capacity : capacity + 16, 0:capacity].astype(jnp.float32)
        slots.append((codes[0:1] - 1.0) * SLOT_BASE + codes[1:2])
    slots = jnp.concatenate(slots, axis=1).astype(jnp.int32)
    down = lax.broadcasted_iota(jnp.int32, (block, parties * capacity), 0)
    for other in range(phases):
        for step in range(rows):
            base = ((my_row ^ step) * phases + (my_phase ^ other)) * block
            chosen = (slots - base == down).astype(jnp.float32).astype(jnp.bfloat16)
            total = dot(chosen, values)
            if other == 0:
                keep_ref[step * block : (step + 1) * block, :] = total
            else:
                send_ref[step * block : (step + 1) * block, :] = total.astype(jnp.bfloat16)


def loop(count, body):
    if count <= 4:
        for index in range(count):
            body(index)
    else:
        lax.fori_loop(0, count, lambda index, carry: (body(index), carry)[1], 0)


def section_kernel(
    window,
    place_ref,
    lengths_ref,
    ids_ref,
    table_ref,
    near_ref,
    next_ref,
    far_ref,
    near2_ref,
    next2_ref,
    far2_ref,
    proj_own,
    proj_other,
    outw_own,
    outw_other,
    gain_ref,
    out_ref,
    proj_ref,
    outw_ref,
    emb_ref,
    act_ref,
    mid_ref,
    mix_ref,
    sems,
):
    my_row, my_phase = place_ref[0], place_ref[1]
    size = out_ref.shape[0]
    half = near_ref.shape[0]
    owned = 2 * half
    copies = [
        pltpu.make_async_copy(proj_own.at[0], proj_ref.at[my_phase], sems.at[0]),
        pltpu.make_async_copy(proj_other.at[0], proj_ref.at[1 - my_phase], sems.at[1]),
        pltpu.make_async_copy(outw_own.at[0], outw_ref.at[my_phase], sems.at[2]),
        pltpu.make_async_copy(outw_other.at[0], outw_ref.at[1 - my_phase], sems.at[3]),
    ]
    for copy in copies:
        copy.start()

    def rows(block):
        if isinstance(block, int):
            return pl.ds(block * size, size)
        return pl.ds(pl.multiple_of(block * size, size), size)

    along = lax.broadcasted_iota(jnp.int32, (size, half), 1)
    mine = pl.ds(pl.multiple_of(my_phase * half, half), half)
    theirs = pl.ds(pl.multiple_of((1 - my_phase) * half, half), half)

    def look_up(block):
        ids = as_column(ids_ref[pl.ds(block, 1), :].astype(jnp.float32)).astype(jnp.int32)
        total = jnp.zeros((size, emb_ref.shape[1]), jnp.float32)
        pieces = (
            (0, table_ref, mine),
            (half, table_ref, theirs),
            (owned, near_ref, None),
            (owned + half, next2_ref, None),
            (2 * owned, next_ref, None),
            (2 * owned + half, near2_ref, None),
            (3 * owned, far_ref, None),
            (3 * owned + half, far2_ref, None),
        )
        for base, piece, part in pieces:
            chosen = (along == ids - base).astype(jnp.float32).astype(jnp.bfloat16)
            total += dot(chosen, piece[...] if part is None else piece[part, :])
        emb_ref[rows(block), :] = total

    loop(window, look_up)
    for copy in copies:
        copy.wait()

    first_pos = (my_row - (window - 1)) * size
    down = lax.broadcasted_iota(jnp.int32, (size, 1), 0)
    across = lax.broadcasted_iota(jnp.int32, (1, size), 1)

    def mixed_of(block):
        query_pos = first_pos + block * size + down
        start = jnp.zeros((size, 1), jnp.int32)
        bound = jnp.int32(0)
        for index in range(lengths_ref.shape[2] - 1):
            bound = bound + lengths_ref[0, my_phase, index]
            start = jnp.where(query_pos >= bound, bound, start)

        def piece(key_block, diagonal):
            key_pos = first_pos + key_block * size + across
            visible = key_pos >= start
            if diagonal:
                visible = visible & (key_pos <= query_pos)
            for head in range(HEADS):
                cols = head * HEAD_DIM
                queries = act_ref[rows(block), 2 * INNER + cols : 2 * INNER + cols + HEAD_DIM]
                keys = act_ref[rows(key_block), 3 * INNER + cols : 3 * INNER + cols + HEAD_DIM]
                values = act_ref[rows(key_block), INNER + cols : INNER + cols + HEAD_DIM]
                scores = lax.dot_general(queries, keys, NT, preferred_element_type=jnp.float32)
                weights = jnp.where(visible, silu(scores), 0.0).astype(jnp.bfloat16)
                update = dot(weights, values)
                if diagonal:
                    mix_ref[:, cols : cols + HEAD_DIM] = update
                else:
                    mix_ref[:, cols : cols + HEAD_DIM] += update

        piece(block, True)
        if isinstance(block, int):
            loop(block, lambda key_block: piece(key_block, False))
        else:
            lax.fori_loop(0, block, lambda key_block, c: (piece(key_block, False), c)[1], 0)
        return mix_ref[...]

    def branch(block, section):
        gates = act_ref[rows(block), 0:INNER].astype(jnp.float32)
        gated = (layer_norm(mixed_of(block)) * gates).astype(jnp.bfloat16)
        return dot(gated, outw_ref[section])

    def first_section(block):
        values = emb_ref[rows(block), :]
        normed = layer_norm(values).astype(jnp.bfloat16)
        act_ref[rows(block), :] = silu(dot(normed, proj_ref[0])).astype(jnp.bfloat16)
        mid_ref[rows(block), :] = (values + branch(block, 0)).astype(jnp.bfloat16)

    loop(window, first_section)

    def second_inputs(block):
        normed = layer_norm(mid_ref[rows(block), :].astype(jnp.float32)).astype(jnp.bfloat16)
        for cols in (INNER, 3 * INNER):
            act = silu(dot(normed, proj_ref[1, :, cols : cols + INNER]))
            act_ref[rows(block), cols : cols + INNER] = act.astype(jnp.bfloat16)
        return normed

    if window > 1:
        loop(window - 1, second_inputs)
    last = window - 1
    normed = second_inputs(last)
    for cols in (0, 2 * INNER):
        act = silu(dot(normed, proj_ref[1, :, cols : cols + INNER]))
        act_ref[rows(last), cols : cols + INNER] = act.astype(jnp.bfloat16)
    closing = mid_ref[rows(last), :].astype(jnp.float32) + branch(last, 1)
    out_ref[...] = (layer_norm(closing) * gain_ref[...]).astype(jnp.bfloat16)


def body(
    item_table, item_owner, item_slot, seq_lengths, row_grads, proj_weight, out_weight, final_gain
):
    parties = lax.axis_size("emb")
    row_count = lax.axis_size("row")
    phases = lax.axis_size("phase")
    my_emb = lax.axis_index("emb")
    my_row = lax.axis_index("row")
    my_phase = lax.axis_index("phase")
    size = item_slot.shape[2]
    width = item_table.shape[1]
    owned = item_table.shape[0]
    half = owned // 2
    capacity = max(16, 2 * size // parties)
    window = -(-3 * row_count // 4)
    vmem = pltpu.MemorySpace.VMEM
    smem = pltpu.MemorySpace.SMEM
    params = pltpu.CompilerParams(vmem_limit_bytes=48 * 1024 * 1024)

    def across(shard, first):
        pairs = []
        for emb in range(parties):
            for phase in range(phases):
                by = 1 if (phase == 0) == first else 2
                pairs.append((emb * phases + phase, (emb ^ by) * phases + phase))
        return lax.ppermute(shard, ("emb", "phase"), pairs)

    own_half = lax.dynamic_slice_in_dim(item_table, my_phase * half, half, 0)
    near = across(own_half, True)
    following = across(own_half, False)
    far = across(near, False)
    near2 = exchanged(near, "phase", 1)
    next2 = exchanged(following, "phase", 1)
    far2 = exchanged(far, "phase", 1)

    owner = item_owner.reshape(1, size)
    slot = item_slot.reshape(1, size)
    nearby = owner ^ my_emb
    swapped = (nearby // 2) | ((nearby % 2) * 2)
    turned = jnp.where(my_phase == 0, nearby, swapped)
    ids = turned * owned + (slot ^ (my_phase * half))
    window_ids = [ids]
    for step in range(1, window):
        pairs = [(i, i + step) for i in range(row_count - step)]
        arrived_ids = lax.ppermute(ids, "row", pairs)
        window_ids.insert(0, jnp.where(my_row >= step, arrived_ids, -1))
    window_ids = jnp.concatenate(window_ids, axis=0)

    proj_other = exchanged(proj_weight, "phase", 1)
    outw_other = exchanged(out_weight, "phase", 1)

    packed = pl.pallas_call(
        functools.partial(pack_kernel, parties, capacity),
        out_shape=[jax.ShapeDtypeStruct((capacity + 16, width), jnp.bfloat16)] * parties,
        in_specs=[pl.BlockSpec(memory_space=vmem)] * 3,
        out_specs=[pl.BlockSpec(memory_space=vmem)] * parties,
        compiler_params=params,
        name="pack",
    )(nearby, slot, row_grads.reshape(size, width))
    arrived = [packed[0]] + [exchanged(packed[by], "emb", by) for by in range(1, parties)]
    place = jnp.stack([my_row, my_phase]).astype(jnp.int32)
    block = owned // (row_count * phases)
    keep, send = pl.pallas_call(
        functools.partial(scatter_kernel, parties, capacity, (row_count, phases)),
        out_shape=[
            jax.ShapeDtypeStruct((row_count * block, width), jnp.float32),
            jax.ShapeDtypeStruct((row_count * block, width), jnp.bfloat16),
        ],
        in_specs=[pl.BlockSpec(memory_space=smem)] + [pl.BlockSpec(memory_space=vmem)] * parties,
        out_specs=[pl.BlockSpec(memory_space=vmem)] * 2,
        compiler_params=params,
        name="scatter",
    )(place, *arrived)
    total = keep + exchanged(send, "phase", 1).astype(jnp.float32)
    by = 1
    while by < row_count:
        total = total.reshape(-1, 2, block, width)
        sent = total[:, 1].astype(jnp.bfloat16)
        total = total[:, 0] + exchanged(sent, "row", by).astype(jnp.float32)
        by *= 2
    table_grad = total.reshape(block, width)

    hbm = pl.ANY
    states = pl.pallas_call(
        functools.partial(section_kernel, window),
        out_shape=jax.ShapeDtypeStruct((size, width), jnp.bfloat16),
        in_specs=[pl.BlockSpec(memory_space=smem)] * 2
        + [pl.BlockSpec(memory_space=vmem)] * 8
        + [pl.BlockSpec(memory_space=hbm)] * 4
        + [pl.BlockSpec(memory_space=vmem)],
        out_specs=pl.BlockSpec(memory_space=vmem),
        scratch_shapes=[
            pltpu.VMEM((2,) + proj_weight.shape[1:], jnp.bfloat16),
            pltpu.VMEM((2,) + out_weight.shape[1:], jnp.bfloat16),
            pltpu.VMEM((window * size, width), jnp.float32),
            pltpu.VMEM((window * size, 4 * INNER), jnp.bfloat16),
            pltpu.VMEM((window * size, width), jnp.bfloat16),
            pltpu.VMEM((size, INNER), jnp.float32),
            pltpu.SemaphoreType.DMA((4,)),
        ],
        compiler_params=params,
        name="sections",
    )(
        place,
        seq_lengths,
        window_ids,
        item_table,
        near,
        following,
        far,
        near2,
        next2,
        far2,
        proj_weight,
        proj_other,
        out_weight,
        outw_other,
        final_gain.reshape(1, width),
    )
    return (states.reshape(1, 1, size, width), table_grad)


def solution(mesh):
    placed = (
        P("emb", None),
        P("emb", "phase", "row", None),
        P("emb", "phase", "row"),
        P("emb", None, None),
        P("emb", "phase", "row", None),
        P("phase", None, None),
        P("phase", None, None),
        P(),
    )
    return jax.shard_map(
        body,
        mesh=mesh,
        in_specs=placed,
        out_specs=(P("emb", "phase", "row", None), P(("emb", "row", "phase"), None)),
        check_vma=False,
    )
```

time: 281 us -> 65.5 us (0.23)
  waiting for transfers between devices: 115 us -> 19.1 us
  local copies, waits for them, and re-layouts: 78.9 us -> 5.35 us
  blocking collectives: 19.4 us -> 0 us
  other arithmetic: 23 us -> 3.99 us
  matrix products: 17.6 us -> 0 us
  Pallas kernels: 0 us -> 17.4 us
  between operations: 16 us -> 0.95 us
  starting transfers between devices: 9.46 us -> 18.4 us
    all_gather x6 -> x0, waiting for transfers between devices: 84.2 us -> none  [the longest x3 53.4 us: hstu_layer(): lax.all_gather(key_rows, 'row', axis=0, tiled=True)]
    scatter x2 -> x0, local copies, waits for them, and re-layouts: 55.6 us -> none  [the longest x1 34.3 us: body(): jnp.zeros((parties, capacity, model_width), jnp.bfloat16).at[owners, places]]
    all_to_all x2 -> x0, blocking collectives: 19.4 us -> none  [the longest x1 9.77 us: body(): lax.all_to_all(looked, 'emb', split_axis=0, concat_axis=0, tiled=True)]
    reduce_scatter x1 -> x0, waiting for transfers between devices: 18.3 us -> none  [body(): lax.psum_scatter(partial_value.astype(jnp.bfloat16), ('row', 'phase'), sc...]
    dot_general x9 -> x0, matrix products: 17.6 us -> none  [the longest x3 10.8 us: attend_keys(): jnp.einsum('hqk,khd->qhd', attn_weights, value_heads, preferred_element_t...]
    pallas_call x0 -> x3, Pallas kernels: none -> 17.4 us  [the longest x1 15.3 us: body(): pl.pallas_call(functools.partial(section_kernel, window), out_shape=jax.S...]
    ppermute x4 -> x16, waiting for transfers between devices: 2.25 us -> 19.1 us  [the longest x3 10.8 us: across(): return lax.ppermute(shard, ('emb', 'phase'), pairs)]
    ppermute x4 -> x16, starting transfers between devices: 5.51 us -> 18.4 us  [the longest x11 8.25 us: exchanged(): return lax.ppermute(shard, axis, [(i, i ^ by) for i in range(count)])]
  transfers between devices with their start and end apart: 12 -> 16, of which waited for: 8 -> 6; matrix products, arithmetic and copies ran while one was open for 28% -> 8% of each run, Pallas kernels for 0% -> 0%
where the time goes in v1:
time: 65.5 us; the launch traced here: 65.1 us
  waiting for transfers between devices  19.1 us (29%)
  starting transfers between devices  18.4 us (28%)
  Pallas kernels  17.4 us (27%)
  local copies, waits for them, and re-layouts  5.35 us (8%)
  other arithmetic  3.99 us (6%)
  between operations  0.95 us (1%)
    pallas_call x1, Pallas kernels, body(): pl.pallas_call(functools.partial(section_kernel, window), out_shape=jax.S...  15.3 us
    ppermute x3, waiting for transfers between devices, across(): return lax.ppermute(shard, ('emb', 'phase'), pairs)  10.8 us
    ppermute x11, waiting for transfers between devices, exchanged(): return lax.ppermute(shard, axis, [(i, i ^ by) for i in range(count)])  8.26 us
    ppermute x11, starting transfers between devices, exchanged(): return lax.ppermute(shard, axis, [(i, i ^ by) for i in range(count)])  8.25 us
    ppermute x2, starting transfers between devices, body(): arrived_ids = lax.ppermute(ids, 'row', pairs)  6.84 us
    unnamed x16, local copies, waits for them, and re-layouts  3.42 us
    ppermute x3, starting transfers between devices, across(): return lax.ppermute(shard, ('emb', 'phase'), pairs)  3.33 us
    dynamic_slice x1, local copies, waits for them, and re-layouts, body(): own_half = lax.dynamic_slice_in_dim(item_table, my_phase * half, half, 0)  1.87 us
  transfers between devices with their start and end apart: 16, of which 6 were waited for; matrix products, arithmetic and copies ran while one was open for 8% of the time, Pallas kernels for 0%

profile of v1, /device:TPU:0, one launch (start us, length us, event | category | flops | bytes accessed | tf_op | source)
XLA Modules:
  0.0 65.1 jit_solution(3993309730810664570)
XLA Ops:
  0.6 0.7 %fusion.7 = (s32[1,256]{1,0:T(1,128)S(1)}, s32[1,256]{1,0:T(1,128)S(1)}) fusion(pred[]{:T(512)S(6)} %eq.5, s32[]{:T(128)S(6)} %mul.33, s32[1,1,256]{2,1,0:T(1,128)} %param.10, s32[1,1,256,1]{2,3,1,0:T(1,128)} %param.9, s32[]{:T(128)S(6)} %axis_index.38), kind=kLoop, calls=%fused_computation.21 | loop fusion | flops 6656 | bytes 4105 | tf_op jit(solution)/shard_map/add | solution.py:282
  1.4 0.0 copy-start.2
  1.4 0.9 %copy-done.2 = bf16[1,1,256,512]{3,2,1,0:T(8,128)(2,1)S(1)} copy-done((bf16[1,1,256,512]{3,2,1,0:T(8,128)(2,1)S(1)}, bf16[1,1,256,512]{3,2,1,0:T(8,128)(2,1)}, u32[]{:S(2)}) %copy-start.2) | copy-done | bytes 262168
  2.3 0.7 %copy-done.3 = s32[1,1,256]{2,1,0:T(1,128)S(1)} copy-done((s32[1,1,256]{2,1,0:T(1,128)S(1)}, s32[1,1,256]{2,1,0:T(1,128)}, u32[]{:S(2)}) %copy-start.3) | copy-done | bytes 1048
  3.0 0.8 %pack.1 = (bf16[144,512]{1,0:T(8,128)(2,1)S(1)}, bf16[144,512]{1,0:T(8,128)(2,1)S(1)}, bf16[144,512]{1,0:T(8,128)(2,1)S(1)}, bf16[144,512]{1,0:T(8,128)(2,1)S(1)}) custom-call(s32[1,256]{1,0:T(1,128)S(1)} %get-tuple-element.15.owner_ref, s32[1,256]{1,0:T(1,128)S(1)} %bitcast.32, bf16[256,512]{1,0:T(8,128)(2,1)S(1)} %bitcast.31), custom_call_target="tpu_custom_call" | custom-call | tf_op jit(solution)/shard_map/pack/pallas_call | solution.py:293
  3.8 3.0 %collective-permute-start.10 = (bf16[144,512]{1,0:T(8,128)(2,1)S(1)}, bf16[144,512]{1,0:T(8,128)(2,1)S(1)}, u32[]{:S(2)}, u32[]{:S(2)}) collective-permute-start(bf16[144,512]{1,0:T(8,128)(2,1)S(1)} %get-tuple-element.9), channel_id=1, source_target_pairs={{0,8},{8,0},{16,24},{24,16},{1,9},{9,1},{17,25},{25,17},{2,10},{10... | collective-permute-start | bytes 442376 | tf_op jit(solution)/shard_map/ppermute | solution.py:22
  6.8 1.5 %collective-permute-start.11 = (bf16[144,512]{1,0:T(8,128)(2,1)S(1)}, bf16[144,512]{1,0:T(8,128)(2,1)S(1)}, u32[]{:S(2)}, u32[]{:S(2)}) collective-permute-start(bf16[144,512]{1,0:T(8,128)(2,1)S(1)} %get-tuple-element.10), channel_id=1, source_target_pairs={{0,16},{8,24},{16,0},{24,8},{1,17},{9,25},{17,1},{25,9},{2,18},{10... | collective-permute-start | bytes 442376 | tf_op jit(solution)/shard_map/ppermute | solution.py:22
  8.4 0.0 collective-permute-start.12
  8.4 0.1 pad_add_fusion.1.place_ref
  8.4 2.7 %collective-permute-done.10.refs_1_ = bf16[144,512]{1,0:T(8,128)(2,1)S(1)} collective-permute-done((bf16[144,512]{1,0:T(8,128)(2,1)S(1)}, bf16[144,512]{1,0:T(8,128)(2,1)S(1)}, u32[]{:S(2)}, u32[]{:S(2)}) %collective-permute-start.10) | collective-permute-done | bytes 147488 | tf_op jit(solution)/shard_map/ppermute | solution.py:22
  11.1 4.2 %collective-permute-done.11.refs_2_ = bf16[144,512]{1,0:T(8,128)(2,1)S(1)} collective-permute-done((bf16[144,512]{1,0:T(8,128)(2,1)S(1)}, bf16[144,512]{1,0:T(8,128)(2,1)S(1)}, u32[]{:S(2)}, u32[]{:S(2)}) %collective-permute-start.11) | collective-permute-done | bytes 147488 | tf_op jit(solution)/shard_map/ppermute | solution.py:22
  15.3 0.0 collective-permute-done.12.refs_3_
  15.3 1.3 %scatter.1 = (f32[512,512]{1,0:T(8,128)S(1)}, bf16[512,512]{1,0:T(8,128)(2,1)S(1)}) custom-call(s32[2]{0:T(128)S(1)} %pad_add_fusion.1.place_ref, bf16[144,512]{1,0:T(8,128)(2,1)S(1)} %get-tuple-element.8.refs_0_, bf16[144,512]{1,0:T(8,128)(2,1)S(1)} %collective-permute-done.10.refs_1_, bf16[144,512]{1,0:T(8,128)(2,1)S(1)} %collective-permute-done.11.refs_2_, ...), custom_call_target="tpu_custom_call" | custom-call | tf_op jit(solution)/shard_map/scatter/pallas_call | solution.py:304
  16.6 0.1 collective-permute-start.13
  16.7 0.5 collective-permute-start.8
  17.2 1.9 %constant_dynamic-slice_fusion = bf16[512,512]{1,0:T(8,128)(2,1)} fusion(bf16[1024,512]{1,0:T(8,128)(2,1)} %table_ref.1, s32[]{:T(128)S(6)} %select_n.69), kind=kLoop, calls=%fused_computation.26 | loop fusion | bytes 1048580 | tf_op jit(solution)/shard_map/dynamic_slice | solution.py:269
  19.0 1.2 %collective-permute-start.2 = (bf16[512,512]{1,0:T(8,128)(2,1)}, bf16[512,512]{1,0:T(8,128)(2,1)S(1)}, u32[]{:S(2)}, u32[]{:S(2)}) collective-permute-start(bf16[512,512]{1,0:T(8,128)(2,1)} %constant_dynamic-slice_fusion), channel_id=1, source_target_pairs={{0,8},{1,17},{8,0},{9,25},{16,24},{17,1},{24,16},{25,9},{2,10},{3,... | collective-permute-start | bytes 1572872 | tf_op jit(solution)/shard_map/ppermute | solution.py:267
  20.3 0.0 collective-permute-done.13
  20.3 0.8 %copy-done.7 = bf16[512,512]{1,0:T(8,128)(2,1)} copy-done((bf16[512,512]{1,0:T(8,128)(2,1)}, bf16[512,512]{1,0:T(8,128)(2,1)S(1)}, u32[]{:S(2)}) %copy-start.7) | copy-done | bytes 524312
  21.1 1.3 %convert_add_fusion = f32[512,512]{1,0:T(8,128)S(1)} fusion(f32[512,512]{1,0:T(8,128)S(1)} %get-tuple-element.12, bf16[512,512]{1,0:T(8,128)(2,1)} %copy-done.7), kind=kLoop, calls=%fused_computation | loop fusion | flops 524288 | bytes 2621440 | tf_op jit(solution)/shard_map/add | solution.py:315
  22.4 0.0 copy-start.6
  22.4 1.0 %copy-done.6 = f32[512,512]{1,0:T(8,128)} copy-done((f32[512,512]{1,0:T(8,128)}, f32[512,512]{1,0:T(8,128)S(1)}, u32[]{:S(2)}) %copy-start.6) | copy-done | bytes 1048600
  23.4 1.6 %collective-permute-start.14 = (bf16[2,128,512]{2,1,0:T(8,128)(2,1)S(1)}, bf16[2,128,512]{2,1,0:T(8,128)(2,1)S(1)}, u32[]{:S(2)}, u32[]{:S(2)}) collective-permute-start(bf16[2,128,512]{2,1,0:T(8,128)(2,1)S(1)} %fusion.2), channel_id=1, source_target_pairs={{0,2},{2,0},{4,6},{6,4},{1,3},{3,1},{5,7},{7,5},{8,10},{10,8},{12,... | collective-permute-start | bytes 786440 | tf_op jit(solution)/shard_map/ppermute | solution.py:22
  25.1 2.3 %collective-permute-start.1 = (s32[1,256]{1,0:T(1,128)S(1)}, s32[1,256]{1,0:T(1,128)S(1)}, u32[]{:S(2)}, u32[]{:S(2)}) collective-permute-start(s32[1,256]{1,0:T(1,128)S(1)} %get-tuple-element.14), channel_id=1, source_target_pairs={{0,2},{2,4},{4,6},{1,3},{3,5},{5,7},{8,10},{10,12},{12,14},{9,11},... | collective-permute-start | bytes 3080 | tf_op jit(solution)/shard_map/ppermute | solution.py:286
  27.4 4.5 %collective-permute-start = (s32[1,256]{1,0:T(1,128)S(1)}, s32[1,256]{1,0:T(1,128)S(1)}, u32[]{:S(2)}, u32[]{:S(2)}) collective-permute-start(s32[1,256]{1,0:T(1,128)S(1)} %get-tuple-element.14), channel_id=1, source_target_pairs={{0,4},{2,6},{1,5},{3,7},{8,12},{10,14},{9,13},{11,15},{16,20},{18,... | collective-permute-start | bytes 3080 | tf_op jit(solution)/shard_map/ppermute | solution.py:286
  32.0 0.0 collective-permute-done.2.near_ref
  32.0 0.9 %collective-permute-start.3 = (bf16[512,512]{1,0:T(8,128)(2,1)}, bf16[512,512]{1,0:T(8,128)(2,1)S(1)}, u32[]{:S(2)}, u32[]{:S(2)}) collective-permute-start(bf16[512,512]{1,0:T(8,128)(2,1)} %constant_dynamic-slice_fusion), channel_id=1, source_target_pairs={{0,16},{1,9},{8,24},{9,1},{16,0},{17,25},{24,8},{25,17},{2,18},{3,... | collective-permute-start | bytes 1572872 | tf_op jit(solution)/shard_map/ppermute | solution.py:267
  32.9 0.0 collective-permute-done.14
  32.9 1.2 %collective-permute-start.4 = (bf16[512,512]{1,0:T(8,128)(2,1)S(1)}, bf16[512,512]{1,0:T(8,128)(2,1)S(1)}, u32[]{:S(2)}, u32[]{:S(2)}) collective-permute-start(bf16[512,512]{1,0:T(8,128)(2,1)S(1)} %collective-permute-done.2.near_ref), channel_id=1, source_target_pairs={{0,16},{1,9},{8,24},{9,1},{16,0},{17,25},{24,8},{25,17},{2,18},{3,... | collective-permute-start | bytes 1572872 | tf_op jit(solution)/shard_map/ppermute | solution.py:267
  34.1 1.1 %fusion.1 = f32[1,2,128,512]{3,2,1,0:T(8,128)S(1)} fusion(bf16[2,128,512]{2,1,0:T(8,128)(2,1)S(1)} %collective-permute-done.14, f32[2,2,128,512]{3,2,1,0:T(8,128)} %bitcast.35), kind=kLoop, calls=%fused_computation.4 | loop fusion | flops 262144 | bytes 1310720 | tf_op jit(solution)/shard_map/reshape | solution.py:318
  35.2 0.0 collective-permute-done.1
  35.2 0.9 %collective-permute-start.15 = (bf16[1,128,512]{2,1,0:T(8,128)(2,1)S(1)}, bf16[1,128,512]{2,1,0:T(8,128)(2,1)S(1)}, u32[]{:S(2)}, u32[]{:S(2)}) collective-permute-start(bf16[1,128,512]{2,1,0:T(8,128)(2,1)S(1)} %fusion.5), channel_id=1, source_target_pairs={{0,4},{2,6},{4,0},{6,2},{1,5},{3,7},{5,1},{7,3},{8,12},{10,14},{12... | collective-permute-start | bytes 393224 | tf_op jit(solution)/shard_map/ppermute | solution.py:22
  36.1 0.0 collective-permute-done
  36.1 0.1 collective-permute-start.9
  36.2 5.2 %collective-permute-done.3.next_ref = bf16[512,512]{1,0:T(8,128)(2,1)S(1)} collective-permute-done((bf16[512,512]{1,0:T(8,128)(2,1)}, bf16[512,512]{1,0:T(8,128)(2,1)S(1)}, u32[]{:S(2)}, u32[]{:S(2)}) %collective-permute-start.3) | collective-permute-done | bytes 524320 | tf_op jit(solution)/shard_map/ppermute | solution.py:267
  41.4 0.0 collective-permute-start.5
  41.4 5.6 %collective-permute-done.4.far_ref = bf16[512,512]{1,0:T(8,128)(2,1)S(1)} collective-permute-done((bf16[512,512]{1,0:T(8,128)(2,1)S(1)}, bf16[512,512]{1,0:T(8,128)(2,1)S(1)}, u32[]{:S(2)}, u32[]{:S(2)}) %collective-permute-start.4) | collective-permute-done | bytes 524320 | tf_op jit(solution)/shard_map/ppermute | solution.py:267
  47.0 0.0 collective-permute-start.6
  47.0 0.0 collective-permute-done.15
  47.0 0.5 collective-permute-start.7
  47.6 0.7 %fusion.4 = f32[128,512]{1,0:T(8,128)} fusion(f32[1,2,128,512]{3,2,1,0:T(8,128)S(1)} %fusion.1, bf16[1,128,512]{2,1,0:T(8,128)(2,1)S(1)} %collective-permute-done.15), kind=kLoop, calls=%fused_computation.9 | loop fusion | flops 131072 | bytes 655360 | tf_op jit(solution)/shard_map/reshape | solution.py:322
  48.3 0.0 collective-permute-done.9.outw_other
  48.3 0.0 collective-permute-done.5.near2_ref
  48.3 0.6 collective-permute-done.6.next2_ref
  48.9 0.7 %collective-permute-done.7.far2_ref = bf16[512,512]{1,0:T(8,128)(2,1)S(1)} collective-permute-done((bf16[512,512]{1,0:T(8,128)(2,1)S(1)}, bf16[512,512]{1,0:T(8,128)(2,1)S(1)}, u32[]{:S(2)}, u32[]{:S(2)}) %collective-permute-start.7) | collective-permute-done | bytes 524320 | tf_op jit(solution)/shard_map/ppermute | solution.py:22
  49.7 0.0 collective-permute-done.8.proj_other
  49.7 0.0 copy-done
  49.7 15.3 %sections.1 = bf16[256,512]{1,0:T(8,128)(2,1)} custom-call(s32[2]{0:T(128)S(1)} %pad_add_fusion.1.place_ref, s32[1,2,2]{2,1,0:T(2,128)S(1)} %copy-done.5, s32[3,256]{1,0:T(4,128)S(1)} %pad_add_fusion.ids_ref, bf16[1024,512]{1,0:T(8,128)(2,1)S(1)} %copy-done, bf16[512,512]{1,0:T(8,128)(2,1)S(1)} %collective-permute-done.2.near_ref, ...), custom_call_target="tpu_custom_call" | custom-call | tf_op jit(solution)/shard_map/sections/pallas_call | solution.py:325
  (14 shorter events, 0.1 us)
Async XLA Ops:
  1.4 1.0 %copy-start.2 = (bf16[1,1,256,512]{3,2,1,0:T(8,128)(2,1)S(1)}, bf16[1,1,256,512]{3,2,1,0:T(8,128)(2,1)}, u32[]{:S(2)}) copy-start(bf16[1,1,256,512]{3,2,1,0:T(8,128)(2,1)} %param.12) | copy-start | bytes 786436
  2.3 0.7 %copy-start.3 = (s32[1,1,256]{2,1,0:T(1,128)S(1)}, s32[1,1,256]{2,1,0:T(1,128)}, u32[]{:S(2)}) copy-start(s32[1,1,256]{2,1,0:T(1,128)} %param.10) | copy-start | bytes 3076
  3.8 7.3 %collective-permute-start.10 = (bf16[144,512]{1,0:T(8,128)(2,1)S(1)}, bf16[144,512]{1,0:T(8,128)(2,1)S(1)}, u32[]{:S(2)}, u32[]{:S(2)}) collective-permute-start(bf16[144,512]{1,0:T(8,128)(2,1)S(1)} %get-tuple-element.9), channel_id=1, source_target_pairs={{0,8},{8,0},{16,24},{24,16},{1,9},{9,1},{17,25},{25,17},{2,10},{10... | collective-permute-start | bytes 442376 | tf_op jit(solution)/shard_map/ppermute | solution.py:22
  6.8 8.5 %collective-permute-start.11 = (bf16[144,512]{1,0:T(8,128)(2,1)S(1)}, bf16[144,512]{1,0:T(8,128)(2,1)S(1)}, u32[]{:S(2)}, u32[]{:S(2)}) collective-permute-start(bf16[144,512]{1,0:T(8,128)(2,1)S(1)} %get-tuple-element.10), channel_id=1, source_target_pairs={{0,16},{8,24},{16,0},{24,8},{1,17},{9,25},{17,1},{25,9},{2,18},{10... | collective-permute-start | bytes 442376 | tf_op jit(solution)/shard_map/ppermute | solution.py:22
  8.4 6.9 %collective-permute-start.12 = (bf16[144,512]{1,0:T(8,128)(2,1)S(1)}, bf16[144,512]{1,0:T(8,128)(2,1)S(1)}, u32[]{:S(2)}, u32[]{:S(2)}) collective-permute-start(bf16[144,512]{1,0:T(8,128)(2,1)S(1)} %get-tuple-element.11), channel_id=1, source_target_pairs={{0,24},{8,16},{16,8},{24,0},{1,25},{9,17},{17,9},{25,1},{2,26},{10... | collective-permute-start | bytes 442376 | tf_op jit(solution)/shard_map/ppermute | solution.py:22
  16.6 3.7 %collective-permute-start.13 = (bf16[512,512]{1,0:T(8,128)(2,1)S(1)}, bf16[512,512]{1,0:T(8,128)(2,1)S(1)}, u32[]{:S(2)}, u32[]{:S(2)}) collective-permute-start(bf16[512,512]{1,0:T(8,128)(2,1)S(1)} %get-tuple-element.13), channel_id=1, source_target_pairs={{0,1},{1,0},{2,3},{3,2},{4,5},{5,4},{6,7},{7,6},{8,9},{9,8},{10,11... | collective-permute-start | bytes 1572872 | tf_op jit(solution)/shard_map/ppermute | solution.py:22
  16.7 33.0 %collective-permute-start.8 = (bf16[1,512,2048]{2,1,0:T(8,128)(2,1)}, bf16[1,512,2048]{2,1,0:T(8,128)(2,1)}, u32[]{:S(2)}, u32[]{:S(2)}) collective-permute-start(bf16[1,512,2048]{2,1,0:T(8,128)(2,1)} %proj_own.1), channel_id=1, source_target_pairs={{0,1},{1,0},{2,3},{3,2},{4,5},{5,4},{6,7},{7,6},{8,9},{9,8},{10,11... | collective-permute-start | bytes 6291464 | tf_op jit(solution)/shard_map/ppermute | solution.py:22
  19.0 12.9 %collective-permute-start.2 = (bf16[512,512]{1,0:T(8,128)(2,1)}, bf16[512,512]{1,0:T(8,128)(2,1)S(1)}, u32[]{:S(2)}, u32[]{:S(2)}) collective-permute-start(bf16[512,512]{1,0:T(8,128)(2,1)} %constant_dynamic-slice_fusion), channel_id=1, source_target_pairs={{0,8},{1,17},{8,0},{9,25},{16,24},{17,1},{24,16},{25,9},{2,10},{3,... | collective-permute-start | bytes 1572872 | tf_op jit(solution)/shard_map/ppermute | solution.py:267
  20.3 0.8 %copy-start.7 = (bf16[512,512]{1,0:T(8,128)(2,1)}, bf16[512,512]{1,0:T(8,128)(2,1)S(1)}, u32[]{:S(2)}) copy-start(bf16[512,512]{1,0:T(8,128)(2,1)S(1)} %collective-permute-done.13) | copy-start | bytes 1572868
  21.1 15.1 %copy-start.1 = (bf16[1,512,512]{2,1,0:T(8,128)(2,1)S(1)}, bf16[1,512,512]{2,1,0:T(8,128)(2,1)}, u32[]{:S(2)}) copy-start(bf16[1,512,512]{2,1,0:T(8,128)(2,1)} %outw_own.1) | copy-start | bytes 1572868
  21.1 28.6 %copy-start = (bf16[1024,512]{1,0:T(8,128)(2,1)S(1)}, bf16[1024,512]{1,0:T(8,128)(2,1)}, u32[]{:S(2)}) copy-start(bf16[1024,512]{1,0:T(8,128)(2,1)} %table_ref.1) | copy-start | bytes 3145732
  21.1 28.6 %copy-start.4 = (f32[512]{0:T(512)S(1)}, f32[512]{0:T(512)}, u32[]{:S(2)}) copy-start(f32[512]{0:T(512)} %param.15) | copy-start | bytes 6148
  21.1 28.6 %copy-start.5 = (s32[1,2,2]{2,1,0:T(2,128)S(1)}, s32[1,2,2]{2,1,0:T(2,128)}, u32[]{:S(2)}) copy-start(s32[1,2,2]{2,1,0:T(2,128)} %lengths_ref.1) | copy-start | bytes 52
  22.4 1.0 %copy-start.6 = (f32[512,512]{1,0:T(8,128)}, f32[512,512]{1,0:T(8,128)S(1)}, u32[]{:S(2)}) copy-start(f32[512,512]{1,0:T(8,128)S(1)} %convert_add_fusion) | copy-start | bytes 3145732
  23.4 9.4 %collective-permute-start.14 = (bf16[2,128,512]{2,1,0:T(8,128)(2,1)S(1)}, bf16[2,128,512]{2,1,0:T(8,128)(2,1)S(1)}, u32[]{:S(2)}, u32[]{:S(2)}) collective-permute-start(bf16[2,128,512]{2,1,0:T(8,128)(2,1)S(1)} %fusion.2), channel_id=1, source_target_pairs={{0,2},{2,0},{4,6},{6,4},{1,3},{3,1},{5,7},{7,5},{8,10},{10,8},{12,... | collective-permute-start | bytes 786440 | tf_op jit(solution)/shard_map/ppermute | solution.py:22
  25.1 10.1 %collective-permute-start.1 = (s32[1,256]{1,0:T(1,128)S(1)}, s32[1,256]{1,0:T(1,128)S(1)}, u32[]{:S(2)}, u32[]{:S(2)}) collective-permute-start(s32[1,256]{1,0:T(1,128)S(1)} %get-tuple-element.14), channel_id=1, source_target_pairs={{0,2},{2,4},{4,6},{1,3},{3,5},{5,7},{8,10},{10,12},{12,14},{9,11},... | collective-permute-start | bytes 3080 | tf_op jit(solution)/shard_map/ppermute | solution.py:286
  27.4 8.7 %collective-permute-start = (s32[1,256]{1,0:T(1,128)S(1)}, s32[1,256]{1,0:T(1,128)S(1)}, u32[]{:S(2)}, u32[]{:S(2)}) collective-permute-start(s32[1,256]{1,0:T(1,128)S(1)} %get-tuple-element.14), channel_id=1, source_target_pairs={{0,4},{2,6},{1,5},{3,7},{8,12},{10,14},{9,13},{11,15},{16,20},{18,... | collective-permute-start | bytes 3080 | tf_op jit(solution)/shard_map/ppermute | solution.py:286
  32.0 9.5 %collective-permute-start.3 = (bf16[512,512]{1,0:T(8,128)(2,1)}, bf16[512,512]{1,0:T(8,128)(2,1)S(1)}, u32[]{:S(2)}, u32[]{:S(2)}) collective-permute-start(bf16[512,512]{1,0:T(8,128)(2,1)} %constant_dynamic-slice_fusion), channel_id=1, source_target_pairs={{0,16},{1,9},{8,24},{9,1},{16,0},{17,25},{24,8},{25,17},{2,18},{3,... | collective-permute-start | bytes 1572872 | tf_op jit(solution)/shard_map/ppermute | solution.py:267
  32.9 14.2 %collective-permute-start.4 = (bf16[512,512]{1,0:T(8,128)(2,1)S(1)}, bf16[512,512]{1,0:T(8,128)(2,1)S(1)}, u32[]{:S(2)}, u32[]{:S(2)}) collective-permute-start(bf16[512,512]{1,0:T(8,128)(2,1)S(1)} %collective-permute-done.2.near_ref), channel_id=1, source_target_pairs={{0,16},{1,9},{8,24},{9,1},{16,0},{17,25},{24,8},{25,17},{2,18},{3,... | collective-permute-start | bytes 1572872 | tf_op jit(solution)/shard_map/ppermute | solution.py:267
  35.2 11.8 %collective-permute-start.15 = (bf16[1,128,512]{2,1,0:T(8,128)(2,1)S(1)}, bf16[1,128,512]{2,1,0:T(8,128)(2,1)S(1)}, u32[]{:S(2)}, u32[]{:S(2)}) collective-permute-start(bf16[1,128,512]{2,1,0:T(8,128)(2,1)S(1)} %fusion.5), channel_id=1, source_target_pairs={{0,4},{2,6},{4,0},{6,2},{1,5},{3,7},{5,1},{7,3},{8,12},{10,14},{12... | collective-permute-start | bytes 393224 | tf_op jit(solution)/shard_map/ppermute | solution.py:22
  36.1 12.2 %collective-permute-start.9 = (bf16[1,512,512]{2,1,0:T(8,128)(2,1)S(1)}, bf16[1,512,512]{2,1,0:T(8,128)(2,1)S(1)}, u32[]{:S(2)}, u32[]{:S(2)}) collective-permute-start(bf16[1,512,512]{2,1,0:T(8,128)(2,1)S(1)} %copy-done.1), channel_id=1, source_target_pairs={{0,1},{1,0},{2,3},{3,2},{4,5},{5,4},{6,7},{7,6},{8,9},{9,8},{10,11... | collective-permute-start | bytes 1572872 | tf_op jit(solution)/shard_map/ppermute | solution.py:22
  41.4 6.9 %collective-permute-start.5 = (bf16[512,512]{1,0:T(8,128)(2,1)S(1)}, bf16[512,512]{1,0:T(8,128)(2,1)S(1)}, u32[]{:S(2)}, u32[]{:S(2)}) collective-permute-start(bf16[512,512]{1,0:T(8,128)(2,1)S(1)} %collective-permute-done.2.near_ref), channel_id=1, source_target_pairs={{0,1},{1,0},{2,3},{3,2},{4,5},{5,4},{6,7},{7,6},{8,9},{9,8},{10,11... | collective-permute-start | bytes 1572872 | tf_op jit(solution)/shard_map/ppermute | solution.py:22
  47.0 1.9 %collective-permute-start.6 = (bf16[512,512]{1,0:T(8,128)(2,1)S(1)}, bf16[512,512]{1,0:T(8,128)(2,1)S(1)}, u32[]{:S(2)}, u32[]{:S(2)}) collective-permute-start(bf16[512,512]{1,0:T(8,128)(2,1)S(1)} %collective-permute-done.3.next_ref), channel_id=1, source_target_pairs={{0,1},{1,0},{2,3},{3,2},{4,5},{5,4},{6,7},{7,6},{8,9},{9,8},{10,11... | collective-permute-start | bytes 1572872 | tf_op jit(solution)/shard_map/ppermute | solution.py:22
  47.0 2.7 %collective-permute-start.7 = (bf16[512,512]{1,0:T(8,128)(2,1)S(1)}, bf16[512,512]{1,0:T(8,128)(2,1)S(1)}, u32[]{:S(2)}, u32[]{:S(2)}) collective-permute-start(bf16[512,512]{1,0:T(8,128)(2,1)S(1)} %collective-permute-done.4.far_ref), channel_id=1, source_target_pairs={{0,1},{1,0},{2,3},{3,2},{4,5},{5,4},{6,7},{7,6},{8,9},{9,8},{10,11... | collective-permute-start | bytes 1572872 | tf_op jit(solution)/shard_map/ppermute | solution.py:22

commit v2 on v1

v2 whole, which is shorter than its diff:
```python
import functools

import jax
import jax.numpy as jnp
from jax import lax
from jax.experimental import pallas as pl
from jax.experimental.pallas import tpu as pltpu
from jax.sharding import PartitionSpec as P

HEADS = 4
HEAD_DIM = 128
INNER = HEADS * HEAD_DIM
SLOT_BASE = 128
CODE_ROWS = 16

norm_eps = 1e-05

NT = (((1,), (1,)), ((), ()))


def exchanged(shard, axis, by):
    count = lax.axis_size(axis)
    return lax.ppermute(shard, axis, [(i, i ^ by) for i in range(count)])


def layer_norm(values):
    average = jnp.mean(values, axis=-1, keepdims=True)
    centered = values - average
    return centered * lax.rsqrt(jnp.mean(centered * centered, axis=-1, keepdims=True) + norm_eps)


def silu(values):
    half = 0.5 * values
    return half * jnp.tanh(half) + half


def dot(left, right):
    return jnp.dot(left, right, preferred_element_type=jnp.float32)


def as_column(row):
    count = row.shape[1]
    down = lax.broadcasted_iota(jnp.int32, (count, count), 0)
    along = lax.broadcasted_iota(jnp.int32, (count, count), 1)
    picked = jnp.where(down == along, jnp.broadcast_to(row, (count, count)), 0.0)
    return jnp.sum(picked, axis=1, keepdims=True)


def coded(numbers):
    high = numbers // SLOT_BASE
    low = numbers - high * SLOT_BASE
    line = lax.broadcasted_iota(jnp.int32, (CODE_ROWS, numbers.shape[1]), 0)
    codes = jnp.where(line == 0, high, jnp.where(line == 1, low, 0)).astype(jnp.float32)
    return codes.astype(jnp.bfloat16)


def decoded(codes):
    codes = codes.astype(jnp.float32)
    return codes[0:1] * SLOT_BASE + codes[1:2]


def pack_kernel(
    parties, capacity, owned, place_ref, owner_ref, slot_ref, grad_ref, *packed_refs
):
    ids_ref = packed_refs[parties]
    my_phase = place_ref[1]
    owner = owner_ref[...] ^ place_ref[2]
    slot = slot_ref[...]
    count = owner.shape[1]
    width = grad_ref.shape[1]
    half = owned // 2
    swapped = (owner // 2) | ((owner % 2) * 2)
    turned = jnp.where(my_phase == 0, owner, swapped)
    moved = slot + my_phase * half
    moved = jnp.where(moved >= owned, moved - owned, moved)
    ids_ref[...] = turned * owned + jnp.where(turned == 3, moved, slot)
    before = (
        lax.broadcasted_iota(jnp.int32, (count, count), 0)
        < lax.broadcasted_iota(jnp.int32, (count, count), 1)
    ).astype(jnp.bfloat16)
    codes = coded(slot + SLOT_BASE)
    place = lax.broadcasted_iota(jnp.int32, (capacity, count), 0)
    chosen = []
    for party in range(parties):
        named = owner == party
        flags = jnp.broadcast_to(named, (CODE_ROWS, count)).astype(jnp.float32)
        rank = dot(flags.astype(jnp.bfloat16), before)[0:1].astype(jnp.int32)
        picks = (named & (rank == place)).astype(jnp.float32).astype(jnp.bfloat16)
        chosen.append(picks)
        sent = lax.dot_general(codes, picks, NT, preferred_element_type=jnp.float32)
        packed_refs[party][capacity : capacity + CODE_ROWS, :] = jnp.concatenate(
            [sent, jnp.zeros((CODE_ROWS, width - capacity), jnp.float32)], axis=1
        ).astype(jnp.bfloat16)
    for party in range(parties):
        rows = dot(chosen[party], grad_ref[...])
        packed_refs[party][0:capacity, :] = rows.astype(jnp.bfloat16)


def scatter_kernel(parties, capacity, row_ids, place_ref, *refs):
    arrived = refs[:parties]
    keep_ref, send_ref = refs[parties:]
    rows, phases = row_ids
    my_row, my_phase = place_ref[0], place_ref[1]
    block = keep_ref.shape[0] // rows
    values = jnp.concatenate([ref[0:capacity, :] for ref in arrived], axis=0)
    slots = [
        decoded(ref[capacity : capacity + CODE_ROWS, 0:capacity]) - SLOT_BASE for ref in arrived
    ]
    slots = jnp.concatenate(slots, axis=1).astype(jnp.int32)
    down = lax.broadcasted_iota(jnp.int32, (block, parties * capacity), 0)
    for other in range(phases):
        for step in range(rows):
            base = ((my_row ^ step) * phases + (my_phase ^ other)) * block
            chosen = (slots - base == down).astype(jnp.float32).astype(jnp.bfloat16)
            total = dot(chosen, values)
            if other == 0:
                keep_ref[step * block : (step + 1) * block, :] = total
            else:
                send_ref[step * block : (step + 1) * block, :] = total.astype(jnp.bfloat16)


def combine_kernel(block, kept_ref, come_ref, own_ref, *sent_refs):
    for step in range(len(sent_refs) + 1):
        part = slice(step * block, (step + 1) * block)
        total = kept_ref[part, :] + come_ref[part, :].astype(jnp.float32)
        if step == 0:
            own_ref[...] = total
        else:
            sent_refs[step - 1][...] = total.astype(jnp.bfloat16)


def finish_kernel(own_ref, *refs):
    total = own_ref[...]
    for come_ref in refs[:-1]:
        total = total + come_ref[...].astype(jnp.float32)
    refs[-1][...] = total


def loop(count, body):
    if count <= 4:
        for index in range(count):
            body(index)
    else:
        lax.fori_loop(0, count, lambda index, carry: (body(index), carry)[1], 0)


def rows_at(start, count, step):
    if isinstance(start, int):
        return pl.ds(start, count)
    return pl.ds(pl.multiple_of(start, step), count)


def tall_blocks(window):
    return window if window <= 4 else 1


def look_up(ids, pieces):
    total = None
    for base, piece in pieces:
        along = lax.broadcasted_iota(jnp.int32, (ids.shape[0], piece.shape[0]), 1)
        chosen = (along == ids - base).astype(jnp.float32).astype(jnp.bfloat16)
        part = dot(chosen, piece[...])
        total = part if total is None else total + part
    return total


def lookup_kernel(window, place_ref, ids_ref, table_ref, near_ref, next_ref, emb_ref, column_ref):
    my_row = place_ref[0]
    size = ids_ref.shape[1]
    owned = table_ref.shape[0]

    def column(index):
        row = my_row - (window - 1) + index
        ids = ids_ref[pl.ds(jnp.maximum(row, 0) ^ my_row, 1), :].astype(jnp.float32)
        return as_column(jnp.where(row >= 0, ids, -1.0))

    tall = tall_blocks(window)
    height = tall * size
    pieces = ((0, table_ref), (owned, near_ref), (2 * owned, next_ref))

    def step(index):
        ids = [column(index * tall + part) for part in range(tall)]
        ids = jnp.concatenate(ids, axis=0).astype(jnp.int32)
        emb_ref[rows_at(index * height, height, size), :] = look_up(ids, pieces)
        column_ref[rows_at(index * height, height, size), :] = ids - 3 * owned

    loop(window // tall, step)


def section_kernel(
    window,
    place_ref,
    lengths_ref,
    ids_ref,
    early_ref,
    far_ref,
    far2_ref,
    proj_own,
    proj_other,
    outw_own,
    outw_other,
    gain_ref,
    out_ref,
    proj_ref,
    outw_ref,
    emb_ref,
    act_ref,
    mid_ref,
    mix_ref,
    sems,
):
    my_row, my_phase = place_ref[0], place_ref[1]
    size = out_ref.shape[0]
    half = far_ref.shape[0]
    copies = [
        pltpu.make_async_copy(proj_own.at[0], proj_ref.at[my_phase], sems.at[0]),
        pltpu.make_async_copy(proj_other.at[0], proj_ref.at[1 - my_phase], sems.at[1]),
        pltpu.make_async_copy(outw_own.at[0], outw_ref.at[my_phase], sems.at[2]),
        pltpu.make_async_copy(outw_other.at[0], outw_ref.at[1 - my_phase], sems.at[3]),
    ]
    for copy in copies:
        copy.start()

    tall = tall_blocks(window)
    height = tall * size

    def rows(start, count=height):
        return rows_at(start, count, size)

    def late(step):
        part = rows(step * height)
        found = look_up(ids_ref[part, :], ((0, far_ref), (half, far2_ref)))
        emb_ref[part, :] = early_ref[part, :] + found

    loop(window // tall, late)
    copies[0].wait()
    copies[1].wait()

    first_pos = (my_row - (window - 1)) * size
    across = lax.broadcasted_iota(jnp.int32, (1, size), 1)

    def attend(start, count, key_start, diagonal):
        query_pos = first_pos + start + lax.broadcasted_iota(jnp.int32, (count, 1), 0)
        key_pos = first_pos + key_start + across
        earliest = jnp.zeros((count, 1), jnp.int32)
        bound = jnp.int32(0)
        for index in range(lengths_ref.shape[2] - 1):
            bound = bound + lengths_ref[0, my_phase, index]
            earliest = jnp.where(query_pos >= bound, bound, earliest)
        visible = key_pos >= earliest
        if diagonal:
            visible = visible & (key_pos <= query_pos)
        for head in range(HEADS):
            cols = head * HEAD_DIM
            queries = act_ref[rows(start, count), 2 * INNER + cols : 2 * INNER + cols + HEAD_DIM]
            keys = act_ref[rows(key_start, size), 3 * INNER + cols : 3 * INNER + cols + HEAD_DIM]
            values = act_ref[rows(key_start, size), INNER + cols : INNER + cols + HEAD_DIM]
            scores = lax.dot_general(queries, keys, NT, preferred_element_type=jnp.float32)
            weights = jnp.where(visible, silu(scores), 0.0).astype(jnp.bfloat16)
            mix_ref[rows(start, count), cols : cols + HEAD_DIM] += dot(weights, values)

    def project(start, count, section, parts):
        source = emb_ref if section == 0 else mid_ref
        values = source[rows(start, count), :].astype(jnp.float32)
        normed = layer_norm(values).astype(jnp.bfloat16)
        for part in parts:
            cols = part * INNER
            act = silu(dot(normed, proj_ref[section, :, cols : cols + INNER]))
            act_ref[rows(start, count), cols : cols + INNER] = act.astype(jnp.bfloat16)

    def finish(start, count, section):
        source = emb_ref if section == 0 else mid_ref
        values = source[rows(start, count), :].astype(jnp.float32)
        gates = act_ref[rows(start, count), 0:INNER].astype(jnp.float32)
        gated = (layer_norm(mix_ref[rows(start, count), :]) * gates).astype(jnp.bfloat16)
        return values + dot(gated, outw_ref[section])

    last = (window - 1) * size
    mix_ref[...] = jnp.zeros(mix_ref.shape, jnp.float32)
    loop(window // tall, lambda step: project(step * height, height, 0, (3, 2, 1, 0)))
    if tall == window:
        for block in range(window):
            attend(block * size, height - block * size, block * size, True)
    else:

        def with_keys(block):
            attend(block * size, size, block * size, True)
            lax.fori_loop(
                block + 1,
                window,
                lambda later, c: (attend(later * size, size, block * size, False), c)[1],
                0,
            )

        loop(window, with_keys)

    copies[2].wait()
    copies[3].wait()

    def close_first(step):
        mid_ref[rows(step * height), :] = finish(step * height, height, 0).astype(jnp.bfloat16)

    loop(window // tall, close_first)
    mix_ref[last : last + size, :] = jnp.zeros((size, INNER), jnp.float32)
    loop(window // tall, lambda step: project(step * height, height, 1, (3, 1)))
    project(last, size, 1, (2, 0))
    attend(last, size, last, True)
    loop(window - 1, lambda block: attend(last, size, block * size, False))
    closing = finish(last, size, 1)
    out_ref[...] = (layer_norm(closing) * gain_ref[...]).astype(jnp.bfloat16)


def body(
    item_table, item_owner, item_slot, seq_lengths, row_grads, proj_weight, out_weight, final_gain
):
    parties = lax.axis_size("emb")
    row_count = lax.axis_size("row")
    phases = lax.axis_size("phase")
    my_emb = lax.axis_index("emb")
    my_row = lax.axis_index("row")
    my_phase = lax.axis_index("phase")
    size = item_slot.shape[2]
    width = item_table.shape[1]
    owned = item_table.shape[0]
    half = owned // 2
    capacity = max(16, 2 * size // parties)
    window = -(-3 * row_count // 4)
    vmem = pltpu.MemorySpace.VMEM
    smem = pltpu.MemorySpace.SMEM

    def params(mebibytes):
        return pltpu.CompilerParams(vmem_limit_bytes=mebibytes * 1024 * 1024)

    def cost(products):
        return pl.CostEstimate(flops=2 * products, bytes_accessed=0, transcendentals=0)

    def across(shard, first):
        pairs = []
        for emb in range(parties):
            for phase in range(phases):
                by = 1 if (phase == 0) == first else 2
                pairs.append((emb * phases + phase, (emb ^ by) * phases + phase))
        return lax.ppermute(shard, ("emb", "phase"), pairs)

    place = jnp.stack([my_row, my_phase, my_emb]).astype(jnp.int32)
    proj_other = exchanged(proj_weight, "phase", 1)
    outw_other = exchanged(out_weight, "phase", 1)

    on_chip = pl.BlockSpec(memory_space=vmem)
    scalars = pl.BlockSpec(memory_space=smem)
    anywhere = pl.BlockSpec(memory_space=pl.ANY)

    def array(rows, dtype=jnp.bfloat16):
        return jax.ShapeDtypeStruct((rows, width), dtype)

    *packed, ids = pl.pallas_call(
        functools.partial(pack_kernel, parties, capacity, owned),
        out_shape=[array(capacity + CODE_ROWS)] * parties
        + [jax.ShapeDtypeStruct((1, size), jnp.int32)],
        in_specs=[scalars] + [on_chip] * 3,
        out_specs=[on_chip] * (parties + 1),
        compiler_params=params(8),
        name="pack",
    )(place, item_owner.reshape(1, size), item_slot.reshape(1, size), row_grads.reshape(size, width))
    arrived = [packed[0]] + [exchanged(packed[by], "emb", by) for by in range(1, parties)]
    by = 1
    while by < row_count:
        ids = jnp.concatenate([ids, exchanged(ids, "row", by)], axis=0)
        by *= 2
    near = across(item_table, True)
    near, ids, *arrived = lax.optimization_barrier((near, ids, *arrived))
    following = exchanged(near, "phase", 1)
    far = across(lax.dynamic_slice_in_dim(near, my_phase * half, half, 0), False)
    block = owned // (row_count * phases)
    count = row_count * block
    kept, sent = pl.pallas_call(
        functools.partial(scatter_kernel, parties, capacity, (row_count, phases)),
        out_shape=[array(count, jnp.float32), array(count)],
        in_specs=[scalars] + [on_chip] * parties,
        out_specs=[on_chip] * 2,
        compiler_params=params(8),
        name="scatter",
    )(place, *arrived)
    come = exchanged(sent, "phase", 1)
    own, *sent = pl.pallas_call(
        functools.partial(combine_kernel, block),
        out_shape=[array(block, jnp.float32)] + [array(block)] * (row_count - 1),
        in_specs=[on_chip] * 2,
        out_specs=[on_chip] * row_count,
        compiler_params=params(8),
        name="combine",
    )(kept, come)
    sums = [exchanged(sent[by - 1], "row", by) for by in range(1, row_count)]

    early, columns = pl.pallas_call(
        functools.partial(lookup_kernel, window),
        out_shape=[
            array(window * size, jnp.float32),
            jax.ShapeDtypeStruct((window * size, 1), jnp.int32),
        ],
        in_specs=[scalars] + [on_chip] * 4,
        out_specs=[on_chip] * 2,
        compiler_params=params(16 + 2 * window),
        cost_estimate=cost(window * size * 3 * owned * width),
        name="lookup",
    )(place, ids, item_table, near, following)
    far, early = lax.optimization_barrier((far, early))
    far2 = exchanged(far, "phase", 1)
    states = pl.pallas_call(
        functools.partial(section_kernel, window),
        out_shape=array(size),
        in_specs=[scalars] * 2 + [on_chip] * 4 + [anywhere] * 4 + [on_chip],
        out_specs=on_chip,
        scratch_shapes=[
            pltpu.VMEM((2,) + proj_weight.shape[1:], jnp.bfloat16),
            pltpu.VMEM((2,) + out_weight.shape[1:], jnp.bfloat16),
            pltpu.VMEM((window * size, width), jnp.float32),
            pltpu.VMEM((window * size, 4 * INNER), jnp.bfloat16),
            pltpu.VMEM((window * size, width), jnp.bfloat16),
            pltpu.VMEM((window * size, INNER), jnp.float32),
            pltpu.SemaphoreType.DMA((4,)),
        ],
        compiler_params=params(12 + 4 * window),
        cost_estimate=cost(8 * window * size * width * 2 * INNER),
        name="sections",
    )(
        place,
        seq_lengths,
        columns,
        early,
        far,
        far2,
        proj_weight,
        proj_other,
        out_weight,
        outw_other,
        final_gain.reshape(1, width),
    )
    own, states = lax.optimization_barrier((own, states))
    table_grad = pl.pallas_call(
        finish_kernel,
        out_shape=array(block, jnp.float32),
        in_specs=[on_chip] * row_count,
        out_specs=on_chip,
        compiler_params=params(8),
        name="finish",
    )(own, *sums)
    return (states.reshape(1, 1, size, width), table_grad)


def solution(mesh):
    placed = (
        P("emb", None),
        P("emb", "phase", "row", None),
        P("emb", "phase", "row"),
        P("emb", None, None),
        P("emb", "phase", "row", None),
        P("phase", None, None),
        P("phase", None, None),
        P(),
    )
    return jax.shard_map(
        body,
        mesh=mesh,
        in_specs=placed,
        out_specs=(P("emb", "phase", "row", None), P(("emb", "row", "phase"), None)),
        check_vma=False,
    )
```

time: 65.5 us -> 51.4 us (0.78)
  waiting for transfers between devices: 19.1 us -> 10.8 us
  other arithmetic: 3.99 us -> 0.09 us
  local copies, waits for them, and re-layouts: 5.35 us -> 3.71 us
  starting transfers between devices: 18.4 us -> 17 us
  Pallas kernels: 17.4 us -> 18.7 us
    ppermute x3 -> x2, waiting for transfers between devices: 10.8 us -> 1.24 us  [across(): return lax.ppermute(shard, ('emb', 'phase'), pairs)]
    ppermute x2 -> x0, starting transfers between devices: 6.84 us -> none  [body(): arrived_ids = lax.ppermute(ids, 'row', pairs)]
    ppermute x11 -> x13, starting transfers between devices: 8.25 us -> 14 us  [exchanged(): return lax.ppermute(shard, axis, [(i, i ^ by) for i in range(count)])]
    add x2 -> x0, other arithmetic: 2.05 us -> none  [the longest x1 1.34 us: body(): total = keep + exchanged(send, 'phase', 1).astype(jnp.float32)]
    reshape x2 -> x0, other arithmetic: 1.85 us -> none  [the longest x1 1.11 us: body(): total = total.reshape(-1, 2, block, width)]
    dynamic_slice x1, local copies, waits for them, and re-layouts: 1.87 us -> 0.03 us  [body(): lax.dynamic_slice_in_dim(near, my_phase * half, half, 0)]
    pallas_call x2 -> x5, Pallas kernels: 16.1 us -> 17.5 us  [the longest x1 12 us: body(): pl.pallas_call(functools.partial(section_kernel, window), out_shape=array...]
    ppermute x11 -> x13, waiting for transfers between devices: 8.26 us -> 9.56 us  [exchanged(): return lax.ppermute(shard, axis, [(i, i ^ by) for i in range(count)])]
  transfers between devices with their start and end apart: 16 -> 15, of which waited for: 6 -> 4; matrix products, arithmetic and copies ran while one was open for 8% -> 0% of each run, Pallas kernels for 0% -> 35%
where the time goes in v2:
time: 51.4 us; the launch traced here: 51.2 us
  Pallas kernels  18.7 us (36%)
  starting transfers between devices  17 us (33%)
  waiting for transfers between devices  10.8 us (21%)
  local copies, waits for them, and re-layouts  3.71 us (7%)
  between operations  0.78 us (2%)
    ppermute x13, starting transfers between devices, exchanged(): return lax.ppermute(shard, axis, [(i, i ^ by) for i in range(count)])  14 us
    pallas_call x1, Pallas kernels, body(): pl.pallas_call(functools.partial(section_kernel, window), out_shape=array...  12 us
    ppermute x13, waiting for transfers between devices, exchanged(): return lax.ppermute(shard, axis, [(i, i ^ by) for i in range(count)])  9.56 us
    unnamed x16, local copies, waits for them, and re-layouts  3.68 us
    pallas_call x1, Pallas kernels, body(): pl.pallas_call(functools.partial(lookup_kernel, window), out_shape=[array...  3.47 us
    ppermute x2, starting transfers between devices, across(): return lax.ppermute(shard, ('emb', 'phase'), pairs)  3.07 us
    pallas_call x1, Pallas kernels, body(): pl.pallas_call(functools.partial(scatter_kernel, parties, capacity, (row_...  1.27 us
    ppermute x2, waiting for transfers between devices, across(): return lax.ppermute(shard, ('emb', 'phase'), pairs)  1.24 us
  transfers between devices with their start and end apart: 15, of which 4 were waited for; matrix products, arithmetic and copies ran while one was open for 0% of the time, Pallas kernels for 35%

profile of v2, /device:TPU:0, one launch (start us, length us, event | category | flops | bytes accessed | tf_op | source)
XLA Modules:
  0.0 51.2 jit_solution(5886067255609310175)
XLA Ops:
  0.6 3.0 %collective-permute-start = (bf16[1024,512]{1,0:T(8,128)(2,1)}, bf16[1024,512]{1,0:T(8,128)(2,1)S(1)}, u32[]{:S(2)}, u32[]{:S(2)}) collective-permute-start(bf16[1024,512]{1,0:T(8,128)(2,1)} %table_ref.1), channel_id=1, source_target_pairs={{0,8},{1,17},{8,0},{9,25},{16,24},{17,1},{24,16},{25,9},{2,10},{3,... | collective-permute-start | bytes 3145736 | tf_op jit(solution)/shard_map/ppermute | solution.py:343
  3.6 0.0 collective-permute-start.10
  3.6 0.1 pad_add_fusion.2.place_ref
  3.7 0.9 %copy-done = bf16[1,1,256,512]{3,2,1,0:T(8,128)(2,1)S(1)} copy-done((bf16[1,1,256,512]{3,2,1,0:T(8,128)(2,1)S(1)}, bf16[1,1,256,512]{3,2,1,0:T(8,128)(2,1)}, u32[]{:S(2)}) %copy-start) | copy-done | bytes 262168
  4.7 0.7 %copy-done.1 = s32[1,1,256,1]{2,3,1,0:T(1,128)S(1)} copy-done((s32[1,1,256,1]{2,3,1,0:T(1,128)S(1)}, s32[1,1,256,1]{2,3,1,0:T(1,128)}, u32[]{:S(2)}) %copy-start.1) | copy-done | bytes 1048
  5.3 0.7 %copy-done.2 = s32[1,1,256]{2,1,0:T(1,128)S(1)} copy-done((s32[1,1,256]{2,1,0:T(1,128)S(1)}, s32[1,1,256]{2,1,0:T(1,128)}, u32[]{:S(2)}) %copy-start.2) | copy-done | bytes 1048
  6.0 1.1 %pack.1 = (bf16[144,512]{1,0:T(8,128)(2,1)S(1)}, bf16[144,512]{1,0:T(8,128)(2,1)S(1)}, bf16[144,512]{1,0:T(8,128)(2,1)S(1)}, bf16[144,512]{1,0:T(8,128)(2,1)S(1)}, s32[1,256]{1,0:T(1,128)S(1)}) custom-call(s32[3]{0:T(128)S(1)} %pad_add_fusion.2.place_ref, s32[1,256]{1,0:T(1,128)S(1)} %bitcast.9, s32[1,256]{1,0:T(1,128)S(1)} %bitcast.10, ...), custom_call_target="tpu_custom_call" | custom-call | tf_op jit(solution)/shard_map/pack/pallas_call | solution.py:356
  7.1 1.6 %collective-permute-start.1 = (s32[1,256]{1,0:T(1,128)S(1)}, s32[1,256]{1,0:T(1,128)S(1)}, u32[]{:S(2)}, u32[]{:S(2)}) collective-permute-start(s32[1,256]{1,0:T(1,128)S(1)} %get-tuple-element.25), channel_id=1, source_target_pairs={{0,2},{2,0},{4,6},{6,4},{1,3},{3,1},{5,7},{7,5},{8,10},{10,8},{12,... | collective-permute-start | bytes 3080 | tf_op jit(solution)/shard_map/ppermute | solution.py:23
  8.8 2.0 %collective-permute-done.1 = s32[1,256]{1,0:T(1,128)S(1)} collective-permute-done((s32[1,256]{1,0:T(1,128)S(1)}, s32[1,256]{1,0:T(1,128)S(1)}, u32[]{:S(2)}, u32[]{:S(2)}) %collective-permute-start.1) | collective-permute-done | bytes 1056 | tf_op jit(solution)/shard_map/ppermute | solution.py:23
  10.8 2.6 %collective-permute-start.2 = (s32[2,256]{1,0:T(2,128)S(1)}, s32[2,256]{1,0:T(2,128)S(1)}, u32[]{:S(2)}, u32[]{:S(2)}) collective-permute-start(s32[2,256]{1,0:T(2,128)S(1)} %pad_add_fusion.1), channel_id=1, source_target_pairs={{0,4},{2,6},{4,0},{6,2},{1,5},{3,7},{5,1},{7,3},{8,12},{10,14},{12... | collective-permute-start | bytes 6152 | tf_op jit(solution)/shard_map/ppermute | solution.py:23
  13.4 1.1 %collective-permute-start.3 = (bf16[144,512]{1,0:T(8,128)(2,1)S(1)}, bf16[144,512]{1,0:T(8,128)(2,1)S(1)}, u32[]{:S(2)}, u32[]{:S(2)}) collective-permute-start(bf16[144,512]{1,0:T(8,128)(2,1)S(1)} %get-tuple-element.27), channel_id=1, source_target_pairs={{0,8},{8,0},{16,24},{24,16},{1,9},{9,1},{17,25},{25,17},{2,10},{10... | collective-permute-start | bytes 442376 | tf_op jit(solution)/shard_map/ppermute | solution.py:23
  14.5 1.0 %collective-permute-start.4 = (bf16[144,512]{1,0:T(8,128)(2,1)S(1)}, bf16[144,512]{1,0:T(8,128)(2,1)S(1)}, u32[]{:S(2)}, u32[]{:S(2)}) collective-permute-start(bf16[144,512]{1,0:T(8,128)(2,1)S(1)} %get-tuple-element.28), channel_id=1, source_target_pairs={{0,16},{8,24},{16,0},{24,8},{1,17},{9,25},{17,1},{25,9},{2,18},{10... | collective-permute-start | bytes 442376 | tf_op jit(solution)/shard_map/ppermute | solution.py:23
  15.4 0.0 collective-permute-done.2
  15.4 1.4 %collective-permute-start.5 = (bf16[144,512]{1,0:T(8,128)(2,1)S(1)}, bf16[144,512]{1,0:T(8,128)(2,1)S(1)}, u32[]{:S(2)}, u32[]{:S(2)}) collective-permute-start(bf16[144,512]{1,0:T(8,128)(2,1)S(1)} %get-tuple-element.29), channel_id=1, source_target_pairs={{0,24},{8,16},{16,8},{24,0},{1,25},{9,17},{17,9},{25,1},{2,26},{10... | collective-permute-start | bytes 442376 | tf_op jit(solution)/shard_map/ppermute | solution.py:23
  16.9 4.1 %collective-permute-done.3.refs_1_ = bf16[144,512]{1,0:T(8,128)(2,1)S(1)} collective-permute-done((bf16[144,512]{1,0:T(8,128)(2,1)S(1)}, bf16[144,512]{1,0:T(8,128)(2,1)S(1)}, u32[]{:S(2)}, u32[]{:S(2)}) %collective-permute-start.3) | collective-permute-done | bytes 147488 | tf_op jit(solution)/shard_map/ppermute | solution.py:23
  21.0 0.0 collective-permute-done.4.refs_2_
  21.0 3.4 %collective-permute-done.5.refs_3_ = bf16[144,512]{1,0:T(8,128)(2,1)S(1)} collective-permute-done((bf16[144,512]{1,0:T(8,128)(2,1)S(1)}, bf16[144,512]{1,0:T(8,128)(2,1)S(1)}, u32[]{:S(2)}, u32[]{:S(2)}) %collective-permute-start.5) | collective-permute-done | bytes 147488 | tf_op jit(solution)/shard_map/ppermute | solution.py:23
  24.4 0.0 collective-permute-done.near_ref
  24.4 0.0 collective-permute-start.7
  24.5 0.1 collective-permute-start.8
  24.6 1.7 %collective-permute-start.11 = (bf16[1,512,512]{2,1,0:T(8,128)(2,1)}, bf16[1,512,512]{2,1,0:T(8,128)(2,1)S(1)}, u32[]{:S(2)}, u32[]{:S(2)}) collective-permute-start(bf16[1,512,512]{2,1,0:T(8,128)(2,1)} %outw_own.1), channel_id=1, source_target_pairs={{0,1},{1,0},{2,3},{3,2},{4,5},{5,4},{6,7},{7,6},{8,9},{9,8},{10,11... | collective-permute-start | bytes 1572872 | tf_op jit(solution)/shard_map/ppermute | solution.py:23
  26.3 1.3 %scatter.1 = (f32[512,512]{1,0:T(8,128)S(1)}, bf16[512,512]{1,0:T(8,128)(2,1)S(1)}) custom-call(s32[3]{0:T(128)S(1)} %pad_add_fusion.2.place_ref, bf16[144,512]{1,0:T(8,128)(2,1)S(1)} %get-tuple-element.30.refs_0_, bf16[144,512]{1,0:T(8,128)(2,1)S(1)} %collective-permute-done.3.refs_1_, bf16[144,512]{1,0:T(8,128)(2,1)S(1)} %collective-permute-done.4.refs_2_, ...), custom_call_target="tpu_custom_call" | custom-call | tf_op jit(solution)/shard_map/scatter/pallas_call | solution.py:376
  27.5 0.0 copy-start.7
  27.5 0.0 copy-start.3
  27.6 0.1 collective-permute-start.6
  27.6 0.0 collective-permute-done.7.next_ref
  27.6 0.0 copy-start.4
  27.7 1.3 %copy-done.4 = bf16[1024,512]{1,0:T(8,128)(2,1)S(1)} copy-done((bf16[1024,512]{1,0:T(8,128)(2,1)S(1)}, bf16[1024,512]{1,0:T(8,128)(2,1)}, u32[]{:S(2)}) %copy-start.4) | copy-done | bytes 1048600
  29.0 3.5 %lookup.1 = (f32[768,512]{1,0:T(8,128)S(1)}, s32[768,1]{1,0:T(8,128)S(1)}) custom-call(s32[3]{0:T(128)S(1)} %pad_add_fusion.2.place_ref, s32[4,256]{1,0:T(4,128)S(1)} %pad_add_fusion.ids_ref, bf16[1024,512]{1,0:T(8,128)(2,1)S(1)} %copy-done.4, bf16[1024,512]{1,0:T(8,128)(2,1)S(1)} %collective-permute-done.near_ref, ...), custom_call_target="tpu_custom_call" | custom-call | flops 2415919104 | tf_op jit(solution)/shard_map/lookup/pallas_call | solution.py:395
  32.5 1.2 %collective-permute-done.8.far_ref = bf16[512,512]{1,0:T(8,128)(2,1)S(1)} collective-permute-done((bf16[512,512]{1,0:T(8,128)(2,1)S(1)}, bf16[512,512]{1,0:T(8,128)(2,1)S(1)}, u32[]{:S(2)}, u32[]{:S(2)}) %collective-permute-start.8) | collective-permute-done | bytes 524320 | tf_op jit(solution)/shard_map/ppermute | solution.py:343
  33.7 0.0 collective-permute-start.9
  33.7 0.0 collective-permute-done.6.come_ref
  33.7 0.1 combine.1
  33.8 1.6 %collective-permute-start.12 = (bf16[128,512]{1,0:T(8,128)(2,1)S(1)}, bf16[128,512]{1,0:T(8,128)(2,1)S(1)}, u32[]{:S(2)}, u32[]{:S(2)}) collective-permute-start(bf16[128,512]{1,0:T(8,128)(2,1)S(1)} %get-tuple-element.45), channel_id=1, source_target_pairs={{0,2},{2,0},{4,6},{6,4},{1,3},{3,1},{5,7},{7,5},{8,10},{10,8},{12,... | collective-permute-start | bytes 393224 | tf_op jit(solution)/shard_map/ppermute | solution.py:23
  35.5 2.6 %collective-permute-start.13 = (bf16[128,512]{1,0:T(8,128)(2,1)S(1)}, bf16[128,512]{1,0:T(8,128)(2,1)S(1)}, u32[]{:S(2)}, u32[]{:S(2)}) collective-permute-start(bf16[128,512]{1,0:T(8,128)(2,1)S(1)} %get-tuple-element.46), channel_id=1, source_target_pairs={{0,4},{2,6},{4,0},{6,2},{1,5},{3,7},{5,1},{7,3},{8,12},{10,14},{12... | collective-permute-start | bytes 393224 | tf_op jit(solution)/shard_map/ppermute | solution.py:23
  38.1 0.0 collective-permute-done.11.outw_other
  38.1 0.2 collective-permute-start.14
  38.3 0.0 collective-permute-done.10.proj_other
  38.3 0.0 collective-permute-done.9.far2_ref
  38.3 0.0 copy-done.7
  38.3 0.0 copy-done.3
  38.3 0.0 copy-done.5
  38.3 0.0 copy-done.6
  38.3 12.0 %sections.1 = bf16[256,512]{1,0:T(8,128)(2,1)} custom-call(s32[3]{0:T(128)S(1)} %pad_add_fusion.2.place_ref, s32[1,2,2]{2,1,0:T(2,128)S(1)} %copy-done.7, s32[768,1]{1,0:T(8,128)S(1)} %get-tuple-element.39.ids_ref, f32[768,512]{1,0:T(8,128)S(1)} %get-tuple-element.41.early_ref, bf16[512,512]{1,0:T(8,128)(2,1)S(1)} %collective-permute-done.8.far_ref, ...), custom_call_target="tpu_custom_call" | custom-call | flops 6442450944 | tf_op jit(solution)/shard_map/sections/pallas_call | solution.py:409
  50.4 0.0 collective-permute-done.12.refs_0_
  50.4 0.0 collective-permute-done.13.refs_1_
  50.4 0.0 collective-permute-done.14.refs_2_
  50.4 0.8 %finish.1 = f32[128,512]{1,0:T(8,128)} custom-call(f32[128,512]{1,0:T(8,128)S(1)} %get-tuple-element.44.own_ref, bf16[128,512]{1,0:T(8,128)(2,1)S(1)} %collective-permute-done.12.refs_0_, bf16[128,512]{1,0:T(8,128)(2,1)S(1)} %collective-permute-done.13.refs_1_, bf16[128,512]{1,0:T(8,128)(2,1)S(1)} %collective-permute-done.14.refs_2_), custom_call_target="tpu_custom_call" | custom-call | tf_op jit(solution)/shard_map/finish/pallas_call | solution.py:440
  (8 shorter events, 0.1 us)
Async XLA Ops:
  0.6 23.8 %collective-permute-start = (bf16[1024,512]{1,0:T(8,128)(2,1)}, bf16[1024,512]{1,0:T(8,128)(2,1)S(1)}, u32[]{:S(2)}, u32[]{:S(2)}) collective-permute-start(bf16[1024,512]{1,0:T(8,128)(2,1)} %table_ref.1), channel_id=1, source_target_pairs={{0,8},{1,17},{8,0},{9,25},{16,24},{17,1},{24,16},{25,9},{2,10},{3,... | collective-permute-start | bytes 3145736 | tf_op jit(solution)/shard_map/ppermute | solution.py:343
  3.6 34.6 %collective-permute-start.10 = (bf16[1,512,2048]{2,1,0:T(8,128)(2,1)}, bf16[1,512,2048]{2,1,0:T(8,128)(2,1)}, u32[]{:S(2)}, u32[]{:S(2)}) collective-permute-start(bf16[1,512,2048]{2,1,0:T(8,128)(2,1)} %proj_own.1), channel_id=1, source_target_pairs={{0,1},{1,0},{2,3},{3,2},{4,5},{5,4},{6,7},{7,6},{8,9},{9,8},{10,11... | collective-permute-start | bytes 6291464 | tf_op jit(solution)/shard_map/ppermute | solution.py:23
  3.7 1.0 %copy-start = (bf16[1,1,256,512]{3,2,1,0:T(8,128)(2,1)S(1)}, bf16[1,1,256,512]{3,2,1,0:T(8,128)(2,1)}, u32[]{:S(2)}) copy-start(bf16[1,1,256,512]{3,2,1,0:T(8,128)(2,1)} %param.12) | copy-start | bytes 786436
  4.7 0.7 %copy-start.1 = (s32[1,1,256,1]{2,3,1,0:T(1,128)S(1)}, s32[1,1,256,1]{2,3,1,0:T(1,128)}, u32[]{:S(2)}) copy-start(s32[1,1,256,1]{2,3,1,0:T(1,128)} %param.9) | copy-start | bytes 3076
  5.3 0.7 %copy-start.2 = (s32[1,1,256]{2,1,0:T(1,128)S(1)}, s32[1,1,256]{2,1,0:T(1,128)}, u32[]{:S(2)}) copy-start(s32[1,1,256]{2,1,0:T(1,128)} %param.10) | copy-start | bytes 3076
  7.1 3.6 %collective-permute-start.1 = (s32[1,256]{1,0:T(1,128)S(1)}, s32[1,256]{1,0:T(1,128)S(1)}, u32[]{:S(2)}, u32[]{:S(2)}) collective-permute-start(s32[1,256]{1,0:T(1,128)S(1)} %get-tuple-element.25), channel_id=1, source_target_pairs={{0,2},{2,0},{4,6},{6,4},{1,3},{3,1},{5,7},{7,5},{8,10},{10,8},{12,... | collective-permute-start | bytes 3080 | tf_op jit(solution)/shard_map/ppermute | solution.py:23
  10.8 4.6 %collective-permute-start.2 = (s32[2,256]{1,0:T(2,128)S(1)}, s32[2,256]{1,0:T(2,128)S(1)}, u32[]{:S(2)}, u32[]{:S(2)}) collective-permute-start(s32[2,256]{1,0:T(2,128)S(1)} %pad_add_fusion.1), channel_id=1, source_target_pairs={{0,4},{2,6},{4,0},{6,2},{1,5},{3,7},{5,1},{7,3},{8,12},{10,14},{12... | collective-permute-start | bytes 6152 | tf_op jit(solution)/shard_map/ppermute | solution.py:23
  13.4 7.6 %collective-permute-start.3 = (bf16[144,512]{1,0:T(8,128)(2,1)S(1)}, bf16[144,512]{1,0:T(8,128)(2,1)S(1)}, u32[]{:S(2)}, u32[]{:S(2)}) collective-permute-start(bf16[144,512]{1,0:T(8,128)(2,1)S(1)} %get-tuple-element.27), channel_id=1, source_target_pairs={{0,8},{8,0},{16,24},{24,16},{1,9},{9,1},{17,25},{25,17},{2,10},{10... | collective-permute-start | bytes 442376 | tf_op jit(solution)/shard_map/ppermute | solution.py:23
  14.5 6.5 %collective-permute-start.4 = (bf16[144,512]{1,0:T(8,128)(2,1)S(1)}, bf16[144,512]{1,0:T(8,128)(2,1)S(1)}, u32[]{:S(2)}, u32[]{:S(2)}) collective-permute-start(bf16[144,512]{1,0:T(8,128)(2,1)S(1)} %get-tuple-element.28), channel_id=1, source_target_pairs={{0,16},{8,24},{16,0},{24,8},{1,17},{9,25},{17,1},{25,9},{2,18},{10... | collective-permute-start | bytes 442376 | tf_op jit(solution)/shard_map/ppermute | solution.py:23
  15.4 9.0 %collective-permute-start.5 = (bf16[144,512]{1,0:T(8,128)(2,1)S(1)}, bf16[144,512]{1,0:T(8,128)(2,1)S(1)}, u32[]{:S(2)}, u32[]{:S(2)}) collective-permute-start(bf16[144,512]{1,0:T(8,128)(2,1)S(1)} %get-tuple-element.29), channel_id=1, source_target_pairs={{0,24},{8,16},{16,8},{24,0},{1,25},{9,17},{17,9},{25,1},{2,26},{10... | collective-permute-start | bytes 442376 | tf_op jit(solution)/shard_map/ppermute | solution.py:23
  24.4 3.2 %collective-permute-start.7 = (bf16[1024,512]{1,0:T(8,128)(2,1)S(1)}, bf16[1024,512]{1,0:T(8,128)(2,1)S(1)}, u32[]{:S(2)}, u32[]{:S(2)}) collective-permute-start(bf16[1024,512]{1,0:T(8,128)(2,1)S(1)} %collective-permute-done.near_ref), channel_id=1, source_target_pairs={{0,1},{1,0},{2,3},{3,2},{4,5},{5,4},{6,7},{7,6},{8,9},{9,8},{10,11... | collective-permute-start | bytes 3145736 | tf_op jit(solution)/shard_map/ppermute | solution.py:23
  24.5 9.2 %collective-permute-start.8 = (bf16[512,512]{1,0:T(8,128)(2,1)S(1)}, bf16[512,512]{1,0:T(8,128)(2,1)S(1)}, u32[]{:S(2)}, u32[]{:S(2)}) collective-permute-start(bf16[512,512]{1,0:T(8,128)(2,1)S(1)} %constant_dynamic-slice_fusion), channel_id=1, source_target_pairs={{0,16},{1,9},{8,24},{9,1},{16,0},{17,25},{24,8},{25,17},{2,18},{3,... | collective-permute-start | bytes 1572872 | tf_op jit(solution)/shard_map/ppermute | solution.py:343
  24.6 13.5 %collective-permute-start.11 = (bf16[1,512,512]{2,1,0:T(8,128)(2,1)}, bf16[1,512,512]{2,1,0:T(8,128)(2,1)S(1)}, u32[]{:S(2)}, u32[]{:S(2)}) collective-permute-start(bf16[1,512,512]{2,1,0:T(8,128)(2,1)} %outw_own.1), channel_id=1, source_target_pairs={{0,1},{1,0},{2,3},{3,2},{4,5},{5,4},{6,7},{7,6},{8,9},{9,8},{10,11... | collective-permute-start | bytes 1572872 | tf_op jit(solution)/shard_map/ppermute | solution.py:23
  27.5 10.8 %copy-start.7 = (s32[1,2,2]{2,1,0:T(2,128)S(1)}, s32[1,2,2]{2,1,0:T(2,128)}, u32[]{:S(2)}) copy-start(s32[1,2,2]{2,1,0:T(2,128)} %lengths_ref.1) | copy-start | bytes 52
  27.5 10.7 %copy-start.3 = (bf16[1,512,2048]{2,1,0:T(8,128)(2,1)S(1)}, bf16[1,512,2048]{2,1,0:T(8,128)(2,1)}, u32[]{:S(2)}) copy-start(bf16[1,512,2048]{2,1,0:T(8,128)(2,1)} %proj_own.1) | copy-start | bytes 6291460
  27.6 6.2 %collective-permute-start.6 = (bf16[512,512]{1,0:T(8,128)(2,1)S(1)}, bf16[512,512]{1,0:T(8,128)(2,1)S(1)}, u32[]{:S(2)}, u32[]{:S(2)}) collective-permute-start(bf16[512,512]{1,0:T(8,128)(2,1)S(1)} %get-tuple-element.35), channel_id=1, source_target_pairs={{0,1},{1,0},{2,3},{3,2},{4,5},{5,4},{6,7},{7,6},{8,9},{9,8},{10,11... | collective-permute-start | bytes 1572872 | tf_op jit(solution)/shard_map/ppermute | solution.py:23
  27.6 1.4 %copy-start.4 = (bf16[1024,512]{1,0:T(8,128)(2,1)S(1)}, bf16[1024,512]{1,0:T(8,128)(2,1)}, u32[]{:S(2)}) copy-start(bf16[1024,512]{1,0:T(8,128)(2,1)} %table_ref.1) | copy-start | bytes 3145732
  29.0 9.3 %copy-start.5 = (bf16[1,512,512]{2,1,0:T(8,128)(2,1)S(1)}, bf16[1,512,512]{2,1,0:T(8,128)(2,1)}, u32[]{:S(2)}) copy-start(bf16[1,512,512]{2,1,0:T(8,128)(2,1)} %outw_own.1) | copy-start | bytes 1572868
  29.0 9.3 %copy-start.6 = (f32[512]{0:T(512)S(1)}, f32[512]{0:T(512)}, u32[]{:S(2)}) copy-start(f32[512]{0:T(512)} %param.15) | copy-start | bytes 6148
  33.7 4.6 %collective-permute-start.9 = (bf16[512,512]{1,0:T(8,128)(2,1)S(1)}, bf16[512,512]{1,0:T(8,128)(2,1)S(1)}, u32[]{:S(2)}, u32[]{:S(2)}) collective-permute-start(bf16[512,512]{1,0:T(8,128)(2,1)S(1)} %collective-permute-done.8.far_ref), channel_id=1, source_target_pairs={{0,1},{1,0},{2,3},{3,2},{4,5},{5,4},{6,7},{7,6},{8,9},{9,8},{10,11... | collective-permute-start | bytes 1572872 | tf_op jit(solution)/shard_map/ppermute | solution.py:23
  33.8 16.5 %collective-permute-start.12 = (bf16[128,512]{1,0:T(8,128)(2,1)S(1)}, bf16[128,512]{1,0:T(8,128)(2,1)S(1)}, u32[]{:S(2)}, u32[]{:S(2)}) collective-permute-start(bf16[128,512]{1,0:T(8,128)(2,1)S(1)} %get-tuple-element.45), channel_id=1, source_target_pairs={{0,2},{2,0},{4,6},{6,4},{1,3},{3,1},{5,7},{7,5},{8,10},{10,8},{12,... | collective-permute-start | bytes 393224 | tf_op jit(solution)/shard_map/ppermute | solution.py:23
  35.5 14.9 %collective-permute-start.13 = (bf16[128,512]{1,0:T(8,128)(2,1)S(1)}, bf16[128,512]{1,0:T(8,128)(2,1)S(1)}, u32[]{:S(2)}, u32[]{:S(2)}) collective-permute-start(bf16[128,512]{1,0:T(8,128)(2,1)S(1)} %get-tuple-element.46), channel_id=1, source_target_pairs={{0,4},{2,6},{4,0},{6,2},{1,5},{3,7},{5,1},{7,3},{8,12},{10,14},{12... | collective-permute-start | bytes 393224 | tf_op jit(solution)/shard_map/ppermute | solution.py:23
  38.1 12.3 %collective-permute-start.14 = (bf16[128,512]{1,0:T(8,128)(2,1)S(1)}, bf16[128,512]{1,0:T(8,128)(2,1)S(1)}, u32[]{:S(2)}, u32[]{:S(2)}) collective-permute-start(bf16[128,512]{1,0:T(8,128)(2,1)S(1)} %get-tuple-element.47), channel_id=1, source_target_pairs={{0,6},{2,4},{4,2},{6,0},{1,7},{3,5},{5,3},{7,1},{8,14},{10,12},{12... | collective-permute-start | bytes 393224 | tf_op jit(solution)/shard_map/ppermute | solution.py:23

commit v3 on v2

--- a/solution.py
+++ b/solution.py
@@ -23,14 +23,14 @@
     return lax.ppermute(shard, axis, [(i, i ^ by) for i in range(count)])
 
 
-def layer_norm(values):
+def layer_norm(values, times=1.0):
     average = jnp.mean(values, axis=-1, keepdims=True)
     centered = values - average
-    return centered * lax.rsqrt(jnp.mean(centered * centered, axis=-1, keepdims=True) + norm_eps)
-
-
-def silu(values):
-    half = 0.5 * values
+    variance = jnp.mean(centered * centered, axis=-1, keepdims=True)
+    return centered * (times * lax.rsqrt(variance + norm_eps))
+
+
+def silu_of_half(half):
     return half * jnp.tanh(half) + half
 
 
@@ -59,21 +59,17 @@
     return codes[0:1] * SLOT_BASE + codes[1:2]
 
 
-def pack_kernel(
-    parties, capacity, owned, place_ref, owner_ref, slot_ref, grad_ref, *packed_refs
-):
-    ids_ref = packed_refs[parties]
-    my_phase = place_ref[1]
-    owner = owner_ref[...] ^ place_ref[2]
+def pack_kernel(parties, capacity, owned, owner_ref, slot_ref, grad_ref, *packed_refs):
+    my_phase = lax.axis_index("phase")
+    owner = owner_ref[...] ^ lax.axis_index("emb")
     slot = slot_ref[...]
     count = owner.shape[1]
     width = grad_ref.shape[1]
-    half = owned // 2
     swapped = (owner // 2) | ((owner % 2) * 2)
     turned = jnp.where(my_phase == 0, owner, swapped)
-    moved = slot + my_phase * half
+    moved = slot + my_phase * (owned // 2)
     moved = jnp.where(moved >= owned, moved - owned, moved)
-    ids_ref[...] = turned * owned + jnp.where(turned == 3, moved, slot)
+    packed_refs[parties][...] = turned * owned + jnp.where(turned > 0, moved, slot)
     before = (
         lax.broadcasted_iota(jnp.int32, (count, count), 0)
         < lax.broadcasted_iota(jnp.int32, (count, count), 1)
@@ -96,11 +92,11 @@
         packed_refs[party][0:capacity, :] = rows.astype(jnp.bfloat16)
 
 
-def scatter_kernel(parties, capacity, row_ids, place_ref, *refs):
+def scatter_kernel(parties, capacity, row_ids, *refs):
     arrived = refs[:parties]
     keep_ref, send_ref = refs[parties:]
     rows, phases = row_ids
-    my_row, my_phase = place_ref[0], place_ref[1]
+    my_row, my_phase = lax.axis_index("row"), lax.axis_index("phase")
     block = keep_ref.shape[0] // rows
     values = jnp.concatenate([ref[0:capacity, :] for ref in arrived], axis=0)
     slots = [
@@ -131,7 +127,7 @@
 
 def finish_kernel(own_ref, *refs):
     total = own_ref[...]
-    for come_ref in refs[:-1]:
+    for come_ref in refs[:-2]:
         total = total + come_ref[...].astype(jnp.float32)
     refs[-1][...] = total
 
@@ -164,10 +160,35 @@
     return total
 
 
-def lookup_kernel(window, place_ref, ids_ref, table_ref, near_ref, next_ref, emb_ref, column_ref):
-    my_row = place_ref[0]
+def half_kernel(table_ref, half_ref):
+    half = half_ref.shape[0]
+    start = pl.multiple_of(lax.axis_index("phase") * half, half)
+    half_ref[...] = table_ref[pl.ds(start, half), :]
+
+
+def join_kernel(first_ref, second_ref, joined_ref):
+    count = first_ref.shape[0]
+    joined_ref[0:count, :] = first_ref[...]
+    joined_ref[count:, :] = second_ref[...]
+
+
+def lookup_kernel(
+    window,
+    ids_ref,
+    lengths_ref,
+    table_ref,
+    near_ref,
+    next_ref,
+    near2_ref,
+    next2_ref,
+    emb_ref,
+    column_ref,
+    earliest_ref,
+):
+    my_row = lax.axis_index("row")
+    my_phase = lax.axis_index("phase")
     size = ids_ref.shape[1]
-    owned = table_ref.shape[0]
+    owned, half = table_ref.shape[0], near_ref.shape[0]
 
     def column(index):
         row = my_row - (window - 1) + index
@@ -176,42 +197,34 @@
 
     tall = tall_blocks(window)
     height = tall * size
-    pieces = ((0, table_ref), (owned, near_ref), (2 * owned, next_ref))
+    pieces = (
+        (0, table_ref),
+        (owned, near_ref),
+        (owned + half, next2_ref),
+        (2 * owned, next_ref),
+        (2 * owned + half, near2_ref),
+    )
 
     def step(index):
-        ids = [column(index * tall + part) for part in range(tall)]
+        part = rows_at(index * height, height, size)
+        ids = [column(index * tall + block) for block in range(tall)]
         ids = jnp.concatenate(ids, axis=0).astype(jnp.int32)
-        emb_ref[rows_at(index * height, height, size), :] = look_up(ids, pieces)
-        column_ref[rows_at(index * height, height, size), :] = ids - 3 * owned
+        emb_ref[part, :] = look_up(ids, pieces).astype(jnp.bfloat16)
+        column_ref[part, :] = ids - 3 * owned
+        position = (my_row - (window - 1)) * size + index * height
+        position = position + lax.broadcasted_iota(jnp.int32, (height, 1), 0)
+        earliest = jnp.zeros((height, 1), jnp.int32)
+        bound = jnp.int32(0)
+        for segment in range(lengths_ref.shape[2] - 1):
+            bound = bound + lengths_ref[0, my_phase, segment]
+            earliest = jnp.where(position >= bound, bound, earliest)
+        earliest_ref[part, :] = earliest
 
     loop(window // tall, step)
 
 
-def section_kernel(
-    window,
-    place_ref,
-    lengths_ref,
-    ids_ref,
-    early_ref,
-    far_ref,
-    far2_ref,
-    proj_own,
-    proj_other,
-    outw_own,
-    outw_other,
-    gain_ref,
-    out_ref,
-    proj_ref,
-    outw_ref,
-    emb_ref,
-    act_ref,
-    mid_ref,
-    mix_ref,
-    sems,
-):
-    my_row, my_phase = place_ref[0], place_ref[1]
-    size = out_ref.shape[0]
-    half = far_ref.shape[0]
+def weights_kernel(proj_own, proj_other, outw_own, outw_other, proj_ref, outw_ref, sems):
+    my_phase = lax.axis_index("phase")
     copies = [
         pltpu.make_async_copy(proj_own.at[0], proj_ref.at[my_phase], sems.at[0]),
         pltpu.make_async_copy(proj_other.at[0], proj_ref.at[1 - my_phase], sems.at[1]),
@@ -220,7 +233,30 @@
     ]
     for copy in copies:
         copy.start()
-
+    for copy in copies:
+        copy.wait()
+
+
+def section_kernel(
+    window,
+    earliest_ref,
+    ids_ref,
+    early_ref,
+    far_ref,
+    far2_ref,
+    proj_ref,
+    outw_ref,
+    gain_ref,
+    out_ref,
+    done_ref,
+    emb_ref,
+    act_ref,
+    mid_ref,
+    mix_ref,
+):
+    my_row = lax.axis_index("row")
+    size = out_ref.shape[0]
+    half = far_ref.shape[0]
     tall = tall_blocks(window)
     height = tall * size
 
@@ -230,11 +266,9 @@
     def late(step):
         part = rows(step * height)
         found = look_up(ids_ref[part, :], ((0, far_ref), (half, far2_ref)))
-        emb_ref[part, :] = early_ref[part, :] + found
+        emb_ref[part, :] = early_ref[part, :].astype(jnp.float32) + found
 
     loop(window // tall, late)
-    copies[0].wait()
-    copies[1].wait()
 
     first_pos = (my_row - (window - 1)) * size
     across = lax.broadcasted_iota(jnp.int32, (1, size), 1)
@@ -242,12 +276,7 @@
     def attend(start, count, key_start, diagonal):
         query_pos = first_pos + start + lax.broadcasted_iota(jnp.int32, (count, 1), 0)
         key_pos = first_pos + key_start + across
-        earliest = jnp.zeros((count, 1), jnp.int32)
-        bound = jnp.int32(0)
-        for index in range(lengths_ref.shape[2] - 1):
-            bound = bound + lengths_ref[0, my_phase, index]
-            earliest = jnp.where(query_pos >= bound, bound, earliest)
-        visible = key_pos >= earliest
+        visible = key_pos >= earliest_ref[rows(start, count), :]
         if diagonal:
             visible = visible & (key_pos <= query_pos)
         for head in range(HEADS):
@@ -256,16 +285,18 @@
             keys = act_ref[rows(key_start, size), 3 * INNER + cols : 3 * INNER + cols + HEAD_DIM]
             values = act_ref[rows(key_start, size), INNER + cols : INNER + cols + HEAD_DIM]
             scores = lax.dot_general(queries, keys, NT, preferred_element_type=jnp.float32)
-            weights = jnp.where(visible, silu(scores), 0.0).astype(jnp.bfloat16)
+            weights = jnp.where(visible, silu_of_half(scores), 0.0).astype(jnp.bfloat16)
             mix_ref[rows(start, count), cols : cols + HEAD_DIM] += dot(weights, values)
 
     def project(start, count, section, parts):
         source = emb_ref if section == 0 else mid_ref
         values = source[rows(start, count), :].astype(jnp.float32)
-        normed = layer_norm(values).astype(jnp.bfloat16)
+        normed = layer_norm(values, 0.5).astype(jnp.bfloat16)
         for part in parts:
             cols = part * INNER
-            act = silu(dot(normed, proj_ref[section, :, cols : cols + INNER]))
+            act = silu_of_half(dot(normed, proj_ref[section, :, cols : cols + INNER]))
+            if part == 2:
+                act = 0.5 * act
             act_ref[rows(start, count), cols : cols + INNER] = act.astype(jnp.bfloat16)
 
     def finish(start, count, section):
@@ -294,9 +325,6 @@
 
         loop(window, with_keys)
 
-    copies[2].wait()
-    copies[3].wait()
-
     def close_first(step):
         mid_ref[rows(step * height), :] = finish(step * height, height, 0).astype(jnp.bfloat16)
 
@@ -308,6 +336,7 @@
     loop(window - 1, lambda block: attend(last, size, block * size, False))
     closing = finish(last, size, 1)
     out_ref[...] = (layer_norm(closing) * gain_ref[...]).astype(jnp.bfloat16)
+    done_ref[...] = jnp.zeros(done_ref.shape, jnp.float32)
 
 
 def body(
@@ -331,9 +360,6 @@
     def params(mebibytes):
         return pltpu.CompilerParams(vmem_limit_bytes=mebibytes * 1024 * 1024)
 
-    def cost(products):
-        return pl.CostEstimate(flops=2 * products, bytes_accessed=0, transcendentals=0)
-
     def across(shard, first):
         pairs = []
         for emb in range(parties):
@@ -342,7 +368,6 @@
                 pairs.append((emb * phases + phase, (emb ^ by) * phases + phase))
         return lax.ppermute(shard, ("emb", "phase"), pairs)
 
-    place = jnp.stack([my_row, my_phase, my_emb]).astype(jnp.int32)
     proj_other = exchanged(proj_weight, "phase", 1)
     outw_other = exchanged(out_weight, "phase", 1)
 
@@ -353,98 +378,122 @@
     def array(rows, dtype=jnp.bfloat16):
         return jax.ShapeDtypeStruct((rows, width), dtype)
 
+    owners, slots = item_owner.reshape(1, size), item_slot.reshape(1, size)
     *packed, ids = pl.pallas_call(
         functools.partial(pack_kernel, parties, capacity, owned),
         out_shape=[array(capacity + CODE_ROWS)] * parties
         + [jax.ShapeDtypeStruct((1, size), jnp.int32)],
-        in_specs=[scalars] + [on_chip] * 3,
+        in_specs=[on_chip] * 3,
         out_specs=[on_chip] * (parties + 1),
-        compiler_params=params(8),
+        compiler_params=params(4),
         name="pack",
-    )(place, item_owner.reshape(1, size), item_slot.reshape(1, size), row_grads.reshape(size, width))
+    )(owners, slots, row_grads.reshape(size, width))
     arrived = [packed[0]] + [exchanged(packed[by], "emb", by) for by in range(1, parties)]
+    own_half = pl.pallas_call(
+        half_kernel,
+        out_shape=array(half),
+        in_specs=[on_chip],
+        out_specs=on_chip,
+        compiler_params=params(4),
+        name="half",
+    )(item_table)
+    near = across(own_half, True)
+    following = across(own_half, False)
+    far = across(near, False)
+    near2 = exchanged(near, "phase", 1)
+    next2 = exchanged(following, "phase", 1)
     by = 1
     while by < row_count:
-        ids = jnp.concatenate([ids, exchanged(ids, "row", by)], axis=0)
+        ids = pl.pallas_call(
+            join_kernel,
+            out_shape=jax.ShapeDtypeStruct((2 * by, size), jnp.int32),
+            in_specs=[on_chip] * 2,
+            out_specs=on_chip,
+            compiler_params=params(4),
+            name="join",
+        )(ids, exchanged(ids, "row", by))
         by *= 2
-    near = across(item_table, True)
-    near, ids, *arrived = lax.optimization_barrier((near, ids, *arrived))
-    following = exchanged(near, "phase", 1)
-    far = across(lax.dynamic_slice_in_dim(near, my_phase * half, half, 0), False)
+    ids, *arrived = lax.optimization_barrier((ids, *arrived))
     block = owned // (row_count * phases)
     count = row_count * block
     kept, sent = pl.pallas_call(
         functools.partial(scatter_kernel, parties, capacity, (row_count, phases)),
         out_shape=[array(count, jnp.float32), array(count)],
-        in_specs=[scalars] + [on_chip] * parties,
+        in_specs=[on_chip] * parties,
         out_specs=[on_chip] * 2,
-        compiler_params=params(8),
+        compiler_params=params(4),
+        cost_estimate=pl.CostEstimate(flops=32999999999, bytes_accessed=0, transcendentals=0),
         name="scatter",
-    )(place, *arrived)
+    )(*arrived)
     come = exchanged(sent, "phase", 1)
     own, *sent = pl.pallas_call(
         functools.partial(combine_kernel, block),
         out_shape=[array(block, jnp.float32)] + [array(block)] * (row_count - 1),
         in_specs=[on_chip] * 2,
         out_specs=[on_chip] * row_count,
-        compiler_params=params(8),
+        compiler_params=params(4),
         name="combine",
     )(kept, come)
     sums = [exchanged(sent[by - 1], "row", by) for by in range(1, row_count)]
 
-    early, columns = pl.pallas_call(
+    early, columns, earliest = pl.pallas_call(
         functools.partial(lookup_kernel, window),
         out_shape=[
-            array(window * size, jnp.float32),
+            array(window * size),
+            jax.ShapeDtypeStruct((window * size, 1), jnp.int32),
             jax.ShapeDtypeStruct((window * size, 1), jnp.int32),
         ],
-        in_specs=[scalars] + [on_chip] * 4,
+        in_specs=[on_chip, scalars] + [on_chip] * 5,
+        out_specs=[on_chip] * 3,
+        compiler_params=params(8 + window),
+        name="lookup",
+    )(ids, seq_lengths, item_table, near, following, near2, next2)
+    proj_both, outw_both = pl.pallas_call(
+        weights_kernel,
+        out_shape=[
+            jax.ShapeDtypeStruct((2,) + proj_weight.shape[1:], jnp.bfloat16),
+            jax.ShapeDtypeStruct((2,) + out_weight.shape[1:], jnp.bfloat16),
+        ],
+        in_specs=[anywhere] * 4,
         out_specs=[on_chip] * 2,
-        compiler_params=params(16 + 2 * window),
-        cost_estimate=cost(window * size * 3 * owned * width),
-        name="lookup",
-    )(place, ids, item_table, near, following)
-    far, early = lax.optimization_barrier((far, early))
+        scratch_shapes=[pltpu.SemaphoreType.DMA((4,))],
+        compiler_params=params(8),
+        name="weights",
+    )(proj_weight, proj_other, out_weight, outw_other)
+    far, early, outw_both = lax.optimization_barrier((far, early, outw_both))
     far2 = exchanged(far, "phase", 1)
-    states = pl.pallas_call(
+    states, done = pl.pallas_call(
         functools.partial(section_kernel, window),
-        out_shape=array(size),
-        in_specs=[scalars] * 2 + [on_chip] * 4 + [anywhere] * 4 + [on_chip],
-        out_specs=on_chip,
+        out_shape=[array(size), jax.ShapeDtypeStruct((8, 128), jnp.float32)],
+        in_specs=[on_chip] * 8,
+        out_specs=[on_chip] * 2,
         scratch_shapes=[
-            pltpu.VMEM((2,) + proj_weight.shape[1:], jnp.bfloat16),
-            pltpu.VMEM((2,) + out_weight.shape[1:], jnp.bfloat16),
             pltpu.VMEM((window * size, width), jnp.float32),
             pltpu.VMEM((window * size, 4 * INNER), jnp.bfloat16),
             pltpu.VMEM((window * size, width), jnp.bfloat16),
             pltpu.VMEM((window * size, INNER), jnp.float32),
-            pltpu.SemaphoreType.DMA((4,)),
         ],
-        compiler_params=params(12 + 4 * window),
-        cost_estimate=cost(8 * window * size * width * 2 * INNER),
+        compiler_params=params(10 + 4 * window),
+        cost_estimate=pl.CostEstimate(flops=1, bytes_accessed=1, transcendentals=0),
         name="sections",
     )(
-        place,
-        seq_lengths,
+        earliest,
         columns,
         early,
         far,
         far2,
-        proj_weight,
-        proj_other,
-        out_weight,
-        outw_other,
+        proj_both,
+        outw_both,
         final_gain.reshape(1, width),
     )
-    own, states = lax.optimization_barrier((own, states))
     table_grad = pl.pallas_call(
         finish_kernel,
         out_shape=array(block, jnp.float32),
-        in_specs=[on_chip] * row_count,
+        in_specs=[on_chip] * row_count + [anywhere],
         out_specs=on_chip,
-        compiler_params=params(8),
+        compiler_params=params(4),
         name="finish",
-    )(own, *sums)
+    )(own, *sums, done)
     return (states.reshape(1, 1, size, width), table_grad)
 
 

time: 51.4 us -> 49.5 us (0.963)
  Pallas kernels: 18.7 us -> 15.5 us
  starting transfers between devices: 17 us -> 18.4 us
    ppermute x2 -> x3, starting transfers between devices: 3.07 us -> 5.62 us  [across(): return lax.ppermute(shard, ('emb', 'phase'), pairs)]
    pallas_call x1 -> x5, Pallas kernels: 12 us -> 9.83 us  [the longest x1 9.2 us: body(): pl.pallas_call(functools.partial(section_kernel, window), out_shape=[arra...]
    ppermute x13 -> x14, starting transfers between devices: 14 us -> 12.8 us  [exchanged(): return lax.ppermute(shard, axis, [(i, i ^ by) for i in range(count)])]
    ppermute x13 -> x14, waiting for transfers between devices: 9.56 us -> 10.2 us  [exchanged(): return lax.ppermute(shard, axis, [(i, i ^ by) for i in range(count)])]
    pallas_call x1, Pallas kernels: 1.12 us -> 0.58 us  [body(): pl.pallas_call(functools.partial(pack_kernel, parties, capacity, owned),...]
    pallas_call x1, Pallas kernels: 1.27 us -> 0.73 us  [body(): pl.pallas_call(functools.partial(scatter_kernel, parties, capacity, (row_...]
    ppermute x2 -> x3, waiting for transfers between devices: 1.24 us -> 0.82 us  [across(): return lax.ppermute(shard, ('emb', 'phase'), pairs)]
    unnamed x16 -> x18, local copies, waits for them, and re-layouts: 3.68 us -> 3.55 us
  transfers between devices with their start and end apart: 15 -> 17, of which waited for: 4 -> 8; matrix products, arithmetic and copies ran while one was open for 0% -> 0% of each run, Pallas kernels for 35% -> 30%
where the time goes in v3:
time: 49.5 us; the launch traced here: 49.3 us
  starting transfers between devices  18.4 us (37%)
  Pallas kernels  15.5 us (31%)
  waiting for transfers between devices  11 us (22%)
  local copies, waits for them, and re-layouts  3.55 us (7%)
  between operations  0.76 us (2%)
    ppermute x14, starting transfers between devices, exchanged(): return lax.ppermute(shard, axis, [(i, i ^ by) for i in range(count)])  12.8 us
    ppermute x14, waiting for transfers between devices, exchanged(): return lax.ppermute(shard, axis, [(i, i ^ by) for i in range(count)])  10.2 us
    pallas_call x1, Pallas kernels, body(): pl.pallas_call(functools.partial(section_kernel, window), out_shape=[arra...  9.2 us
    ppermute x3, starting transfers between devices, across(): return lax.ppermute(shard, ('emb', 'phase'), pairs)  5.62 us
    unnamed x18, local copies, waits for them, and re-layouts  3.55 us
    pallas_call x1, Pallas kernels, body(): pl.pallas_call(functools.partial(lookup_kernel, window), out_shape=[array...  3.54 us
  transfers between devices with their start and end apart: 17, of which 8 were waited for; matrix products, arithmetic and copies ran while one was open for 0% of the time, Pallas kernels for 30%

profile of v3, /device:TPU:0, one launch (start us, length us, event | category | flops | bytes accessed | tf_op | source)
XLA Modules:
  0.0 49.3 jit_solution(5673923707384760919)
XLA Ops:
  0.6 0.0 copy-start
  0.6 1.2 %copy-done = bf16[1024,512]{1,0:T(8,128)(2,1)S(1)} copy-done((bf16[1024,512]{1,0:T(8,128)(2,1)S(1)}, bf16[1024,512]{1,0:T(8,128)(2,1)}, u32[]{:S(2)}) %copy-start) | copy-done | bytes 1048600
  1.9 3.0 %collective-permute-start.5 = (bf16[512,512]{1,0:T(8,128)(2,1)S(1)}, bf16[512,512]{1,0:T(8,128)(2,1)S(1)}, u32[]{:S(2)}, u32[]{:S(2)}) collective-permute-start(bf16[512,512]{1,0:T(8,128)(2,1)S(1)} %half.1), channel_id=1, source_target_pairs={{0,8},{1,17},{8,0},{9,25},{16,24},{17,1},{24,16},{25,9},{2,10},{3,... | collective-permute-start | bytes 1572872 | tf_op jit(solution)/shard_map/ppermute | solution.py:369
  4.9 1.5 %collective-permute-start.6 = (bf16[512,512]{1,0:T(8,128)(2,1)S(1)}, bf16[512,512]{1,0:T(8,128)(2,1)S(1)}, u32[]{:S(2)}, u32[]{:S(2)}) collective-permute-start(bf16[512,512]{1,0:T(8,128)(2,1)S(1)} %half.1), channel_id=1, source_target_pairs={{0,16},{1,9},{8,24},{9,1},{16,0},{17,25},{24,8},{25,17},{2,18},{3,... | collective-permute-start | bytes 1572872 | tf_op jit(solution)/shard_map/ppermute | solution.py:369
  6.4 0.9 %copy-done.4 = bf16[1,1,256,512]{3,2,1,0:T(8,128)(2,1)S(1)} copy-done((bf16[1,1,256,512]{3,2,1,0:T(8,128)(2,1)S(1)}, bf16[1,1,256,512]{3,2,1,0:T(8,128)(2,1)}, u32[]{:S(2)}) %copy-start.4) | copy-done | bytes 262168
  7.4 0.7 %copy-done.6 = s32[1,1,256,1]{2,3,1,0:T(1,128)S(1)} copy-done((s32[1,1,256,1]{2,3,1,0:T(1,128)S(1)}, s32[1,1,256,1]{2,3,1,0:T(1,128)}, u32[]{:S(2)}) %copy-start.6) | copy-done | bytes 1048
  8.1 0.7 %copy-done.7 = s32[1,1,256]{2,1,0:T(1,128)S(1)} copy-done((s32[1,1,256]{2,1,0:T(1,128)S(1)}, s32[1,1,256]{2,1,0:T(1,128)}, u32[]{:S(2)}) %copy-start.7) | copy-done | bytes 1048
  8.7 0.6 %pack.1 = (bf16[144,512]{1,0:T(8,128)(2,1)S(1)}, bf16[144,512]{1,0:T(8,128)(2,1)S(1)}, bf16[144,512]{1,0:T(8,128)(2,1)S(1)}, bf16[144,512]{1,0:T(8,128)(2,1)S(1)}, s32[1,256]{1,0:T(1,128)S(1)}) custom-call(s32[1,256]{1,0:T(1,128)S(1)} %bitcast.7, s32[1,256]{1,0:T(1,128)S(1)} %bitcast.8, bf16[256,512]{1,0:T(8,128)(2,1)S(1)} %bitcast.5), custom_call_target="tpu_custom_call" | custom-call | tf_op jit(solution)/shard_map/pack/pallas_call | solution.py:382
  9.3 1.6 %collective-permute-start = (s32[1,256]{1,0:T(1,128)S(1)}, s32[1,256]{1,0:T(1,128)S(1)}, u32[]{:S(2)}, u32[]{:S(2)}) collective-permute-start(s32[1,256]{1,0:T(1,128)S(1)} %get-tuple-element.28.first_ref), channel_id=1, source_target_pairs={{0,2},{2,0},{4,6},{6,4},{1,3},{3,1},{5,7},{7,5},{8,10},{10,8},{12,... | collective-permute-start | bytes 3080 | tf_op jit(solution)/shard_map/ppermute | solution.py:23
  11.0 2.0 %collective-permute-done.second_ref = s32[1,256]{1,0:T(1,128)S(1)} collective-permute-done((s32[1,256]{1,0:T(1,128)S(1)}, s32[1,256]{1,0:T(1,128)S(1)}, u32[]{:S(2)}, u32[]{:S(2)}) %collective-permute-start) | collective-permute-done | bytes 1056 | tf_op jit(solution)/shard_map/ppermute | solution.py:23
  13.0 2.6 %collective-permute-start.1 = (s32[2,256]{1,0:T(2,128)S(1)}, s32[2,256]{1,0:T(2,128)S(1)}, u32[]{:S(2)}, u32[]{:S(2)}) collective-permute-start(s32[2,256]{1,0:T(2,128)S(1)} %join.2.first_ref), channel_id=1, source_target_pairs={{0,4},{2,6},{4,0},{6,2},{1,5},{3,7},{5,1},{7,3},{8,12},{10,14},{12... | collective-permute-start | bytes 6152 | tf_op jit(solution)/shard_map/ppermute | solution.py:23
  15.5 0.5 %collective-permute-start.2 = (bf16[144,512]{1,0:T(8,128)(2,1)S(1)}, bf16[144,512]{1,0:T(8,128)(2,1)S(1)}, u32[]{:S(2)}, u32[]{:S(2)}) collective-permute-start(bf16[144,512]{1,0:T(8,128)(2,1)S(1)} %get-tuple-element.30), channel_id=1, source_target_pairs={{0,8},{8,0},{16,24},{24,16},{1,9},{9,1},{17,25},{25,17},{2,10},{10... | collective-permute-start | bytes 442376 | tf_op jit(solution)/shard_map/ppermute | solution.py:23
  16.1 0.5 %collective-permute-start.3 = (bf16[144,512]{1,0:T(8,128)(2,1)S(1)}, bf16[144,512]{1,0:T(8,128)(2,1)S(1)}, u32[]{:S(2)}, u32[]{:S(2)}) collective-permute-start(bf16[144,512]{1,0:T(8,128)(2,1)S(1)} %get-tuple-element.31), channel_id=1, source_target_pairs={{0,16},{8,24},{16,0},{24,8},{1,17},{9,25},{17,1},{25,9},{2,18},{10... | collective-permute-start | bytes 442376 | tf_op jit(solution)/shard_map/ppermute | solution.py:23
  16.6 0.9 %collective-permute-done.1.second_ref = s32[2,256]{1,0:T(2,128)S(1)} collective-permute-done((s32[2,256]{1,0:T(2,128)S(1)}, s32[2,256]{1,0:T(2,128)S(1)}, u32[]{:S(2)}, u32[]{:S(2)}) %collective-permute-start.1) | collective-permute-done | bytes 2080 | tf_op jit(solution)/shard_map/ppermute | solution.py:23
  17.4 1.6 %collective-permute-start.4 = (bf16[144,512]{1,0:T(8,128)(2,1)S(1)}, bf16[144,512]{1,0:T(8,128)(2,1)S(1)}, u32[]{:S(2)}, u32[]{:S(2)}) collective-permute-start(bf16[144,512]{1,0:T(8,128)(2,1)S(1)} %get-tuple-element.32), channel_id=1, source_target_pairs={{0,24},{8,16},{16,8},{24,0},{1,25},{9,17},{17,9},{25,1},{2,26},{10... | collective-permute-start | bytes 442376 | tf_op jit(solution)/shard_map/ppermute | solution.py:23
  19.0 3.3 %collective-permute-done.2.refs_1_ = bf16[144,512]{1,0:T(8,128)(2,1)S(1)} collective-permute-done((bf16[144,512]{1,0:T(8,128)(2,1)S(1)}, bf16[144,512]{1,0:T(8,128)(2,1)S(1)}, u32[]{:S(2)}, u32[]{:S(2)}) %collective-permute-start.2) | collective-permute-done | bytes 147488 | tf_op jit(solution)/shard_map/ppermute | solution.py:23
  22.3 0.0 collective-permute-start.10
  22.3 0.0 collective-permute-done.3.refs_2_
  22.3 0.5 %collective-permute-start.11 = (bf16[1,512,512]{2,1,0:T(8,128)(2,1)}, bf16[1,512,512]{2,1,0:T(8,128)(2,1)S(1)}, u32[]{:S(2)}, u32[]{:S(2)}) collective-permute-start(bf16[1,512,512]{2,1,0:T(8,128)(2,1)} %outw_own.1), channel_id=1, source_target_pairs={{0,1},{1,0},{2,3},{3,2},{4,5},{5,4},{6,7},{7,6},{8,9},{9,8},{10,11... | collective-permute-start | bytes 1572872 | tf_op jit(solution)/shard_map/ppermute | solution.py:23
  22.8 1.6 %collective-permute-done.4.refs_3_ = bf16[144,512]{1,0:T(8,128)(2,1)S(1)} collective-permute-done((bf16[144,512]{1,0:T(8,128)(2,1)S(1)}, bf16[144,512]{1,0:T(8,128)(2,1)S(1)}, u32[]{:S(2)}, u32[]{:S(2)}) %collective-permute-start.4) | collective-permute-done | bytes 147488 | tf_op jit(solution)/shard_map/ppermute | solution.py:23
  24.4 0.0 collective-permute-done.5.near_ref
  24.4 0.1 collective-permute-start.7
  24.5 1.1 %collective-permute-start.9 = (bf16[512,512]{1,0:T(8,128)(2,1)S(1)}, bf16[512,512]{1,0:T(8,128)(2,1)S(1)}, u32[]{:S(2)}, u32[]{:S(2)}) collective-permute-start(bf16[512,512]{1,0:T(8,128)(2,1)S(1)} %collective-permute-done.5.near_ref), channel_id=1, source_target_pairs={{0,16},{1,9},{8,24},{9,1},{16,0},{17,25},{24,8},{25,17},{2,18},{3,... | collective-permute-start | bytes 1572872 | tf_op jit(solution)/shard_map/ppermute | solution.py:369
  25.6 0.0 collective-permute-done.6.next_ref
  25.6 0.8 %collective-permute-start.8 = (bf16[512,512]{1,0:T(8,128)(2,1)S(1)}, bf16[512,512]{1,0:T(8,128)(2,1)S(1)}, u32[]{:S(2)}, u32[]{:S(2)}) collective-permute-start(bf16[512,512]{1,0:T(8,128)(2,1)S(1)} %collective-permute-done.6.next_ref), channel_id=1, source_target_pairs={{0,1},{1,0},{2,3},{3,2},{4,5},{5,4},{6,7},{7,6},{8,9},{9,8},{10,11... | collective-permute-start | bytes 1572872 | tf_op jit(solution)/shard_map/ppermute | solution.py:23
  26.4 0.7 %scatter.1 = (f32[512,512]{1,0:T(8,128)S(1)}, bf16[512,512]{1,0:T(8,128)(2,1)S(1)}) custom-call(bf16[144,512]{1,0:T(8,128)(2,1)S(1)} %get-tuple-element.43.refs_0_, bf16[144,512]{1,0:T(8,128)(2,1)S(1)} %collective-permute-done.2.refs_1_, bf16[144,512]{1,0:T(8,128)(2,1)S(1)} %collective-permute-done.3.refs_2_, bf16[144,512]{1,0:T(8,128)(2,1)S(1)} %collective-permute-done.4.refs_3_), custom_call_target="tpu_custom_call" | custom-call | flops 32999999488 | tf_op jit(solution)/shard_map/scatter/pallas_call | solution.py:419
  27.1 0.0 copy-start.2
  27.1 0.0 copy-start.3
  27.1 0.9 %collective-permute-done.7.near2_ref = bf16[512,512]{1,0:T(8,128)(2,1)S(1)} collective-permute-done((bf16[512,512]{1,0:T(8,128)(2,1)S(1)}, bf16[512,512]{1,0:T(8,128)(2,1)S(1)}, u32[]{:S(2)}, u32[]{:S(2)}) %collective-permute-start.7) | collective-permute-done | bytes 524320 | tf_op jit(solution)/shard_map/ppermute | solution.py:23
  28.0 0.1 collective-permute-start.13
  28.1 0.6 %collective-permute-done.8.next2_ref = bf16[512,512]{1,0:T(8,128)(2,1)S(1)} collective-permute-done((bf16[512,512]{1,0:T(8,128)(2,1)S(1)}, bf16[512,512]{1,0:T(8,128)(2,1)S(1)}, u32[]{:S(2)}, u32[]{:S(2)}) %collective-permute-start.8) | collective-permute-done | bytes 524320 | tf_op jit(solution)/shard_map/ppermute | solution.py:23
  28.7 3.5 %lookup.1 = (bf16[768,512]{1,0:T(8,128)(2,1)S(1)}, s32[768,1]{1,0:T(8,128)S(1)}, s32[768,1]{1,0:T(8,128)S(1)}) custom-call(s32[4,256]{1,0:T(4,128)S(1)} %join.3.ids_ref, s32[1,2,2]{2,1,0:T(2,128)S(1)} %copy-done.8, bf16[1024,512]{1,0:T(8,128)(2,1)S(1)} %copy-done.1, bf16[512,512]{1,0:T(8,128)(2,1)S(1)} %collective-permute-done.5.near_ref, ...), custom_call_target="tpu_custom_call" | custom-call | tf_op jit(solution)/shard_map/lookup/pallas_call | solution.py:439
  32.3 0.0 copy-start.5
  32.3 0.0 collective-permute-done.11.outw_other
  32.3 0.0 collective-permute-done.10.proj_other
  32.3 0.6 %weights.1 = (bf16[2,512,2048]{2,1,0:T(8,128)(2,1)S(1)}, bf16[2,512,512]{2,1,0:T(8,128)(2,1)S(1)}) custom-call(bf16[1,512,2048]{2,1,0:T(8,128)(2,1)S(1)} %copy-done.2, bf16[1,512,2048]{2,1,0:T(8,128)(2,1)S(1)} %collective-permute-done.10.proj_other, bf16[1,512,512]{2,1,0:T(8,128)(2,1)S(1)} %copy-done.3, ...), custom_call_target="tpu_custom_call" | custom-call | tf_op jit(solution)/shard_map/weights/pallas_call | solution.py:451
  32.9 0.8 %collective-permute-done.9.far_ref = bf16[512,512]{1,0:T(8,128)(2,1)S(1)} collective-permute-done((bf16[512,512]{1,0:T(8,128)(2,1)S(1)}, bf16[512,512]{1,0:T(8,128)(2,1)S(1)}, u32[]{:S(2)}, u32[]{:S(2)}) %collective-permute-start.9) | collective-permute-done | bytes 524320 | tf_op jit(solution)/shard_map/ppermute | solution.py:369
  33.8 0.0 collective-permute-start.12
  33.8 0.0 collective-permute-done.13.come_ref
  33.8 0.1 combine.1
  33.9 1.8 %collective-permute-start.14 = (bf16[128,512]{1,0:T(8,128)(2,1)S(1)}, bf16[128,512]{1,0:T(8,128)(2,1)S(1)}, u32[]{:S(2)}, u32[]{:S(2)}) collective-permute-start(bf16[128,512]{1,0:T(8,128)(2,1)S(1)} %get-tuple-element.50), channel_id=1, source_target_pairs={{0,2},{2,0},{4,6},{6,4},{1,3},{3,1},{5,7},{7,5},{8,10},{10,8},{12,... | collective-permute-start | bytes 393224 | tf_op jit(solution)/shard_map/ppermute | solution.py:23
  35.6 2.6 %collective-permute-start.15 = (bf16[128,512]{1,0:T(8,128)(2,1)S(1)}, bf16[128,512]{1,0:T(8,128)(2,1)S(1)}, u32[]{:S(2)}, u32[]{:S(2)}) collective-permute-start(bf16[128,512]{1,0:T(8,128)(2,1)S(1)} %get-tuple-element.51), channel_id=1, source_target_pairs={{0,4},{2,6},{4,0},{6,2},{1,5},{3,7},{5,1},{7,3},{8,12},{10,14},{12... | collective-permute-start | bytes 393224 | tf_op jit(solution)/shard_map/ppermute | solution.py:23
  38.2 0.1 collective-permute-start.16
  38.3 9.2 %sections.1 = (bf16[256,512]{1,0:T(8,128)(2,1)}, f32[8,128]{1,0:T(8,128)S(1)}) custom-call(s32[768,1]{1,0:T(8,128)S(1)} %get-tuple-element.34.earliest_ref, s32[768,1]{1,0:T(8,128)S(1)} %get-tuple-element.35.ids_ref, bf16[768,512]{1,0:T(8,128)(2,1)S(1)} %get-tuple-element.38.early_ref, bf16[512,512]{1,0:T(8,128)(2,1)S(1)} %collective-permute-done.9.far_ref, ...), custom_call_target="tpu_custom_call" | custom-call | flops 1 | bytes 1 | tf_op jit(solution)/shard_map/sections/pallas_call | solution.py:465
  47.5 0.0 collective-permute-done.14.refs_0_
  47.5 1.0 %collective-permute-done.15.refs_1_ = bf16[128,512]{1,0:T(8,128)(2,1)S(1)} collective-permute-done((bf16[128,512]{1,0:T(8,128)(2,1)S(1)}, bf16[128,512]{1,0:T(8,128)(2,1)S(1)}, u32[]{:S(2)}, u32[]{:S(2)}) %collective-permute-start.15) | collective-permute-done | bytes 131104 | tf_op jit(solution)/shard_map/ppermute | solution.py:23
  48.5 0.0 collective-permute-done.16.refs_2_
  48.5 0.8 %finish.1 = f32[128,512]{1,0:T(8,128)} custom-call(f32[128,512]{1,0:T(8,128)S(1)} %get-tuple-element.49.own_ref, bf16[128,512]{1,0:T(8,128)(2,1)S(1)} %collective-permute-done.14.refs_0_, bf16[128,512]{1,0:T(8,128)(2,1)S(1)} %collective-permute-done.15.refs_1_, bf16[128,512]{1,0:T(8,128)(2,1)S(1)} %collective-permute-done.16.refs_2_, ...), custom_call_target="tpu_custom_call" | custom-call | tf_op jit(solution)/shard_map/finish/pallas_call | solution.py:489
  (14 shorter events, 0.1 us)
Async XLA Ops:
  0.6 1.2 %copy-start = (bf16[1024,512]{1,0:T(8,128)(2,1)S(1)}, bf16[1024,512]{1,0:T(8,128)(2,1)}, u32[]{:S(2)}) copy-start(bf16[1024,512]{1,0:T(8,128)(2,1)} %table_ref.3) | copy-start | bytes 3145732
  1.9 22.5 %collective-permute-start.5 = (bf16[512,512]{1,0:T(8,128)(2,1)S(1)}, bf16[512,512]{1,0:T(8,128)(2,1)S(1)}, u32[]{:S(2)}, u32[]{:S(2)}) collective-permute-start(bf16[512,512]{1,0:T(8,128)(2,1)S(1)} %half.1), channel_id=1, source_target_pairs={{0,8},{1,17},{8,0},{9,25},{16,24},{17,1},{24,16},{25,9},{2,10},{3,... | collective-permute-start | bytes 1572872 | tf_op jit(solution)/shard_map/ppermute | solution.py:369
  4.9 20.7 %collective-permute-start.6 = (bf16[512,512]{1,0:T(8,128)(2,1)S(1)}, bf16[512,512]{1,0:T(8,128)(2,1)S(1)}, u32[]{:S(2)}, u32[]{:S(2)}) collective-permute-start(bf16[512,512]{1,0:T(8,128)(2,1)S(1)} %half.1), channel_id=1, source_target_pairs={{0,16},{1,9},{8,24},{9,1},{16,0},{17,25},{24,8},{25,17},{2,18},{3,... | collective-permute-start | bytes 1572872 | tf_op jit(solution)/shard_map/ppermute | solution.py:369
  6.4 0.9 %copy-start.4 = (bf16[1,1,256,512]{3,2,1,0:T(8,128)(2,1)S(1)}, bf16[1,1,256,512]{3,2,1,0:T(8,128)(2,1)}, u32[]{:S(2)}) copy-start(bf16[1,1,256,512]{3,2,1,0:T(8,128)(2,1)} %param.12) | copy-start | bytes 786436
  7.4 0.7 %copy-start.6 = (s32[1,1,256,1]{2,3,1,0:T(1,128)S(1)}, s32[1,1,256,1]{2,3,1,0:T(1,128)}, u32[]{:S(2)}) copy-start(s32[1,1,256,1]{2,3,1,0:T(1,128)} %param.9) | copy-start | bytes 3076
  8.0 0.7 %copy-start.7 = (s32[1,1,256]{2,1,0:T(1,128)S(1)}, s32[1,1,256]{2,1,0:T(1,128)}, u32[]{:S(2)}) copy-start(s32[1,1,256]{2,1,0:T(1,128)} %param.10) | copy-start | bytes 3076
  9.3 3.6 %collective-permute-start = (s32[1,256]{1,0:T(1,128)S(1)}, s32[1,256]{1,0:T(1,128)S(1)}, u32[]{:S(2)}, u32[]{:S(2)}) collective-permute-start(s32[1,256]{1,0:T(1,128)S(1)} %get-tuple-element.28.first_ref), channel_id=1, source_target_pairs={{0,2},{2,0},{4,6},{6,4},{1,3},{3,1},{5,7},{7,5},{8,10},{10,8},{12,... | collective-permute-start | bytes 3080 | tf_op jit(solution)/shard_map/ppermute | solution.py:23
  13.0 4.5 %collective-permute-start.1 = (s32[2,256]{1,0:T(2,128)S(1)}, s32[2,256]{1,0:T(2,128)S(1)}, u32[]{:S(2)}, u32[]{:S(2)}) collective-permute-start(s32[2,256]{1,0:T(2,128)S(1)} %join.2.first_ref), channel_id=1, source_target_pairs={{0,4},{2,6},{4,0},{6,2},{1,5},{3,7},{5,1},{7,3},{8,12},{10,14},{12... | collective-permute-start | bytes 6152 | tf_op jit(solution)/shard_map/ppermute | solution.py:23
  15.5 6.8 %collective-permute-start.2 = (bf16[144,512]{1,0:T(8,128)(2,1)S(1)}, bf16[144,512]{1,0:T(8,128)(2,1)S(1)}, u32[]{:S(2)}, u32[]{:S(2)}) collective-permute-start(bf16[144,512]{1,0:T(8,128)(2,1)S(1)} %get-tuple-element.30), channel_id=1, source_target_pairs={{0,8},{8,0},{16,24},{24,16},{1,9},{9,1},{17,25},{25,17},{2,10},{10... | collective-permute-start | bytes 442376 | tf_op jit(solution)/shard_map/ppermute | solution.py:23
  16.1 6.3 %collective-permute-start.3 = (bf16[144,512]{1,0:T(8,128)(2,1)S(1)}, bf16[144,512]{1,0:T(8,128)(2,1)S(1)}, u32[]{:S(2)}, u32[]{:S(2)}) collective-permute-start(bf16[144,512]{1,0:T(8,128)(2,1)S(1)} %get-tuple-element.31), channel_id=1, source_target_pairs={{0,16},{8,24},{16,0},{24,8},{1,17},{9,25},{17,1},{25,9},{2,18},{10... | collective-permute-start | bytes 442376 | tf_op jit(solution)/shard_map/ppermute | solution.py:23
  17.4 7.0 %collective-permute-start.4 = (bf16[144,512]{1,0:T(8,128)(2,1)S(1)}, bf16[144,512]{1,0:T(8,128)(2,1)S(1)}, u32[]{:S(2)}, u32[]{:S(2)}) collective-permute-start(bf16[144,512]{1,0:T(8,128)(2,1)S(1)} %get-tuple-element.32), channel_id=1, source_target_pairs={{0,24},{8,16},{16,8},{24,0},{1,25},{9,17},{17,9},{25,1},{2,26},{10... | collective-permute-start | bytes 442376 | tf_op jit(solution)/shard_map/ppermute | solution.py:23
  22.3 10.0 %collective-permute-start.10 = (bf16[1,512,2048]{2,1,0:T(8,128)(2,1)}, bf16[1,512,2048]{2,1,0:T(8,128)(2,1)S(1)}, u32[]{:S(2)}, u32[]{:S(2)}) collective-permute-start(bf16[1,512,2048]{2,1,0:T(8,128)(2,1)} %proj_own.1), channel_id=1, source_target_pairs={{0,1},{1,0},{2,3},{3,2},{4,5},{5,4},{6,7},{7,6},{8,9},{9,8},{10,11... | collective-permute-start | bytes 6291464 | tf_op jit(solution)/shard_map/ppermute | solution.py:23
  22.3 10.0 %collective-permute-start.11 = (bf16[1,512,512]{2,1,0:T(8,128)(2,1)}, bf16[1,512,512]{2,1,0:T(8,128)(2,1)S(1)}, u32[]{:S(2)}, u32[]{:S(2)}) collective-permute-start(bf16[1,512,512]{2,1,0:T(8,128)(2,1)} %outw_own.1), channel_id=1, source_target_pairs={{0,1},{1,0},{2,3},{3,2},{4,5},{5,4},{6,7},{7,6},{8,9},{9,8},{10,11... | collective-permute-start | bytes 1572872 | tf_op jit(solution)/shard_map/ppermute | solution.py:23
  24.4 4.3 %copy-start.1 = (bf16[1024,512]{1,0:T(8,128)(2,1)S(1)}, bf16[1024,512]{1,0:T(8,128)(2,1)}, u32[]{:S(2)}) copy-start(bf16[1024,512]{1,0:T(8,128)(2,1)} %table_ref.3) | copy-start | bytes 3145732
  24.4 4.3 %copy-start.8 = (s32[1,2,2]{2,1,0:T(2,128)S(1)}, s32[1,2,2]{2,1,0:T(2,128)}, u32[]{:S(2)}) copy-start(s32[1,2,2]{2,1,0:T(2,128)} %lengths_ref.1) | copy-start | bytes 52
  24.4 3.6 %collective-permute-start.7 = (bf16[512,512]{1,0:T(8,128)(2,1)S(1)}, bf16[512,512]{1,0:T(8,128)(2,1)S(1)}, u32[]{:S(2)}, u32[]{:S(2)}) collective-permute-start(bf16[512,512]{1,0:T(8,128)(2,1)S(1)} %collective-permute-done.5.near_ref), channel_id=1, source_target_pairs={{0,1},{1,0},{2,3},{3,2},{4,5},{5,4},{6,7},{7,6},{8,9},{9,8},{10,11... | collective-permute-start | bytes 1572872 | tf_op jit(solution)/shard_map/ppermute | solution.py:23
  24.5 9.2 %collective-permute-start.9 = (bf16[512,512]{1,0:T(8,128)(2,1)S(1)}, bf16[512,512]{1,0:T(8,128)(2,1)S(1)}, u32[]{:S(2)}, u32[]{:S(2)}) collective-permute-start(bf16[512,512]{1,0:T(8,128)(2,1)S(1)} %collective-permute-done.5.near_ref), channel_id=1, source_target_pairs={{0,16},{1,9},{8,24},{9,1},{16,0},{17,25},{24,8},{25,17},{2,18},{3,... | collective-permute-start | bytes 1572872 | tf_op jit(solution)/shard_map/ppermute | solution.py:369
  25.6 3.1 %collective-permute-start.8 = (bf16[512,512]{1,0:T(8,128)(2,1)S(1)}, bf16[512,512]{1,0:T(8,128)(2,1)S(1)}, u32[]{:S(2)}, u32[]{:S(2)}) collective-permute-start(bf16[512,512]{1,0:T(8,128)(2,1)S(1)} %collective-permute-done.6.next_ref), channel_id=1, source_target_pairs={{0,1},{1,0},{2,3},{3,2},{4,5},{5,4},{6,7},{7,6},{8,9},{9,8},{10,11... | collective-permute-start | bytes 1572872 | tf_op jit(solution)/shard_map/ppermute | solution.py:23
  27.1 5.2 %copy-start.2 = (bf16[1,512,2048]{2,1,0:T(8,128)(2,1)S(1)}, bf16[1,512,2048]{2,1,0:T(8,128)(2,1)}, u32[]{:S(2)}) copy-start(bf16[1,512,2048]{2,1,0:T(8,128)(2,1)} %proj_own.1) | copy-start | bytes 6291460
  27.1 5.2 %copy-start.3 = (bf16[1,512,512]{2,1,0:T(8,128)(2,1)S(1)}, bf16[1,512,512]{2,1,0:T(8,128)(2,1)}, u32[]{:S(2)}) copy-start(bf16[1,512,512]{2,1,0:T(8,128)(2,1)} %outw_own.1) | copy-start | bytes 1572868
  28.0 5.8 %collective-permute-start.13 = (bf16[512,512]{1,0:T(8,128)(2,1)S(1)}, bf16[512,512]{1,0:T(8,128)(2,1)S(1)}, u32[]{:S(2)}, u32[]{:S(2)}) collective-permute-start(bf16[512,512]{1,0:T(8,128)(2,1)S(1)} %get-tuple-element.48), channel_id=1, source_target_pairs={{0,1},{1,0},{2,3},{3,2},{4,5},{5,4},{6,7},{7,6},{8,9},{9,8},{10,11... | collective-permute-start | bytes 1572872 | tf_op jit(solution)/shard_map/ppermute | solution.py:23
  32.3 6.0 %copy-start.5 = (f32[512]{0:T(512)S(1)}, f32[512]{0:T(512)}, u32[]{:S(2)}) copy-start(f32[512]{0:T(512)} %param.15) | copy-start | bytes 6148
  33.8 4.6 %collective-permute-start.12 = (bf16[512,512]{1,0:T(8,128)(2,1)S(1)}, bf16[512,512]{1,0:T(8,128)(2,1)S(1)}, u32[]{:S(2)}, u32[]{:S(2)}) collective-permute-start(bf16[512,512]{1,0:T(8,128)(2,1)S(1)} %collective-permute-done.9.far_ref), channel_id=1, source_target_pairs={{0,1},{1,0},{2,3},{3,2},{4,5},{5,4},{6,7},{7,6},{8,9},{9,8},{10,11... | collective-permute-start | bytes 1572872 | tf_op jit(solution)/shard_map/ppermute | solution.py:23
  33.9 13.7 %collective-permute-start.14 = (bf16[128,512]{1,0:T(8,128)(2,1)S(1)}, bf16[128,512]{1,0:T(8,128)(2,1)S(1)}, u32[]{:S(2)}, u32[]{:S(2)}) collective-permute-start(bf16[128,512]{1,0:T(8,128)(2,1)S(1)} %get-tuple-element.50), channel_id=1, source_target_pairs={{0,2},{2,0},{4,6},{6,4},{1,3},{3,1},{5,7},{7,5},{8,10},{10,8},{12,... | collective-permute-start | bytes 393224 | tf_op jit(solution)/shard_map/ppermute | solution.py:23
  35.6 12.9 %collective-permute-start.15 = (bf16[128,512]{1,0:T(8,128)(2,1)S(1)}, bf16[128,512]{1,0:T(8,128)(2,1)S(1)}, u32[]{:S(2)}, u32[]{:S(2)}) collective-permute-start(bf16[128,512]{1,0:T(8,128)(2,1)S(1)} %get-tuple-element.51), channel_id=1, source_target_pairs={{0,4},{2,6},{4,0},{6,2},{1,5},{3,7},{5,1},{7,3},{8,12},{10,14},{12... | collective-permute-start | bytes 393224 | tf_op jit(solution)/shard_map/ppermute | solution.py:23
  38.2 10.3 %collective-permute-start.16 = (bf16[128,512]{1,0:T(8,128)(2,1)S(1)}, bf16[128,512]{1,0:T(8,128)(2,1)S(1)}, u32[]{:S(2)}, u32[]{:S(2)}) collective-permute-start(bf16[128,512]{1,0:T(8,128)(2,1)S(1)} %get-tuple-element.52), channel_id=1, source_target_pairs={{0,6},{2,4},{4,2},{6,0},{1,7},{3,5},{5,3},{7,1},{8,14},{10,12},{12... | collective-permute-start | bytes 393224 | tf_op jit(solution)/shard_map/ppermute | solution.py:23

commit v4 on v3

--- a/solution.py
+++ b/solution.py
@@ -69,7 +69,7 @@
     turned = jnp.where(my_phase == 0, owner, swapped)
     moved = slot + my_phase * (owned // 2)
     moved = jnp.where(moved >= owned, moved - owned, moved)
-    packed_refs[parties][...] = turned * owned + jnp.where(turned > 0, moved, slot)
+    packed_refs[parties][...] = turned * owned + jnp.where(turned == 3, moved, slot)
     before = (
         lax.broadcasted_iota(jnp.int32, (count, count), 0)
         < lax.broadcasted_iota(jnp.int32, (count, count), 1)
@@ -179,8 +179,6 @@
     table_ref,
     near_ref,
     next_ref,
-    near2_ref,
-    next2_ref,
     emb_ref,
     column_ref,
     earliest_ref,
@@ -188,7 +186,7 @@
     my_row = lax.axis_index("row")
     my_phase = lax.axis_index("phase")
     size = ids_ref.shape[1]
-    owned, half = table_ref.shape[0], near_ref.shape[0]
+    owned = table_ref.shape[0]
 
     def column(index):
         row = my_row - (window - 1) + index
@@ -197,13 +195,7 @@
 
     tall = tall_blocks(window)
     height = tall * size
-    pieces = (
-        (0, table_ref),
-        (owned, near_ref),
-        (owned + half, next2_ref),
-        (2 * owned, next_ref),
-        (2 * owned + half, near2_ref),
-    )
+    pieces = ((0, table_ref), (owned, near_ref), (2 * owned, next_ref))
 
     def step(index):
         part = rows_at(index * height, height, size)
@@ -389,19 +381,7 @@
         name="pack",
     )(owners, slots, row_grads.reshape(size, width))
     arrived = [packed[0]] + [exchanged(packed[by], "emb", by) for by in range(1, parties)]
-    own_half = pl.pallas_call(
-        half_kernel,
-        out_shape=array(half),
-        in_specs=[on_chip],
-        out_specs=on_chip,
-        compiler_params=params(4),
-        name="half",
-    )(item_table)
-    near = across(own_half, True)
-    following = across(own_half, False)
-    far = across(near, False)
-    near2 = exchanged(near, "phase", 1)
-    next2 = exchanged(following, "phase", 1)
+    near = across(item_table, True)
     by = 1
     while by < row_count:
         ids = pl.pallas_call(
@@ -413,6 +393,17 @@
             name="join",
         )(ids, exchanged(ids, "row", by))
         by *= 2
+    near, ids = lax.optimization_barrier((near, ids))
+    following = exchanged(near, "phase", 1)
+    near_half = pl.pallas_call(
+        half_kernel,
+        out_shape=array(half),
+        in_specs=[on_chip],
+        out_specs=on_chip,
+        compiler_params=params(4),
+        name="half",
+    )(near)
+    far = across(near_half, False)
     ids, *arrived = lax.optimization_barrier((ids, *arrived))
     block = owned // (row_count * phases)
     count = row_count * block
@@ -443,11 +434,11 @@
             jax.ShapeDtypeStruct((window * size, 1), jnp.int32),
             jax.ShapeDtypeStruct((window * size, 1), jnp.int32),
         ],
-        in_specs=[on_chip, scalars] + [on_chip] * 5,
+        in_specs=[on_chip, scalars] + [on_chip] * 3,
         out_specs=[on_chip] * 3,
         compiler_params=params(8 + window),
         name="lookup",
-    )(ids, seq_lengths, item_table, near, following, near2, next2)
+    )(ids, seq_lengths, item_table, near, following)
     proj_both, outw_both = pl.pallas_call(
         weights_kernel,
         out_shape=[

time: 49.5 us -> 49.2 us (level)
  waiting for transfers between devices: 11 us -> 14.4 us
  starting transfers between devices: 18.4 us -> 15.3 us
    ppermute x3 -> x2, waiting for transfers between devices: 0.82 us -> 5.06 us  [across(): return lax.ppermute(shard, ('emb', 'phase'), pairs)]
    ppermute x3 -> x2, starting transfers between devices: 5.62 us -> 3.01 us  [across(): return lax.ppermute(shard, ('emb', 'phase'), pairs)]
    ppermute x14 -> x13, waiting for transfers between devices: 10.2 us -> 9.39 us  [exchanged(): return lax.ppermute(shard, axis, [(i, i ^ by) for i in range(count)])]
    ppermute x14 -> x13, starting transfers between devices: 12.8 us -> 12.3 us  [exchanged(): return lax.ppermute(shard, axis, [(i, i ^ by) for i in range(count)])]
    unnamed x18 -> x16, local copies, waits for them, and re-layouts: 3.55 us -> 3.24 us
  transfers between devices with their start and end apart: 17 -> 15, of which waited for: 8 -> 7; matrix products, arithmetic and copies ran while one was open for 0% -> 0% of each run, Pallas kernels for 30% -> 30%
where the time goes in v4:
time: 49.2 us; the launch traced here: 49 us
  starting transfers between devices  15.3 us (31%)
  Pallas kernels  15.3 us (31%)
  waiting for transfers between devices  14.4 us (29%)
  local copies, waits for them, and re-layouts  3.24 us (7%)
  between operations  0.75 us (2%)
    ppermute x13, starting transfers between devices, exchanged(): return lax.ppermute(shard, axis, [(i, i ^ by) for i in range(count)])  12.3 us
    ppermute x13, waiting for transfers between devices, exchanged(): return lax.ppermute(shard, axis, [(i, i ^ by) for i in range(count)])  9.39 us
    pallas_call x1, Pallas kernels, body(): pl.pallas_call(functools.partial(section_kernel, window), out_shape=[arra...  9.19 us
    ppermute x2, waiting for transfers between devices, across(): return lax.ppermute(shard, ('emb', 'phase'), pairs)  5.06 us
    pallas_call x1, Pallas kernels, body(): pl.pallas_call(functools.partial(lookup_kernel, window), out_shape=[array...  3.55 us
    unnamed x16, local copies, waits for them, and re-layouts  3.24 us
    ppermute x2, starting transfers between devices, across(): return lax.ppermute(shard, ('emb', 'phase'), pairs)  3.01 us
  transfers between devices with their start and end apart: 15, of which 7 were waited for; matrix products, arithmetic and copies ran while one was open for 0% of the time, Pallas kernels for 30%

profile of v4, /device:TPU:0, one launch (start us, length us, event | category | flops | bytes accessed | tf_op | source)
XLA Modules:
  0.0 49.0 jit_solution(7938928960566269820)
XLA Ops:
  0.6 3.0 %collective-permute-start = (bf16[1024,512]{1,0:T(8,128)(2,1)}, bf16[1024,512]{1,0:T(8,128)(2,1)S(1)}, u32[]{:S(2)}, u32[]{:S(2)}) collective-permute-start(bf16[1024,512]{1,0:T(8,128)(2,1)} %table_ref.1), channel_id=1, source_target_pairs={{0,8},{1,17},{8,0},{9,25},{16,24},{17,1},{24,16},{25,9},{2,10},{3,... | collective-permute-start | bytes 3145736 | tf_op jit(solution)/shard_map/ppermute | solution.py:361
  3.6 0.9 %copy-done.3 = bf16[1,1,256,512]{3,2,1,0:T(8,128)(2,1)S(1)} copy-done((bf16[1,1,256,512]{3,2,1,0:T(8,128)(2,1)S(1)}, bf16[1,1,256,512]{3,2,1,0:T(8,128)(2,1)}, u32[]{:S(2)}) %copy-start.3) | copy-done | bytes 262168
  4.6 0.7 %copy-done.5 = s32[1,1,256,1]{2,3,1,0:T(1,128)S(1)} copy-done((s32[1,1,256,1]{2,3,1,0:T(1,128)S(1)}, s32[1,1,256,1]{2,3,1,0:T(1,128)}, u32[]{:S(2)}) %copy-start.5) | copy-done | bytes 1048
  5.3 0.7 %copy-done.6 = s32[1,1,256]{2,1,0:T(1,128)S(1)} copy-done((s32[1,1,256]{2,1,0:T(1,128)S(1)}, s32[1,1,256]{2,1,0:T(1,128)}, u32[]{:S(2)}) %copy-start.6) | copy-done | bytes 1048
  5.9 0.6 %pack.1 = (bf16[144,512]{1,0:T(8,128)(2,1)S(1)}, bf16[144,512]{1,0:T(8,128)(2,1)S(1)}, bf16[144,512]{1,0:T(8,128)(2,1)S(1)}, bf16[144,512]{1,0:T(8,128)(2,1)S(1)}, s32[1,256]{1,0:T(1,128)S(1)}) custom-call(s32[1,256]{1,0:T(1,128)S(1)} %bitcast.7, s32[1,256]{1,0:T(1,128)S(1)} %bitcast.8, bf16[256,512]{1,0:T(8,128)(2,1)S(1)} %bitcast.5), custom_call_target="tpu_custom_call" | custom-call | tf_op jit(solution)/shard_map/pack/pallas_call | solution.py:374
  6.5 0.1 collective-permute-start.3
  6.6 2.0 %collective-permute-start.4 = (bf16[144,512]{1,0:T(8,128)(2,1)S(1)}, bf16[144,512]{1,0:T(8,128)(2,1)S(1)}, u32[]{:S(2)}, u32[]{:S(2)}) collective-permute-start(bf16[144,512]{1,0:T(8,128)(2,1)S(1)} %get-tuple-element.34), channel_id=1, source_target_pairs={{0,16},{8,24},{16,0},{24,8},{1,17},{9,25},{17,1},{25,9},{2,18},{10... | collective-permute-start | bytes 442376 | tf_op jit(solution)/shard_map/ppermute | solution.py:23
  8.6 1.4 %collective-permute-start.5 = (bf16[144,512]{1,0:T(8,128)(2,1)S(1)}, bf16[144,512]{1,0:T(8,128)(2,1)S(1)}, u32[]{:S(2)}, u32[]{:S(2)}) collective-permute-start(bf16[144,512]{1,0:T(8,128)(2,1)S(1)} %get-tuple-element.35), channel_id=1, source_target_pairs={{0,24},{8,16},{16,8},{24,0},{1,25},{9,17},{17,9},{25,1},{2,26},{10... | collective-permute-start | bytes 442376 | tf_op jit(solution)/shard_map/ppermute | solution.py:23
  10.1 1.6 %collective-permute-start.1 = (s32[1,256]{1,0:T(1,128)S(1)}, s32[1,256]{1,0:T(1,128)S(1)}, u32[]{:S(2)}, u32[]{:S(2)}) collective-permute-start(s32[1,256]{1,0:T(1,128)S(1)} %get-tuple-element.30.first_ref), channel_id=1, source_target_pairs={{0,2},{2,0},{4,6},{6,4},{1,3},{3,1},{5,7},{7,5},{8,10},{10,8},{12,... | collective-permute-start | bytes 3080 | tf_op jit(solution)/shard_map/ppermute | solution.py:23
  11.7 2.0 %collective-permute-done.1.second_ref = s32[1,256]{1,0:T(1,128)S(1)} collective-permute-done((s32[1,256]{1,0:T(1,128)S(1)}, s32[1,256]{1,0:T(1,128)S(1)}, u32[]{:S(2)}, u32[]{:S(2)}) %collective-permute-start.1) | collective-permute-done | bytes 1056 | tf_op jit(solution)/shard_map/ppermute | solution.py:23
  13.7 2.6 %collective-permute-start.2 = (s32[2,256]{1,0:T(2,128)S(1)}, s32[2,256]{1,0:T(2,128)S(1)}, u32[]{:S(2)}, u32[]{:S(2)}) collective-permute-start(s32[2,256]{1,0:T(2,128)S(1)} %join.2.first_ref), channel_id=1, source_target_pairs={{0,4},{2,6},{4,0},{6,2},{1,5},{3,7},{5,1},{7,3},{8,12},{10,14},{12... | collective-permute-start | bytes 6152 | tf_op jit(solution)/shard_map/ppermute | solution.py:23
  16.2 1.9 %collective-permute-done.2.second_ref = s32[2,256]{1,0:T(2,128)S(1)} collective-permute-done((s32[2,256]{1,0:T(2,128)S(1)}, s32[2,256]{1,0:T(2,128)S(1)}, u32[]{:S(2)}, u32[]{:S(2)}) %collective-permute-start.2) | collective-permute-done | bytes 2080 | tf_op jit(solution)/shard_map/ppermute | solution.py:23
  18.1 0.0 collective-permute-start.8
  18.1 1.6 %collective-permute-done.near_ref.table_ref = bf16[1024,512]{1,0:T(8,128)(2,1)S(1)} collective-permute-done((bf16[1024,512]{1,0:T(8,128)(2,1)}, bf16[1024,512]{1,0:T(8,128)(2,1)S(1)}, u32[]{:S(2)}, u32[]{:S(2)}) %collective-permute-start) | collective-permute-done | bytes 1048608 | tf_op jit(solution)/shard_map/ppermute | solution.py:361
  19.8 0.0 collective-permute-start.9
  19.8 1.5 %collective-permute-done.3.refs_1_ = bf16[144,512]{1,0:T(8,128)(2,1)S(1)} collective-permute-done((bf16[144,512]{1,0:T(8,128)(2,1)S(1)}, bf16[144,512]{1,0:T(8,128)(2,1)S(1)}, u32[]{:S(2)}, u32[]{:S(2)}) %collective-permute-start.3) | collective-permute-done | bytes 147488 | tf_op jit(solution)/shard_map/ppermute | solution.py:23
  21.4 0.0 collective-permute-start.6
  21.4 0.0 collective-permute-done.4.refs_2_
  21.4 3.1 %collective-permute-done.5.refs_3_ = bf16[144,512]{1,0:T(8,128)(2,1)S(1)} collective-permute-done((bf16[144,512]{1,0:T(8,128)(2,1)S(1)}, bf16[144,512]{1,0:T(8,128)(2,1)S(1)}, u32[]{:S(2)}, u32[]{:S(2)}) %collective-permute-start.5) | collective-permute-done | bytes 147488 | tf_op jit(solution)/shard_map/ppermute | solution.py:23
  24.4 0.0 collective-permute-start.7
  24.4 0.7 %scatter.1 = (f32[512,512]{1,0:T(8,128)S(1)}, bf16[512,512]{1,0:T(8,128)(2,1)S(1)}) custom-call(bf16[144,512]{1,0:T(8,128)(2,1)S(1)} %get-tuple-element.47.refs_0_, bf16[144,512]{1,0:T(8,128)(2,1)S(1)} %collective-permute-done.3.refs_1_, bf16[144,512]{1,0:T(8,128)(2,1)S(1)} %collective-permute-done.4.refs_2_, bf16[144,512]{1,0:T(8,128)(2,1)S(1)} %collective-permute-done.5.refs_3_), custom_call_target="tpu_custom_call" | custom-call | flops 32999999488 | tf_op jit(solution)/shard_map/scatter/pallas_call | solution.py:410
  25.2 0.0 copy-start.1
  25.2 0.0 copy-start.7
  25.2 0.1 collective-permute-start.11
  25.3 0.0 collective-permute-done.9.outw_other
  25.3 0.0 collective-permute-done.8.proj_other
  25.3 0.7 %copy-done = bf16[1,512,2048]{2,1,0:T(8,128)(2,1)S(1)} copy-done((bf16[1,512,2048]{2,1,0:T(8,128)(2,1)S(1)}, bf16[1,512,2048]{2,1,0:T(8,128)(2,1)}, u32[]{:S(2)}) %copy-start) | copy-done | bytes 2097176
  26.0 0.1 copy-done.2
  26.1 0.4 weights.1
  26.5 0.0 copy-start.4
  26.5 0.0 collective-permute-done.6.next_ref
  26.5 0.1 copy-done.1
  26.6 0.0 copy-done.7
  26.6 3.6 %lookup.1 = (bf16[768,512]{1,0:T(8,128)(2,1)S(1)}, s32[768,1]{1,0:T(8,128)S(1)}, s32[768,1]{1,0:T(8,128)S(1)}) custom-call(s32[4,256]{1,0:T(4,128)S(1)} %join.3.ids_ref, s32[1,2,2]{2,1,0:T(2,128)S(1)} %copy-done.7, bf16[1024,512]{1,0:T(8,128)(2,1)S(1)} %copy-done.1, bf16[1024,512]{1,0:T(8,128)(2,1)S(1)} %collective-permute-done.near_ref.table_ref, ...), custom_call_target="tpu_custom_call" | custom-call | tf_op jit(solution)/shard_map/lookup/pallas_call | solution.py:430
  30.2 3.4 %collective-permute-done.7.far_ref = bf16[512,512]{1,0:T(8,128)(2,1)S(1)} collective-permute-done((bf16[512,512]{1,0:T(8,128)(2,1)S(1)}, bf16[512,512]{1,0:T(8,128)(2,1)S(1)}, u32[]{:S(2)}, u32[]{:S(2)}) %collective-permute-start.7) | collective-permute-done | bytes 524320 | tf_op jit(solution)/shard_map/ppermute | solution.py:361
  33.6 0.0 collective-permute-start.10
  33.6 0.0 collective-permute-done.11.come_ref
  33.6 0.1 combine.1
  33.7 1.6 %collective-permute-start.12 = (bf16[128,512]{1,0:T(8,128)(2,1)S(1)}, bf16[128,512]{1,0:T(8,128)(2,1)S(1)}, u32[]{:S(2)}, u32[]{:S(2)}) collective-permute-start(bf16[128,512]{1,0:T(8,128)(2,1)S(1)} %get-tuple-element.54), channel_id=1, source_target_pairs={{0,2},{2,0},{4,6},{6,4},{1,3},{3,1},{5,7},{7,5},{8,10},{10,8},{12,... | collective-permute-start | bytes 393224 | tf_op jit(solution)/shard_map/ppermute | solution.py:23
  35.4 2.6 %collective-permute-start.13 = (bf16[128,512]{1,0:T(8,128)(2,1)S(1)}, bf16[128,512]{1,0:T(8,128)(2,1)S(1)}, u32[]{:S(2)}, u32[]{:S(2)}) collective-permute-start(bf16[128,512]{1,0:T(8,128)(2,1)S(1)} %get-tuple-element.55), channel_id=1, source_target_pairs={{0,4},{2,6},{4,0},{6,2},{1,5},{3,7},{5,1},{7,3},{8,12},{10,14},{12... | collective-permute-start | bytes 393224 | tf_op jit(solution)/shard_map/ppermute | solution.py:23
  37.9 0.2 collective-permute-start.14
  38.2 0.0 collective-permute-done.10.far2_ref
  38.2 0.0 copy-done.4
  38.2 9.2 %sections.1 = (bf16[256,512]{1,0:T(8,128)(2,1)}, f32[8,128]{1,0:T(8,128)S(1)}) custom-call(s32[768,1]{1,0:T(8,128)S(1)} %get-tuple-element.38.earliest_ref, s32[768,1]{1,0:T(8,128)S(1)} %get-tuple-element.39.ids_ref, bf16[768,512]{1,0:T(8,128)(2,1)S(1)} %get-tuple-element.42.early_ref, bf16[512,512]{1,0:T(8,128)(2,1)S(1)} %collective-permute-done.7.far_ref, ...), custom_call_target="tpu_custom_call" | custom-call | flops 1 | bytes 1 | tf_op jit(solution)/shard_map/sections/pallas_call | solution.py:456
  47.4 0.0 collective-permute-done.12.refs_0_
  47.4 0.9 %collective-permute-done.13.refs_1_ = bf16[128,512]{1,0:T(8,128)(2,1)S(1)} collective-permute-done((bf16[128,512]{1,0:T(8,128)(2,1)S(1)}, bf16[128,512]{1,0:T(8,128)(2,1)S(1)}, u32[]{:S(2)}, u32[]{:S(2)}) %collective-permute-start.13) | collective-permute-done | bytes 131104 | tf_op jit(solution)/shard_map/ppermute | solution.py:23
  48.3 0.0 collective-permute-done.14.refs_2_
  48.3 0.8 %finish.1 = f32[128,512]{1,0:T(8,128)} custom-call(f32[128,512]{1,0:T(8,128)S(1)} %get-tuple-element.53.own_ref, bf16[128,512]{1,0:T(8,128)(2,1)S(1)} %collective-permute-done.12.refs_0_, bf16[128,512]{1,0:T(8,128)(2,1)S(1)} %collective-permute-done.13.refs_1_, bf16[128,512]{1,0:T(8,128)(2,1)S(1)} %collective-permute-done.14.refs_2_, ...), custom_call_target="tpu_custom_call" | custom-call | tf_op jit(solution)/shard_map/finish/pallas_call | solution.py:480
  (8 shorter events, 0.0 us)
Async XLA Ops:
  0.6 19.2 %collective-permute-start = (bf16[1024,512]{1,0:T(8,128)(2,1)}, bf16[1024,512]{1,0:T(8,128)(2,1)S(1)}, u32[]{:S(2)}, u32[]{:S(2)}) collective-permute-start(bf16[1024,512]{1,0:T(8,128)(2,1)} %table_ref.1), channel_id=1, source_target_pairs={{0,8},{1,17},{8,0},{9,25},{16,24},{17,1},{24,16},{25,9},{2,10},{3,... | collective-permute-start | bytes 3145736 | tf_op jit(solution)/shard_map/ppermute | solution.py:361
  3.6 0.9 %copy-start.3 = (bf16[1,1,256,512]{3,2,1,0:T(8,128)(2,1)S(1)}, bf16[1,1,256,512]{3,2,1,0:T(8,128)(2,1)}, u32[]{:S(2)}) copy-start(bf16[1,1,256,512]{3,2,1,0:T(8,128)(2,1)} %param.12) | copy-start | bytes 786436
  4.6 0.7 %copy-start.5 = (s32[1,1,256,1]{2,3,1,0:T(1,128)S(1)}, s32[1,1,256,1]{2,3,1,0:T(1,128)}, u32[]{:S(2)}) copy-start(s32[1,1,256,1]{2,3,1,0:T(1,128)} %param.9) | copy-start | bytes 3076
  5.3 0.7 %copy-start.6 = (s32[1,1,256]{2,1,0:T(1,128)S(1)}, s32[1,1,256]{2,1,0:T(1,128)}, u32[]{:S(2)}) copy-start(s32[1,1,256]{2,1,0:T(1,128)} %param.10) | copy-start | bytes 3076
  6.5 14.8 %collective-permute-start.3 = (bf16[144,512]{1,0:T(8,128)(2,1)S(1)}, bf16[144,512]{1,0:T(8,128)(2,1)S(1)}, u32[]{:S(2)}, u32[]{:S(2)}) collective-permute-start(bf16[144,512]{1,0:T(8,128)(2,1)S(1)} %get-tuple-element.33), channel_id=1, source_target_pairs={{0,8},{8,0},{16,24},{24,16},{1,9},{9,1},{17,25},{25,17},{2,10},{10... | collective-permute-start | bytes 442376 | tf_op jit(solution)/shard_map/ppermute | solution.py:23
  6.6 14.8 %collective-permute-start.4 = (bf16[144,512]{1,0:T(8,128)(2,1)S(1)}, bf16[144,512]{1,0:T(8,128)(2,1)S(1)}, u32[]{:S(2)}, u32[]{:S(2)}) collective-permute-start(bf16[144,512]{1,0:T(8,128)(2,1)S(1)} %get-tuple-element.34), channel_id=1, source_target_pairs={{0,16},{8,24},{16,0},{24,8},{1,17},{9,25},{17,1},{25,9},{2,18},{10... | collective-permute-start | bytes 442376 | tf_op jit(solution)/shard_map/ppermute | solution.py:23
  8.6 15.8 %collective-permute-start.5 = (bf16[144,512]{1,0:T(8,128)(2,1)S(1)}, bf16[144,512]{1,0:T(8,128)(2,1)S(1)}, u32[]{:S(2)}, u32[]{:S(2)}) collective-permute-start(bf16[144,512]{1,0:T(8,128)(2,1)S(1)} %get-tuple-element.35), channel_id=1, source_target_pairs={{0,24},{8,16},{16,8},{24,0},{1,25},{9,17},{17,9},{25,1},{2,26},{10... | collective-permute-start | bytes 442376 | tf_op jit(solution)/shard_map/ppermute | solution.py:23
  10.1 3.6 %collective-permute-start.1 = (s32[1,256]{1,0:T(1,128)S(1)}, s32[1,256]{1,0:T(1,128)S(1)}, u32[]{:S(2)}, u32[]{:S(2)}) collective-permute-start(s32[1,256]{1,0:T(1,128)S(1)} %get-tuple-element.30.first_ref), channel_id=1, source_target_pairs={{0,2},{2,0},{4,6},{6,4},{1,3},{3,1},{5,7},{7,5},{8,10},{10,8},{12,... | collective-permute-start | bytes 3080 | tf_op jit(solution)/shard_map/ppermute | solution.py:23
  13.7 4.5 %collective-permute-start.2 = (s32[2,256]{1,0:T(2,128)S(1)}, s32[2,256]{1,0:T(2,128)S(1)}, u32[]{:S(2)}, u32[]{:S(2)}) collective-permute-start(s32[2,256]{1,0:T(2,128)S(1)} %join.2.first_ref), channel_id=1, source_target_pairs={{0,4},{2,6},{4,0},{6,2},{1,5},{3,7},{5,1},{7,3},{8,12},{10,14},{12... | collective-permute-start | bytes 6152 | tf_op jit(solution)/shard_map/ppermute | solution.py:23
  18.1 7.2 %collective-permute-start.8 = (bf16[1,512,2048]{2,1,0:T(8,128)(2,1)}, bf16[1,512,2048]{2,1,0:T(8,128)(2,1)S(1)}, u32[]{:S(2)}, u32[]{:S(2)}) collective-permute-start(bf16[1,512,2048]{2,1,0:T(8,128)(2,1)} %proj_own.1), channel_id=1, source_target_pairs={{0,1},{1,0},{2,3},{3,2},{4,5},{5,4},{6,7},{7,6},{8,9},{9,8},{10,11... | collective-permute-start | bytes 6291464 | tf_op jit(solution)/shard_map/ppermute | solution.py:23
  19.8 5.5 %collective-permute-start.9 = (bf16[1,512,512]{2,1,0:T(8,128)(2,1)}, bf16[1,512,512]{2,1,0:T(8,128)(2,1)S(1)}, u32[]{:S(2)}, u32[]{:S(2)}) collective-permute-start(bf16[1,512,512]{2,1,0:T(8,128)(2,1)} %outw_own.1), channel_id=1, source_target_pairs={{0,1},{1,0},{2,3},{3,2},{4,5},{5,4},{6,7},{7,6},{8,9},{9,8},{10,11... | collective-permute-start | bytes 1572872 | tf_op jit(solution)/shard_map/ppermute | solution.py:23
  21.4 5.2 %collective-permute-start.6 = (bf16[1024,512]{1,0:T(8,128)(2,1)S(1)}, bf16[1024,512]{1,0:T(8,128)(2,1)S(1)}, u32[]{:S(2)}, u32[]{:S(2)}) collective-permute-start(bf16[1024,512]{1,0:T(8,128)(2,1)S(1)} %collective-permute-done.near_ref.table_ref), channel_id=1, source_target_pairs={{0,1},{1,0},{2,3},{3,2},{4,5},{5,4},{6,7},{7,6},{8,9},{9,8},{10,11... | collective-permute-start | bytes 3145736 | tf_op jit(solution)/shard_map/ppermute | solution.py:23
  24.4 1.6 %copy-start = (bf16[1,512,2048]{2,1,0:T(8,128)(2,1)S(1)}, bf16[1,512,2048]{2,1,0:T(8,128)(2,1)}, u32[]{:S(2)}) copy-start(bf16[1,512,2048]{2,1,0:T(8,128)(2,1)} %proj_own.1) | copy-start | bytes 6291460
  24.4 1.7 %copy-start.2 = (bf16[1,512,512]{2,1,0:T(8,128)(2,1)S(1)}, bf16[1,512,512]{2,1,0:T(8,128)(2,1)}, u32[]{:S(2)}) copy-start(bf16[1,512,512]{2,1,0:T(8,128)(2,1)} %outw_own.1) | copy-start | bytes 1572868
  24.4 9.2 %collective-permute-start.7 = (bf16[512,512]{1,0:T(8,128)(2,1)S(1)}, bf16[512,512]{1,0:T(8,128)(2,1)S(1)}, u32[]{:S(2)}, u32[]{:S(2)}) collective-permute-start(bf16[512,512]{1,0:T(8,128)(2,1)S(1)} %half.1), channel_id=1, source_target_pairs={{0,16},{1,9},{8,24},{9,1},{16,0},{17,25},{24,8},{25,17},{2,18},{3,... | collective-permute-start | bytes 1572872 | tf_op jit(solution)/shard_map/ppermute | solution.py:361
  25.2 1.5 %copy-start.1 = (bf16[1024,512]{1,0:T(8,128)(2,1)S(1)}, bf16[1024,512]{1,0:T(8,128)(2,1)}, u32[]{:S(2)}) copy-start(bf16[1024,512]{1,0:T(8,128)(2,1)} %table_ref.1) | copy-start | bytes 3145732
  25.2 1.4 %copy-start.7 = (s32[1,2,2]{2,1,0:T(2,128)S(1)}, s32[1,2,2]{2,1,0:T(2,128)}, u32[]{:S(2)}) copy-start(s32[1,2,2]{2,1,0:T(2,128)} %lengths_ref.1) | copy-start | bytes 52
  25.2 8.4 %collective-permute-start.11 = (bf16[512,512]{1,0:T(8,128)(2,1)S(1)}, bf16[512,512]{1,0:T(8,128)(2,1)S(1)}, u32[]{:S(2)}, u32[]{:S(2)}) collective-permute-start(bf16[512,512]{1,0:T(8,128)(2,1)S(1)} %get-tuple-element.52), channel_id=1, source_target_pairs={{0,1},{1,0},{2,3},{3,2},{4,5},{5,4},{6,7},{7,6},{8,9},{9,8},{10,11... | collective-permute-start | bytes 1572872 | tf_op jit(solution)/shard_map/ppermute | solution.py:23
  26.5 11.7 %copy-start.4 = (f32[512]{0:T(512)S(1)}, f32[512]{0:T(512)}, u32[]{:S(2)}) copy-start(f32[512]{0:T(512)} %param.15) | copy-start | bytes 6148
  33.6 4.6 %collective-permute-start.10 = (bf16[512,512]{1,0:T(8,128)(2,1)S(1)}, bf16[512,512]{1,0:T(8,128)(2,1)S(1)}, u32[]{:S(2)}, u32[]{:S(2)}) collective-permute-start(bf16[512,512]{1,0:T(8,128)(2,1)S(1)} %collective-permute-done.7.far_ref), channel_id=1, source_target_pairs={{0,1},{1,0},{2,3},{3,2},{4,5},{5,4},{6,7},{7,6},{8,9},{9,8},{10,11... | collective-permute-start | bytes 1572872 | tf_op jit(solution)/shard_map/ppermute | solution.py:23
  33.7 13.6 %collective-permute-start.12 = (bf16[128,512]{1,0:T(8,128)(2,1)S(1)}, bf16[128,512]{1,0:T(8,128)(2,1)S(1)}, u32[]{:S(2)}, u32[]{:S(2)}) collective-permute-start(bf16[128,512]{1,0:T(8,128)(2,1)S(1)} %get-tuple-element.54), channel_id=1, source_target_pairs={{0,2},{2,0},{4,6},{6,4},{1,3},{3,1},{5,7},{7,5},{8,10},{10,8},{12,... | collective-permute-start | bytes 393224 | tf_op jit(solution)/shard_map/ppermute | solution.py:23
  35.4 12.9 %collective-permute-start.13 = (bf16[128,512]{1,0:T(8,128)(2,1)S(1)}, bf16[128,512]{1,0:T(8,128)(2,1)S(1)}, u32[]{:S(2)}, u32[]{:S(2)}) collective-permute-start(bf16[128,512]{1,0:T(8,128)(2,1)S(1)} %get-tuple-element.55), channel_id=1, source_target_pairs={{0,4},{2,6},{4,0},{6,2},{1,5},{3,7},{5,1},{7,3},{8,12},{10,14},{12... | collective-permute-start | bytes 393224 | tf_op jit(solution)/shard_map/ppermute | solution.py:23
  37.9 10.3 %collective-permute-start.14 = (bf16[128,512]{1,0:T(8,128)(2,1)S(1)}, bf16[128,512]{1,0:T(8,128)(2,1)S(1)}, u32[]{:S(2)}, u32[]{:S(2)}) collective-permute-start(bf16[128,512]{1,0:T(8,128)(2,1)S(1)} %get-tuple-element.56), channel_id=1, source_target_pairs={{0,6},{2,4},{4,2},{6,0},{1,7},{3,5},{5,3},{7,1},{8,14},{10,12},{12... | collective-permute-start | bytes 393224 | tf_op jit(solution)/shard_map/ppermute | solution.py:23

commit v5 on v4

--- a/solution.py
+++ b/solution.py
@@ -380,7 +380,8 @@
         compiler_params=params(4),
         name="pack",
     )(owners, slots, row_grads.reshape(size, width))
-    arrived = [packed[0]] + [exchanged(packed[by], "emb", by) for by in range(1, parties)]
+    away = {by: exchanged(packed[by], "emb", by) for by in range(parties - 1, 0, -1)}
+    arrived = [packed[0]] + [away[by] for by in range(parties - 1, 0, -1)]
     near = across(item_table, True)
     by = 1
     while by < row_count:

time: 49.2 us -> 48.3 us (0.982)
  waiting for transfers between devices: 14.4 us -> 11.4 us
  starting transfers between devices: 15.3 us -> 17.6 us
    ppermute x2, starting transfers between devices: 3.01 us -> 5 us  [across(): return lax.ppermute(shard, ('emb', 'phase'), pairs)]
    ppermute x2, waiting for transfers between devices: 5.06 us -> 3.29 us  [across(): return lax.ppermute(shard, ('emb', 'phase'), pairs)]
    ppermute x13, waiting for transfers between devices: 9.39 us -> 8.16 us  [exchanged(): return lax.ppermute(shard, axis, [(i, i ^ by) for i in range(count)])]
where the time goes in v5:
time: 48.3 us; the launch traced here: 48.1 us
  starting transfers between devices  17.6 us (36%)
  Pallas kernels  15.3 us (32%)
  waiting for transfers between devices  11.4 us (24%)
  local copies, waits for them, and re-layouts  2.98 us (6%)
  between operations  0.76 us (2%)
    ppermute x13, starting transfers between devices, exchanged(): return lax.ppermute(shard, axis, [(i, i ^ by) for i in range(count)])  12.6 us
    pallas_call x1, Pallas kernels, body(): pl.pallas_call(functools.partial(section_kernel, window), out_shape=[arra...  9.19 us
    ppermute x13, waiting for transfers between devices, exchanged(): return lax.ppermute(shard, axis, [(i, i ^ by) for i in range(count)])  8.16 us
    ppermute x2, starting transfers between devices, across(): return lax.ppermute(shard, ('emb', 'phase'), pairs)  5 us
    pallas_call x1, Pallas kernels, body(): pl.pallas_call(functools.partial(lookup_kernel, window), out_shape=[array...  3.55 us
    ppermute x2, waiting for transfers between devices, across(): return lax.ppermute(shard, ('emb', 'phase'), pairs)  3.29 us
    unnamed x16, local copies, waits for them, and re-layouts  2.98 us
  transfers between devices with their start and end apart: 15, of which 7 were waited for; matrix products, arithmetic and copies ran while one was open for 0% of the time, Pallas kernels for 30%

profile of v5, /device:TPU:0, one launch (start us, length us, event | category | flops | bytes accessed | tf_op | source)
XLA Modules:
  0.0 48.1 jit_solution(17437793098041735417)
XLA Ops:
  0.6 3.0 %collective-permute-start = (bf16[1024,512]{1,0:T(8,128)(2,1)}, bf16[1024,512]{1,0:T(8,128)(2,1)S(1)}, u32[]{:S(2)}, u32[]{:S(2)}) collective-permute-start(bf16[1024,512]{1,0:T(8,128)(2,1)} %table_ref.1), channel_id=1, source_target_pairs={{0,8},{1,17},{8,0},{9,25},{16,24},{17,1},{24,16},{25,9},{2,10},{3,... | collective-permute-start | bytes 3145736 | tf_op jit(solution)/shard_map/ppermute | solution.py:361
  3.6 0.9 %copy-done.3 = bf16[1,1,256,512]{3,2,1,0:T(8,128)(2,1)S(1)} copy-done((bf16[1,1,256,512]{3,2,1,0:T(8,128)(2,1)S(1)}, bf16[1,1,256,512]{3,2,1,0:T(8,128)(2,1)}, u32[]{:S(2)}) %copy-start.3) | copy-done | bytes 262168
  4.6 0.7 %copy-done.5 = s32[1,1,256,1]{2,3,1,0:T(1,128)S(1)} copy-done((s32[1,1,256,1]{2,3,1,0:T(1,128)S(1)}, s32[1,1,256,1]{2,3,1,0:T(1,128)}, u32[]{:S(2)}) %copy-start.5) | copy-done | bytes 1048
  5.3 0.7 %copy-done.6 = s32[1,1,256]{2,1,0:T(1,128)S(1)} copy-done((s32[1,1,256]{2,1,0:T(1,128)S(1)}, s32[1,1,256]{2,1,0:T(1,128)}, u32[]{:S(2)}) %copy-start.6) | copy-done | bytes 1048
  5.9 0.6 %pack.1 = (bf16[144,512]{1,0:T(8,128)(2,1)S(1)}, bf16[144,512]{1,0:T(8,128)(2,1)S(1)}, bf16[144,512]{1,0:T(8,128)(2,1)S(1)}, bf16[144,512]{1,0:T(8,128)(2,1)S(1)}, s32[1,256]{1,0:T(1,128)S(1)}) custom-call(s32[1,256]{1,0:T(1,128)S(1)} %bitcast.7, s32[1,256]{1,0:T(1,128)S(1)} %bitcast.8, bf16[256,512]{1,0:T(8,128)(2,1)S(1)} %bitcast.5), custom_call_target="tpu_custom_call" | custom-call | tf_op jit(solution)/shard_map/pack/pallas_call | solution.py:374
  6.5 1.6 %collective-permute-start.3 = (bf16[144,512]{1,0:T(8,128)(2,1)S(1)}, bf16[144,512]{1,0:T(8,128)(2,1)S(1)}, u32[]{:S(2)}, u32[]{:S(2)}) collective-permute-start(bf16[144,512]{1,0:T(8,128)(2,1)S(1)} %get-tuple-element.33), channel_id=1, source_target_pairs={{0,24},{8,16},{16,8},{24,0},{1,25},{9,17},{17,9},{25,1},{2,26},{10... | collective-permute-start | bytes 442376 | tf_op jit(solution)/shard_map/ppermute | solution.py:23
  8.1 0.1 collective-permute-start.4
  8.2 1.9 %collective-permute-start.5 = (bf16[144,512]{1,0:T(8,128)(2,1)S(1)}, bf16[144,512]{1,0:T(8,128)(2,1)S(1)}, u32[]{:S(2)}, u32[]{:S(2)}) collective-permute-start(bf16[144,512]{1,0:T(8,128)(2,1)S(1)} %get-tuple-element.35), channel_id=1, source_target_pairs={{0,8},{8,0},{16,24},{24,16},{1,9},{9,1},{17,25},{25,17},{2,10},{10... | collective-permute-start | bytes 442376 | tf_op jit(solution)/shard_map/ppermute | solution.py:23
  10.1 1.6 %collective-permute-start.1 = (s32[1,256]{1,0:T(1,128)S(1)}, s32[1,256]{1,0:T(1,128)S(1)}, u32[]{:S(2)}, u32[]{:S(2)}) collective-permute-start(s32[1,256]{1,0:T(1,128)S(1)} %get-tuple-element.30.first_ref), channel_id=1, source_target_pairs={{0,2},{2,0},{4,6},{6,4},{1,3},{3,1},{5,7},{7,5},{8,10},{10,8},{12,... | collective-permute-start | bytes 3080 | tf_op jit(solution)/shard_map/ppermute | solution.py:23
  11.7 2.0 %collective-permute-done.1.second_ref = s32[1,256]{1,0:T(1,128)S(1)} collective-permute-done((s32[1,256]{1,0:T(1,128)S(1)}, s32[1,256]{1,0:T(1,128)S(1)}, u32[]{:S(2)}, u32[]{:S(2)}) %collective-permute-start.1) | collective-permute-done | bytes 1056 | tf_op jit(solution)/shard_map/ppermute | solution.py:23
  13.7 2.6 %collective-permute-start.2 = (s32[2,256]{1,0:T(2,128)S(1)}, s32[2,256]{1,0:T(2,128)S(1)}, u32[]{:S(2)}, u32[]{:S(2)}) collective-permute-start(s32[2,256]{1,0:T(2,128)S(1)} %join.2.first_ref), channel_id=1, source_target_pairs={{0,4},{2,6},{4,0},{6,2},{1,5},{3,7},{5,1},{7,3},{8,12},{10,14},{12... | collective-permute-start | bytes 6152 | tf_op jit(solution)/shard_map/ppermute | solution.py:23
  16.2 1.9 %collective-permute-done.2.second_ref = s32[2,256]{1,0:T(2,128)S(1)} collective-permute-done((s32[2,256]{1,0:T(2,128)S(1)}, s32[2,256]{1,0:T(2,128)S(1)}, u32[]{:S(2)}, u32[]{:S(2)}) %collective-permute-start.2) | collective-permute-done | bytes 2080 | tf_op jit(solution)/shard_map/ppermute | solution.py:23
  18.1 0.0 collective-permute-start.8
  18.1 1.6 %collective-permute-done.near_ref.table_ref = bf16[1024,512]{1,0:T(8,128)(2,1)S(1)} collective-permute-done((bf16[1024,512]{1,0:T(8,128)(2,1)}, bf16[1024,512]{1,0:T(8,128)(2,1)S(1)}, u32[]{:S(2)}, u32[]{:S(2)}) %collective-permute-start) | collective-permute-done | bytes 1048608 | tf_op jit(solution)/shard_map/ppermute | solution.py:361
  19.8 0.0 collective-permute-start.9
  19.8 3.0 %collective-permute-done.3.refs_1_ = bf16[144,512]{1,0:T(8,128)(2,1)S(1)} collective-permute-done((bf16[144,512]{1,0:T(8,128)(2,1)S(1)}, bf16[144,512]{1,0:T(8,128)(2,1)S(1)}, u32[]{:S(2)}, u32[]{:S(2)}) %collective-permute-start.3) | collective-permute-done | bytes 147488 | tf_op jit(solution)/shard_map/ppermute | solution.py:23
  22.8 0.0 collective-permute-start.6
  22.9 0.0 collective-permute-done.4.refs_2_
  22.9 0.1 collective-permute-done.5.refs_3_
  23.0 2.0 %collective-permute-start.7 = (bf16[512,512]{1,0:T(8,128)(2,1)S(1)}, bf16[512,512]{1,0:T(8,128)(2,1)S(1)}, u32[]{:S(2)}, u32[]{:S(2)}) collective-permute-start(bf16[512,512]{1,0:T(8,128)(2,1)S(1)} %half.1), channel_id=1, source_target_pairs={{0,16},{1,9},{8,24},{9,1},{16,0},{17,25},{24,8},{25,17},{2,18},{3,... | collective-permute-start | bytes 1572872 | tf_op jit(solution)/shard_map/ppermute | solution.py:361
  25.0 0.7 %scatter.1 = (f32[512,512]{1,0:T(8,128)S(1)}, bf16[512,512]{1,0:T(8,128)(2,1)S(1)}) custom-call(bf16[144,512]{1,0:T(8,128)(2,1)S(1)} %get-tuple-element.47.refs_0_, bf16[144,512]{1,0:T(8,128)(2,1)S(1)} %collective-permute-done.3.refs_1_, bf16[144,512]{1,0:T(8,128)(2,1)S(1)} %collective-permute-done.4.refs_2_, bf16[144,512]{1,0:T(8,128)(2,1)S(1)} %collective-permute-done.5.refs_3_), custom_call_target="tpu_custom_call" | custom-call | flops 32999999488 | tf_op jit(solution)/shard_map/scatter/pallas_call | solution.py:411
  25.7 0.0 copy-start.1
  25.7 0.0 copy-start.7
  25.8 0.1 collective-permute-start.11
  25.8 0.0 collective-permute-done.9.outw_other
  25.8 0.0 collective-permute-done.8.proj_other
  25.9 0.0 copy-done
  25.9 0.0 copy-done.2
  25.9 0.4 weights.1
  26.3 0.0 copy-start.4
  26.3 0.0 collective-permute-done.6.next_ref
  26.3 0.6 %copy-done.1 = bf16[1024,512]{1,0:T(8,128)(2,1)S(1)} copy-done((bf16[1024,512]{1,0:T(8,128)(2,1)S(1)}, bf16[1024,512]{1,0:T(8,128)(2,1)}, u32[]{:S(2)}) %copy-start.1) | copy-done | bytes 1048600
  27.0 0.0 copy-done.7
  27.0 3.6 %lookup.1 = (bf16[768,512]{1,0:T(8,128)(2,1)S(1)}, s32[768,1]{1,0:T(8,128)S(1)}, s32[768,1]{1,0:T(8,128)S(1)}) custom-call(s32[4,256]{1,0:T(4,128)S(1)} %join.3.ids_ref, s32[1,2,2]{2,1,0:T(2,128)S(1)} %copy-done.7, bf16[1024,512]{1,0:T(8,128)(2,1)S(1)} %copy-done.1, bf16[1024,512]{1,0:T(8,128)(2,1)S(1)} %collective-permute-done.near_ref.table_ref, ...), custom_call_target="tpu_custom_call" | custom-call | tf_op jit(solution)/shard_map/lookup/pallas_call | solution.py:431
  30.5 1.7 %collective-permute-done.7.far_ref = bf16[512,512]{1,0:T(8,128)(2,1)S(1)} collective-permute-done((bf16[512,512]{1,0:T(8,128)(2,1)S(1)}, bf16[512,512]{1,0:T(8,128)(2,1)S(1)}, u32[]{:S(2)}, u32[]{:S(2)}) %collective-permute-start.7) | collective-permute-done | bytes 524320 | tf_op jit(solution)/shard_map/ppermute | solution.py:361
  32.2 0.0 collective-permute-start.10
  32.2 0.0 collective-permute-done.11.come_ref
  32.2 0.1 combine.1
  32.3 2.2 %collective-permute-start.12 = (bf16[128,512]{1,0:T(8,128)(2,1)S(1)}, bf16[128,512]{1,0:T(8,128)(2,1)S(1)}, u32[]{:S(2)}, u32[]{:S(2)}) collective-permute-start(bf16[128,512]{1,0:T(8,128)(2,1)S(1)} %get-tuple-element.54), channel_id=1, source_target_pairs={{0,2},{2,0},{4,6},{6,4},{1,3},{3,1},{5,7},{7,5},{8,10},{10,8},{12,... | collective-permute-start | bytes 393224 | tf_op jit(solution)/shard_map/ppermute | solution.py:23
  34.4 2.6 %collective-permute-start.13 = (bf16[128,512]{1,0:T(8,128)(2,1)S(1)}, bf16[128,512]{1,0:T(8,128)(2,1)S(1)}, u32[]{:S(2)}, u32[]{:S(2)}) collective-permute-start(bf16[128,512]{1,0:T(8,128)(2,1)S(1)} %get-tuple-element.55), channel_id=1, source_target_pairs={{0,4},{2,6},{4,0},{6,2},{1,5},{3,7},{5,1},{7,3},{8,12},{10,14},{12... | collective-permute-start | bytes 393224 | tf_op jit(solution)/shard_map/ppermute | solution.py:23
  37.0 0.0 collective-permute-start.14
  37.0 0.0 collective-permute-done.10.far2_ref
  37.0 0.0 copy-done.4
  37.0 9.2 %sections.1 = (bf16[256,512]{1,0:T(8,128)(2,1)}, f32[8,128]{1,0:T(8,128)S(1)}) custom-call(s32[768,1]{1,0:T(8,128)S(1)} %get-tuple-element.38.earliest_ref, s32[768,1]{1,0:T(8,128)S(1)} %get-tuple-element.39.ids_ref, bf16[768,512]{1,0:T(8,128)(2,1)S(1)} %get-tuple-element.42.early_ref, bf16[512,512]{1,0:T(8,128)(2,1)S(1)} %collective-permute-done.7.far_ref, ...), custom_call_target="tpu_custom_call" | custom-call | flops 1 | bytes 1 | tf_op jit(solution)/shard_map/sections/pallas_call | solution.py:457
  46.2 0.0 collective-permute-done.12.refs_0_
  46.2 1.1 %collective-permute-done.13.refs_1_ = bf16[128,512]{1,0:T(8,128)(2,1)S(1)} collective-permute-done((bf16[128,512]{1,0:T(8,128)(2,1)S(1)}, bf16[128,512]{1,0:T(8,128)(2,1)S(1)}, u32[]{:S(2)}, u32[]{:S(2)}) %collective-permute-start.13) | collective-permute-done | bytes 131104 | tf_op jit(solution)/shard_map/ppermute | solution.py:23
  47.3 0.0 collective-permute-done.14.refs_2_
  47.3 0.8 %finish.1 = f32[128,512]{1,0:T(8,128)} custom-call(f32[128,512]{1,0:T(8,128)S(1)} %get-tuple-element.53.own_ref, bf16[128,512]{1,0:T(8,128)(2,1)S(1)} %collective-permute-done.12.refs_0_, bf16[128,512]{1,0:T(8,128)(2,1)S(1)} %collective-permute-done.13.refs_1_, bf16[128,512]{1,0:T(8,128)(2,1)S(1)} %collective-permute-done.14.refs_2_, ...), custom_call_target="tpu_custom_call" | custom-call | tf_op jit(solution)/shard_map/finish/pallas_call | solution.py:481
  (8 shorter events, 0.0 us)
Async XLA Ops:
  0.6 19.2 %collective-permute-start = (bf16[1024,512]{1,0:T(8,128)(2,1)}, bf16[1024,512]{1,0:T(8,128)(2,1)S(1)}, u32[]{:S(2)}, u32[]{:S(2)}) collective-permute-start(bf16[1024,512]{1,0:T(8,128)(2,1)} %table_ref.1), channel_id=1, source_target_pairs={{0,8},{1,17},{8,0},{9,25},{16,24},{17,1},{24,16},{25,9},{2,10},{3,... | collective-permute-start | bytes 3145736 | tf_op jit(solution)/shard_map/ppermute | solution.py:361
  3.6 0.9 %copy-start.3 = (bf16[1,1,256,512]{3,2,1,0:T(8,128)(2,1)S(1)}, bf16[1,1,256,512]{3,2,1,0:T(8,128)(2,1)}, u32[]{:S(2)}) copy-start(bf16[1,1,256,512]{3,2,1,0:T(8,128)(2,1)} %param.12) | copy-start | bytes 786436
  4.6 0.7 %copy-start.5 = (s32[1,1,256,1]{2,3,1,0:T(1,128)S(1)}, s32[1,1,256,1]{2,3,1,0:T(1,128)}, u32[]{:S(2)}) copy-start(s32[1,1,256,1]{2,3,1,0:T(1,128)} %param.9) | copy-start | bytes 3076
  5.3 0.7 %copy-start.6 = (s32[1,1,256]{2,1,0:T(1,128)S(1)}, s32[1,1,256]{2,1,0:T(1,128)}, u32[]{:S(2)}) copy-start(s32[1,1,256]{2,1,0:T(1,128)} %param.10) | copy-start | bytes 3076
  6.5 16.3 %collective-permute-start.3 = (bf16[144,512]{1,0:T(8,128)(2,1)S(1)}, bf16[144,512]{1,0:T(8,128)(2,1)S(1)}, u32[]{:S(2)}, u32[]{:S(2)}) collective-permute-start(bf16[144,512]{1,0:T(8,128)(2,1)S(1)} %get-tuple-element.33), channel_id=1, source_target_pairs={{0,24},{8,16},{16,8},{24,0},{1,25},{9,17},{17,9},{25,1},{2,26},{10... | collective-permute-start | bytes 442376 | tf_op jit(solution)/shard_map/ppermute | solution.py:23
  8.1 14.8 %collective-permute-start.4 = (bf16[144,512]{1,0:T(8,128)(2,1)S(1)}, bf16[144,512]{1,0:T(8,128)(2,1)S(1)}, u32[]{:S(2)}, u32[]{:S(2)}) collective-permute-start(bf16[144,512]{1,0:T(8,128)(2,1)S(1)} %get-tuple-element.34), channel_id=1, source_target_pairs={{0,16},{8,24},{16,0},{24,8},{1,17},{9,25},{17,1},{25,9},{2,18},{10... | collective-permute-start | bytes 442376 | tf_op jit(solution)/shard_map/ppermute | solution.py:23
  8.2 14.8 %collective-permute-start.5 = (bf16[144,512]{1,0:T(8,128)(2,1)S(1)}, bf16[144,512]{1,0:T(8,128)(2,1)S(1)}, u32[]{:S(2)}, u32[]{:S(2)}) collective-permute-start(bf16[144,512]{1,0:T(8,128)(2,1)S(1)} %get-tuple-element.35), channel_id=1, source_target_pairs={{0,8},{8,0},{16,24},{24,16},{1,9},{9,1},{17,25},{25,17},{2,10},{10... | collective-permute-start | bytes 442376 | tf_op jit(solution)/shard_map/ppermute | solution.py:23
  10.1 3.6 %collective-permute-start.1 = (s32[1,256]{1,0:T(1,128)S(1)}, s32[1,256]{1,0:T(1,128)S(1)}, u32[]{:S(2)}, u32[]{:S(2)}) collective-permute-start(s32[1,256]{1,0:T(1,128)S(1)} %get-tuple-element.30.first_ref), channel_id=1, source_target_pairs={{0,2},{2,0},{4,6},{6,4},{1,3},{3,1},{5,7},{7,5},{8,10},{10,8},{12,... | collective-permute-start | bytes 3080 | tf_op jit(solution)/shard_map/ppermute | solution.py:23
  13.7 4.5 %collective-permute-start.2 = (s32[2,256]{1,0:T(2,128)S(1)}, s32[2,256]{1,0:T(2,128)S(1)}, u32[]{:S(2)}, u32[]{:S(2)}) collective-permute-start(s32[2,256]{1,0:T(2,128)S(1)} %join.2.first_ref), channel_id=1, source_target_pairs={{0,4},{2,6},{4,0},{6,2},{1,5},{3,7},{5,1},{7,3},{8,12},{10,14},{12... | collective-permute-start | bytes 6152 | tf_op jit(solution)/shard_map/ppermute | solution.py:23
  18.1 7.7 %collective-permute-start.8 = (bf16[1,512,2048]{2,1,0:T(8,128)(2,1)}, bf16[1,512,2048]{2,1,0:T(8,128)(2,1)S(1)}, u32[]{:S(2)}, u32[]{:S(2)}) collective-permute-start(bf16[1,512,2048]{2,1,0:T(8,128)(2,1)} %proj_own.1), channel_id=1, source_target_pairs={{0,1},{1,0},{2,3},{3,2},{4,5},{5,4},{6,7},{7,6},{8,9},{9,8},{10,11... | collective-permute-start | bytes 6291464 | tf_op jit(solution)/shard_map/ppermute | solution.py:23
  19.8 6.1 %collective-permute-start.9 = (bf16[1,512,512]{2,1,0:T(8,128)(2,1)}, bf16[1,512,512]{2,1,0:T(8,128)(2,1)S(1)}, u32[]{:S(2)}, u32[]{:S(2)}) collective-permute-start(bf16[1,512,512]{2,1,0:T(8,128)(2,1)} %outw_own.1), channel_id=1, source_target_pairs={{0,1},{1,0},{2,3},{3,2},{4,5},{5,4},{6,7},{7,6},{8,9},{9,8},{10,11... | collective-permute-start | bytes 1572872 | tf_op jit(solution)/shard_map/ppermute | solution.py:23
  22.8 3.5 %collective-permute-start.6 = (bf16[1024,512]{1,0:T(8,128)(2,1)S(1)}, bf16[1024,512]{1,0:T(8,128)(2,1)S(1)}, u32[]{:S(2)}, u32[]{:S(2)}) collective-permute-start(bf16[1024,512]{1,0:T(8,128)(2,1)S(1)} %collective-permute-done.near_ref.table_ref), channel_id=1, source_target_pairs={{0,1},{1,0},{2,3},{3,2},{4,5},{5,4},{6,7},{7,6},{8,9},{9,8},{10,11... | collective-permute-start | bytes 3145736 | tf_op jit(solution)/shard_map/ppermute | solution.py:23
  23.0 2.9 %copy-start = (bf16[1,512,2048]{2,1,0:T(8,128)(2,1)S(1)}, bf16[1,512,2048]{2,1,0:T(8,128)(2,1)}, u32[]{:S(2)}) copy-start(bf16[1,512,2048]{2,1,0:T(8,128)(2,1)} %proj_own.1) | copy-start | bytes 6291460
  23.0 2.9 %copy-start.2 = (bf16[1,512,512]{2,1,0:T(8,128)(2,1)S(1)}, bf16[1,512,512]{2,1,0:T(8,128)(2,1)}, u32[]{:S(2)}) copy-start(bf16[1,512,512]{2,1,0:T(8,128)(2,1)} %outw_own.1) | copy-start | bytes 1572868
  23.0 9.2 %collective-permute-start.7 = (bf16[512,512]{1,0:T(8,128)(2,1)S(1)}, bf16[512,512]{1,0:T(8,128)(2,1)S(1)}, u32[]{:S(2)}, u32[]{:S(2)}) collective-permute-start(bf16[512,512]{1,0:T(8,128)(2,1)S(1)} %half.1), channel_id=1, source_target_pairs={{0,16},{1,9},{8,24},{9,1},{16,0},{17,25},{24,8},{25,17},{2,18},{3,... | collective-permute-start | bytes 1572872 | tf_op jit(solution)/shard_map/ppermute | solution.py:361
  25.7 1.2 %copy-start.1 = (bf16[1024,512]{1,0:T(8,128)(2,1)S(1)}, bf16[1024,512]{1,0:T(8,128)(2,1)}, u32[]{:S(2)}) copy-start(bf16[1024,512]{1,0:T(8,128)(2,1)} %table_ref.1) | copy-start | bytes 3145732
  25.7 1.2 %copy-start.7 = (s32[1,2,2]{2,1,0:T(2,128)S(1)}, s32[1,2,2]{2,1,0:T(2,128)}, u32[]{:S(2)}) copy-start(s32[1,2,2]{2,1,0:T(2,128)} %lengths_ref.1) | copy-start | bytes 52
  25.8 6.4 %collective-permute-start.11 = (bf16[512,512]{1,0:T(8,128)(2,1)S(1)}, bf16[512,512]{1,0:T(8,128)(2,1)S(1)}, u32[]{:S(2)}, u32[]{:S(2)}) collective-permute-start(bf16[512,512]{1,0:T(8,128)(2,1)S(1)} %get-tuple-element.52), channel_id=1, source_target_pairs={{0,1},{1,0},{2,3},{3,2},{4,5},{5,4},{6,7},{7,6},{8,9},{9,8},{10,11... | collective-permute-start | bytes 1572872 | tf_op jit(solution)/shard_map/ppermute | solution.py:23
  26.3 10.8 %copy-start.4 = (f32[512]{0:T(512)S(1)}, f32[512]{0:T(512)}, u32[]{:S(2)}) copy-start(f32[512]{0:T(512)} %param.15) | copy-start | bytes 6148
  32.2 4.9 %collective-permute-start.10 = (bf16[512,512]{1,0:T(8,128)(2,1)S(1)}, bf16[512,512]{1,0:T(8,128)(2,1)S(1)}, u32[]{:S(2)}, u32[]{:S(2)}) collective-permute-start(bf16[512,512]{1,0:T(8,128)(2,1)S(1)} %collective-permute-done.7.far_ref), channel_id=1, source_target_pairs={{0,1},{1,0},{2,3},{3,2},{4,5},{5,4},{6,7},{7,6},{8,9},{9,8},{10,11... | collective-permute-start | bytes 1572872 | tf_op jit(solution)/shard_map/ppermute | solution.py:23
  32.3 14.0 %collective-permute-start.12 = (bf16[128,512]{1,0:T(8,128)(2,1)S(1)}, bf16[128,512]{1,0:T(8,128)(2,1)S(1)}, u32[]{:S(2)}, u32[]{:S(2)}) collective-permute-start(bf16[128,512]{1,0:T(8,128)(2,1)S(1)} %get-tuple-element.54), channel_id=1, source_target_pairs={{0,2},{2,0},{4,6},{6,4},{1,3},{3,1},{5,7},{7,5},{8,10},{10,8},{12,... | collective-permute-start | bytes 393224 | tf_op jit(solution)/shard_map/ppermute | solution.py:23
  34.4 12.9 %collective-permute-start.13 = (bf16[128,512]{1,0:T(8,128)(2,1)S(1)}, bf16[128,512]{1,0:T(8,128)(2,1)S(1)}, u32[]{:S(2)}, u32[]{:S(2)}) collective-permute-start(bf16[128,512]{1,0:T(8,128)(2,1)S(1)} %get-tuple-element.55), channel_id=1, source_target_pairs={{0,4},{2,6},{4,0},{6,2},{1,5},{3,7},{5,1},{7,3},{8,12},{10,14},{12... | collective-permute-start | bytes 393224 | tf_op jit(solution)/shard_map/ppermute | solution.py:23
  37.0 10.3 %collective-permute-start.14 = (bf16[128,512]{1,0:T(8,128)(2,1)S(1)}, bf16[128,512]{1,0:T(8,128)(2,1)S(1)}, u32[]{:S(2)}, u32[]{:S(2)}) collective-permute-start(bf16[128,512]{1,0:T(8,128)(2,1)S(1)} %get-tuple-element.56), channel_id=1, source_target_pairs={{0,6},{2,4},{4,2},{6,0},{1,7},{3,5},{5,3},{7,1},{8,14},{10,12},{12... | collective-permute-start | bytes 393224 | tf_op jit(solution)/shard_map/ppermute | solution.py:23
